TPU v7x, 32 devices: a whole 2x2x4 slice. The times are simulated.
32 devices in a mesh: dp: 4 (over x, core), row: 4 (over z), col: 2 (over y).
Axes of the slice: x: 2, y: 2, z: 4, core: 2. Of those that a mesh axis runs over, the one named last changes fastest.
Arguments:
- inputs: bfloat16 [2048, 8192], P(('dp', 'col'), 'row'), may hold values from -6 to 6
- w_in: bfloat16 [8192, 16384], P('row', 'col'), may hold values from -0.0625 to 0.0625
- w_out: bfloat16 [16384, 8192], P('col', 'row'), may hold values from -0.046875 to 0.046875
- grad_outputs: bfloat16 [2048, 8192], P(('dp', 'col'), 'row'), may hold values from -6 to 6
Outputs:
- outputs: bfloat16 [2048, 8192], P(('dp', 'col'), 'row')
- grad_inputs: bfloat16 [2048, 8192], P(('dp', 'col'), 'row')
- grad_w_in: bfloat16 [8192, 16384], P(('row', 'dp'), 'col')
- grad_w_out: bfloat16 [16384, 8192], P('col', ('row', 'dp'))
All inputs are finite; a program needn't handle non-finite values.
Results may differ from a plain program's by a relative error of at most 0.024.
Values may be sent and summed in bfloat16 or wider, within the bound.
A program may use at most 320 MiB of HBM per device.

v0:
```python
import jax
import jax.numpy as jnp
from jax import lax
from jax.sharding import PartitionSpec as P


def gelu_fn(values):
    return jax.nn.gelu(values, approximate=True)


def contract(left, right, left_dim, right_dim):
    return lax.dot_general(
        left, right, (((left_dim,), (right_dim,)), ((), ())), preferred_element_type=jnp.float32
    )


def shards(inputs, w_in, w_out, grad_outputs):
    gathered_in = lax.all_gather(inputs, "col", axis=0, tiled=True)
    preact = lax.psum_scatter(
        jnp.dot(gathered_in, w_in, preferred_element_type=jnp.float32).astype(jnp.bfloat16),
        "row",
        scatter_dimension=0,
        tiled=True,
    ).astype(jnp.float32)
    activated = gelu_fn(preact).astype(jnp.bfloat16)
    gathered_act = lax.all_gather(activated, "row", axis=0, tiled=True)
    out_part = lax.psum_scatter(
        jnp.dot(gathered_act, w_out, preferred_element_type=jnp.float32).astype(jnp.bfloat16),
        "col",
        scatter_dimension=0,
        tiled=True,
    ).astype(jnp.float32)
    outputs = (inputs.astype(jnp.float32) + out_part).astype(jnp.bfloat16)
    gathered_cot = lax.all_gather(grad_outputs, "col", axis=0, tiled=True)
    grad_activated = lax.psum_scatter(
        contract(gathered_cot, w_out, 1, 1).astype(jnp.bfloat16),
        "row",
        scatter_dimension=0,
        tiled=True,
    ).astype(jnp.float32)
    grad_preact = jax.vjp(gelu_fn, preact)[1](grad_activated)[0].astype(jnp.bfloat16)
    gathered_grad = lax.all_gather(grad_preact, "row", axis=0, tiled=True)
    input_part = lax.psum_scatter(
        contract(gathered_grad, w_in, 1, 1).astype(jnp.bfloat16),
        "col",
        scatter_dimension=0,
        tiled=True,
    ).astype(jnp.float32)
    grad_inputs = (grad_outputs.astype(jnp.float32) + input_part).astype(jnp.bfloat16)
    grad_w_in = lax.psum_scatter(
        contract(gathered_in, gathered_grad, 0, 0).astype(jnp.bfloat16),
        "dp",
        scatter_dimension=0,
        tiled=True,
    )
    out_full = contract(gathered_act, gathered_cot, 0, 0)
    grad_w_out = lax.psum_scatter(
        out_full.astype(jnp.bfloat16), "dp", scatter_dimension=1, tiled=True
    )
    return (outputs, grad_inputs, grad_w_in, grad_w_out)


def solution(mesh):
    return jax.shard_map(
        shards,
        mesh=mesh,
        in_specs=(
            P(("dp", "col"), "row"),
            P("row", "col"),
            P("col", "row"),
            P(("dp", "col"), "row"),
        ),
        out_specs=(
            P(("dp", "col"), "row"),
            P(("dp", "col"), "row"),
            P(("row", "dp"), "col"),
            P("col", ("row", "dp")),
        ),
        check_vma=False,
    )
```

profile of v0, /device:TPU:0, one launch (start us, length us, event | category | flops | bytes accessed | tf_op | source)
XLA Modules:
  0.0 1231.4 jit_solution(9352762878691512944)
XLA Ops:
  7.2 0.0 all-gather.9.cloned.1.call-start
  7.2 0.7 all-gather.9.cloned.1.call-update
  7.9 0.0 all-gather.5.cloned.1.call-start
  7.9 0.7 all-gather.5.cloned.1.call-update
  8.6 0.0 reduce-scatter.11.cloned.1.call-start
  8.7 36.7 %all-gather.9.cloned.1.call-done = bf16[512,2048]{1,0:T(8,128)(2,1)} async-done(((bf16[256,2048]{1,0:T(8,128)(2,1)}), bf16[512,2048]{1,0:T(8,128)(2,1)}) %all-gather.9.cloned.1.call-update) | async-done | bytes 2097168 | tf_op jit(solution)/shard_map/all_gather | solution.py:34
  45.4 24.9 %convolution_convert_fusion.1 = bf16[512,8192]{1,0:T(8,128)(2,1)} fusion(bf16[512,2048]{1,0:T(8,128)(2,1)} %all-gather.9.cloned.1.call-done, bf16[8192,2048]{1,0:T(8,128)(2,1)} %param.6), kind=kOutput, calls=%fused_computation.2 | convolution fusion | flops 17184063488 | bytes 44040192 | tf_op jit(solution)/shard_map/dot_general | solution.py:12
  70.3 0.0 reduce-scatter.11.cloned.1.call-update
  70.3 0.0 reduce-scatter.7.cloned.1.call-start
  70.4 9.7 all-gather.5.cloned.1.call-done
  80.1 26.0 %convolution_convert_fusion.2 = bf16[512,8192]{1,0:T(8,128)(2,1)} fusion(bf16[512,2048]{1,0:T(8,128)(2,1)} %all-gather.5.cloned.1.call-done, bf16[2048,8192]{1,0:T(8,128)(2,1)} %param.5), kind=kOutput, calls=%fused_computation.3 | convolution fusion | flops 17184063488 | bytes 44040192 | tf_op jit(solution)/shard_map/dot_general | solution.py:20
  106.1 0.0 reduce-scatter.7.cloned.1.call-update
  106.2 0.2 all-gather.7.cloned.1.call-start
  106.4 121.1 %reduce-scatter.11.cloned.1.call-done = bf16[128,8192]{1,0:T(8,128)(2,1)} async-done(((bf16[512,8192]{1,0:T(8,128)(2,1)}), bf16[128,8192]{1,0:T(8,128)(2,1)}) %reduce-scatter.11.cloned.1.call-update) | async-done | bytes 2097168 | tf_op jit(solution)/shard_map/reduce_scatter | solution.py:35
  227.5 148.0 %reduce-scatter.7.cloned.1.call-done = bf16[128,8192]{1,0:T(8,128)(2,1)} async-done(((bf16[512,8192]{1,0:T(8,128)(2,1)}), bf16[128,8192]{1,0:T(8,128)(2,1)}) %reduce-scatter.7.cloned.1.call-update) | async-done | bytes 2097168 | tf_op jit(solution)/shard_map/reduce_scatter | solution.py:19
  375.5 6.1 fusion.3
  381.7 0.0 all-gather.7.cloned.1.call-update
  381.7 0.0 all-gather.11.cloned.1.call-start
  381.8 0.5 all-gather.11.cloned.1.call-update
  382.3 0.0 reduce-scatter.9.cloned.1.call-start
  382.3 149.9 %all-gather.7.cloned.1.call-done = bf16[512,8192]{1,0:T(8,128)(2,1)} async-done(((bf16[128,8192]{1,0:T(8,128)(2,1)}), bf16[512,8192]{1,0:T(8,128)(2,1)}) %all-gather.7.cloned.1.call-update) | async-done | bytes 8388624 | tf_op jit(solution)/shard_map/all_gather | solution.py:26
  532.2 24.6 %convolution_convert_fusion.4 = bf16[512,2048]{1,0:T(8,128)(2,1)} fusion(bf16[512,8192]{1,0:T(8,128)(2,1)} %all-gather.7.cloned.1.call-done, bf16[8192,2048]{1,0:T(8,128)(2,1)} %param.6), kind=kOutput, calls=%fused_computation.22 | convolution fusion | flops 17180917760 | bytes 44040192 | tf_op jit(solution)/shard_map/dot_general | solution.py:28
  556.8 0.0 reduce-scatter.9.cloned.1.call-update
  556.8 0.0 copy-start.3
  556.8 0.0 reduce-scatter.13.cloned.1.call-start
  556.9 125.3 %all-gather.11.cloned.1.call-done = bf16[512,8192]{1,0:T(8,128)(2,1)} async-done(((bf16[128,8192]{1,0:T(8,128)(2,1)}), bf16[512,8192]{1,0:T(8,128)(2,1)}) %all-gather.11.cloned.1.call-update) | async-done | bytes 8388624 | tf_op jit(solution)/shard_map/all_gather | solution.py:42
  682.1 24.7 %convolution_convert_fusion.3 = bf16[512,2048]{1,0:T(8,128)(2,1)} fusion(bf16[512,8192]{1,0:T(8,128)(2,1)} %all-gather.11.cloned.1.call-done, bf16[2048,8192]{1,0:T(8,128)(2,1)} %param.5), kind=kOutput, calls=%fused_computation.21 | convolution fusion | flops 17180917760 | bytes 44040192 | tf_op jit(solution)/shard_map/dot_general | solution.py:12
  706.8 0.0 reduce-scatter.13.cloned.1.call-update
  706.9 0.3 reduce-scatter.15.cloned.1.call-start
  707.1 0.0 copy-done.3
  707.2 25.2 %convert_bitcast_fusion = bf16[2048,8192]{0,1:T(8,128)(2,1)} fusion(bf16[512,8192]{1,0:T(8,128)(2,1)} %all-gather.11.cloned.1.call-done, bf16[512,2048]{1,0:T(8,128)(2,1)S(1)} %copy-done.3), kind=kOutput, calls=%fused_computation | convolution fusion | flops 17196646400 | bytes 44040192 | tf_op jit(solution)/shard_map/dot_general | solution.py:12
  732.3 0.0 copy-start.2
  732.3 0.0 reduce-scatter.15.cloned.1.call-update
  732.4 0.0 reduce-scatter.17.cloned.1.call-start
  732.4 1.5 copy-done.2
  733.9 25.5 %convolution_convert_fusion = bf16[8192,2048]{1,0:T(8,128)(2,1)} fusion(bf16[512,8192]{1,0:T(8,128)(2,1)} %all-gather.7.cloned.1.call-done, bf16[512,2048]{1,0:T(8,128)(2,1)S(1)} %copy-done.2), kind=kOutput, calls=%fused_computation.1 | convolution fusion | flops 17196646400 | bytes 44040192 | tf_op jit(solution)/shard_map/dot_general | solution.py:12
  759.5 0.0 copy-start
  759.5 0.0 copy-start.1
  759.5 0.0 reduce-scatter.17.cloned.1.call-update
  759.5 0.0 reduce-scatter.9.cloned.1.call-done
  759.5 1.5 copy-done
  761.0 2.8 add_convert_fusion.1
  763.8 0.0 reduce-scatter.13.cloned.1.call-done
  763.8 0.0 copy-done.1
  763.8 2.8 add_convert_fusion
  766.6 220.1 %reduce-scatter.15.cloned.1.call-done = bf16[512,8192]{0,1:T(8,128)(2,1)} async-done(((bf16[2048,8192]{0,1:T(8,128)(2,1)}), bf16[512,8192]{0,1:T(8,128)(2,1)}) %reduce-scatter.15.cloned.1.call-update) | async-done | bytes 8388624 | tf_op jit(solution)/shard_map/reduce_scatter | solution.py:50
  986.7 11.9 copy.8
  998.6 225.9 %reduce-scatter.17.cloned.1.call-done = bf16[8192,512]{1,0:T(8,128)(2,1)} async-done(((bf16[8192,2048]{1,0:T(8,128)(2,1)}), bf16[8192,512]{1,0:T(8,128)(2,1)}) %reduce-scatter.17.cloned.1.call-update) | async-done | bytes 8388624 | tf_op jit(solution)/shard_map/reduce_scatter | solution.py:57
Async XLA Ops:
  7.2 38.2 %all-gather.9.cloned.1.call-start = ((), (), s32[]{:S(2)}) async-start(), calls=%async_computation.10 | async-start | bytes 3145728 | tf_op jit(solution)/shard_map/all_gather | solution.py:34
  7.9 72.2 %all-gather.5.cloned.1.call-start = ((), (), s32[]{:S(2)}) async-start(), calls=%async_computation.6 | async-start | bytes 3145728 | tf_op jit(solution)/shard_map/all_gather | solution.py:18
  8.6 218.9 %reduce-scatter.11.cloned.1.call-start = ((), (), s32[]{:S(2)}) async-start(), calls=%async_computation.11 | async-start | bytes 10485760 | tf_op jit(solution)/shard_map/reduce_scatter | solution.py:35
  70.3 305.2 %reduce-scatter.7.cloned.1.call-start = ((), (), s32[]{:S(2)}) async-start(), calls=%async_computation.7 | async-start | bytes 10485760 | tf_op jit(solution)/shard_map/reduce_scatter | solution.py:19
  106.2 426.1 %all-gather.7.cloned.1.call-start = ((), (), s32[]{:S(2)}) async-start(), calls=%async_computation.8 | async-start | bytes 10485760 | tf_op jit(solution)/shard_map/all_gather | solution.py:26
  381.7 300.4 %all-gather.11.cloned.1.call-start = ((), (), s32[]{:S(2)}) async-start(), calls=%async_computation.12 | async-start | bytes 10485760 | tf_op jit(solution)/shard_map/all_gather | solution.py:42
  382.3 377.2 %reduce-scatter.9.cloned.1.call-start = ((), (), s32[]{:S(2)}) async-start(), calls=%async_computation.9 | async-start | bytes 3145728 | tf_op jit(solution)/shard_map/reduce_scatter | solution.py:27
  556.8 150.4 %copy-start.3 = (bf16[512,2048]{1,0:T(8,128)(2,1)S(1)}, bf16[512,2048]{1,0:T(8,128)(2,1)}, u32[]{:S(2)}) copy-start(bf16[512,2048]{1,0:T(8,128)(2,1)} %all-gather.5.cloned.1.call-done) | copy-start | bytes 6291460
  556.8 207.0 %reduce-scatter.13.cloned.1.call-start = ((), (), s32[]{:S(2)}) async-start(), calls=%async_computation.13 | async-start | bytes 3145728 | tf_op jit(solution)/shard_map/reduce_scatter | solution.py:43
  706.9 279.8 %reduce-scatter.15.cloned.1.call-start = ((), (), s32[]{:S(2)}) async-start(), calls=%async_computation.14 | async-start | bytes 41943040 | tf_op jit(solution)/shard_map/reduce_scatter | solution.py:50
  732.3 1.6 copy-start.2
  732.4 492.2 %reduce-scatter.17.cloned.1.call-start = ((), (), s32[]{:S(2)}) async-start(), calls=%async_computation.15 | async-start | bytes 41943040 | tf_op jit(solution)/shard_map/reduce_scatter | solution.py:57
  759.5 1.5 copy-start
  759.5 4.4 copy-start.1
Sparse Core Ops, SparseCore 0:
  9.5 35.8 all-gather.8
  46.9 33.1 all-gather.4
  83.0 144.4 reduce-scatter.10
  230.3 145.1 reduce-scatter.6
  381.8 150.3 all-gather.6
  534.2 147.8 all-gather.10
  684.9 30.0 reduce-scatter.8
  717.3 31.8 reduce-scatter.12
  751.8 234.8 reduce-scatter.14
  989.7 234.8 reduce-scatter.16
where the time goes:
time: 1230 us
  waiting for transfers between devices  1040 us (85%)
  matrix products  151 us (12%)
  local copies, waits for them, and re-layouts  14.9 us (1%)
  between operations  14.2 us (1%)
    reduce_scatter x1, waiting for transfers between devices, shards(): lax.psum_scatter(out_full.astype(jnp.bfloat16), 'dp', scatter_dimension=1...  226 us
    reduce_scatter x1, waiting for transfers between devices, shards(): lax.psum_scatter(contract(gathered_in, gathered_grad, 0, 0).astype(jnp.bf...  220 us
    all_gather x1, waiting for transfers between devices, shards(): gathered_act = lax.all_gather(activated, 'row', axis=0, tiled=True)  150 us
    reduce_scatter x1, waiting for transfers between devices, shards(): lax.psum_scatter(jnp.dot(gathered_in, w_in, preferred_element_type=jnp.fl...  148 us
    all_gather x1, waiting for transfers between devices, shards(): gathered_grad = lax.all_gather(grad_preact, 'row', axis=0, tiled=True)  125 us
    reduce_scatter x1, waiting for transfers between devices, shards(): lax.psum_scatter(contract(gathered_cot, w_out, 1, 1).astype(jnp.bfloat16)...  121 us
    dot_general x4, matrix products, contract(): lax.dot_general(left, right, (((left_dim,), (right_dim,)), ((), ())), pre...  100 us
    all_gather x1, waiting for transfers between devices, shards(): gathered_cot = lax.all_gather(grad_outputs, 'col', axis=0, tiled=True)  36.7 us
  transfers between devices with their start and end apart: 10, of which 8 were waited for; matrix products, arithmetic and copies ran while one was open for 14% of the time, Pallas kernels for 0%

commit v1 on v0

v1 whole, which is shorter than its diff:
```python
import jax
import jax.numpy as jnp
from jax import lax
from jax.sharding import PartitionSpec as P

PARTS = 2


def gelu_fn(values):
    return jax.nn.gelu(values, approximate=True)


def contract(left, right, left_dim, right_dim):
    return lax.dot_general(
        left, right, (((left_dim,), (right_dim,)), ((), ())), preferred_element_type=jnp.float32
    )


def plus(left, right):
    return (left.astype(jnp.float32) + right.astype(jnp.float32)).astype(jnp.bfloat16)


def take(array, index, dim):
    return lax.dynamic_index_in_dim(array, index, dim, keepdims=True)


def swap(array, axis, size, mask):
    return lax.ppermute(array, axis, [(k, k ^ mask) for k in range(size)])


def sum_over_row(part, n):
    me = lax.axis_index("row")
    right = left = None
    for t in range(n - 1):
        block = take(part, jnp.clip(n - 1 - t + me, 0, n - 1), 0)
        block = block if right is None else plus(block, right)
        right = lax.ppermute(block, "row", [(k, k + 1) for k in range(t + 1)])
        block = take(part, jnp.clip(t - n + 1 + me, 0, n - 1), 0)
        block = block if left is None else plus(block, left)
        left = lax.ppermute(block, "row", [(k, k - 1) for k in range(n - 1, n - 2 - t, -1)])
    return (
        take(part, me, 0).astype(jnp.float32) + right.astype(jnp.float32) + left.astype(jnp.float32)
    )


def gather_over_row(own, n):
    me = lax.axis_index("row")
    right = left = own
    rights, lefts = [], []
    for t in range(n - 1):
        right = lax.ppermute(right, "row", [(k, k + 1) for k in range(t, n - 1)])
        left = lax.ppermute(left, "row", [(k, k - 1) for k in range(n - 1 - t, 0, -1)])
        rights.append(right)
        lefts.append(left)
    whole = jnp.zeros((n,) + own.shape[1:], own.dtype)
    whole = lax.dynamic_update_slice_in_dim(whole, own, me, 0)
    for t in range(n - 1):
        block = jnp.where(me >= t + 1, rights[t], lefts[n - 2 - t])
        whole = lax.dynamic_update_slice_in_dim(whole, block, lax.rem(me + n - 1 - t, n), 0)
    return whole


def solution(mesh):
    n_dp, n_row, n_col = mesh.shape["dp"], mesh.shape["row"], mesh.shape["col"]
    dp_bits, col_bits = n_dp.bit_length() - 1, n_col.bit_length() - 1
    digits = [("dp", n_dp, 1 << b) for b in reversed(range(dp_bits))]
    digits += [("col", n_col, 1 << b) for b in reversed(range(col_bits))]
    core = [dp_bits - 1]
    far = list(range(dp_bits - 1))
    cols = list(range(dp_bits, dp_bits + col_bits))

    def digit(d):
        axis, _, weight = digits[d]
        return lax.rem(lax.axis_index(axis) // weight, 2)

    def gather_tokens(block, order):
        array = block.reshape((1,) * len(digits) + block.shape)
        for d in order:
            axis, size, weight = digits[d]
            other = swap(array, axis, size, weight)
            low = digit(d) == 0
            array = jnp.concatenate(
                [jnp.where(low, array, other), jnp.where(low, other, array)], axis=d
            )
        return array.reshape(-1, block.shape[-1])

    def scatter_tokens(part, order):
        array = part.reshape((2,) * len(digits) + (-1, part.shape[-1]))
        for at, d in enumerate(order):
            axis, size, weight = digits[d]
            other = swap(take(array, 1 - digit(d), d), axis, size, weight)
            kept = take(array, digit(d), d)
            if at == len(order) - 1:
                array = kept.astype(jnp.float32) + other.astype(jnp.float32)
            else:
                array = plus(kept, other)
        return array.reshape(-1, part.shape[-1])

    def shards(inputs, w_in, w_out, grad_outputs):
        dp = lax.axis_index("dp")
        model, hidden = w_in.shape
        share = hidden // n_dp
        width = share // PARTS
        piece = model // n_dp

        all_in = gather_tokens(inputs, cols + far + core)
        all_cot = gather_tokens(grad_outputs, far + cols + core)
        tokens = all_in.shape[0]
        blocks = (n_row, tokens // n_row, width)
        grad_w_in = jnp.zeros((piece, hidden), jnp.bfloat16)
        grad_w_out = jnp.zeros((hidden, piece), jnp.bfloat16)
        out_part = input_part = None
        for h in range(PARTS):
            first = dp * share + h * width
            w_in_h = lax.dynamic_slice_in_dim(w_in, first, width, 1)
            w_out_h = lax.dynamic_slice_in_dim(w_out, first, width, 0)
            part = contract(all_in, w_in_h, 1, 0).astype(jnp.bfloat16)
            preact = sum_over_row(part.reshape(blocks), n_row)
            activated = gelu_fn(preact).astype(jnp.bfloat16)
            part = contract(all_cot, w_out_h, 1, 1).astype(jnp.bfloat16)
            grad_activated = sum_over_row(part.reshape(blocks), n_row)
            grad_preact = jax.vjp(gelu_fn, preact)[1](grad_activated)[0].astype(jnp.bfloat16)
            all_act = gather_over_row(activated, n_row).reshape(tokens, width)
            all_grad = gather_over_row(grad_preact, n_row).reshape(tokens, width)

            term = contract(all_act, w_out_h, 1, 0)
            out_part = term if out_part is None else out_part + term
            term = contract(all_grad, w_in_h, 1, 1)
            input_part = term if input_part is None else input_part + term

            whole_out = contract(all_act, all_cot, 0, 0).astype(jnp.bfloat16)
            whole_in = contract(all_in, all_grad, 0, 0).astype(jnp.bfloat16)
            for mask in range(n_dp):
                peer = dp ^ mask
                place = peer * share + h * width
                block = lax.dynamic_slice_in_dim(whole_out, peer * piece, piece, 1)
                block = swap(block, "dp", n_dp, mask) if mask else block
                grad_w_out = lax.dynamic_update_slice_in_dim(grad_w_out, block, place, 0)
                block = lax.dynamic_slice_in_dim(whole_in, peer * piece, piece, 0)
                block = swap(block, "dp", n_dp, mask) if mask else block
                grad_w_in = lax.dynamic_update_slice_in_dim(grad_w_in, block, place, 1)
        out_sum = scatter_tokens(out_part.astype(jnp.bfloat16), core + far + cols)
        outputs = (inputs.astype(jnp.float32) + out_sum).astype(jnp.bfloat16)
        input_sum = scatter_tokens(input_part.astype(jnp.bfloat16), core + cols + far)
        grad_inputs = (grad_outputs.astype(jnp.float32) + input_sum).astype(jnp.bfloat16)
        return (outputs, grad_inputs, grad_w_in, grad_w_out)

    return jax.shard_map(
        shards,
        mesh=mesh,
        in_specs=(
            P(("dp", "col"), "row"),
            P("row", "col"),
            P("col", "row"),
            P(("dp", "col"), "row"),
        ),
        out_specs=(
            P(("dp", "col"), "row"),
            P(("dp", "col"), "row"),
            P(("row", "dp"), "col"),
            P("col", ("row", "dp")),
        ),
        check_vma=False,
    )
```

time: 1230 us -> 1080 us (0.88)
  waiting for transfers between devices: 1040 us -> 515 us
  starting transfers between devices: 0.8 us -> 226 us
  other arithmetic: 11.7 us -> 112 us
  local copies, waits for them, and re-layouts: 14.9 us -> 62.2 us
    reduce_scatter x6 -> x0, waiting for transfers between devices: 715 us -> none  [the longest x1 226 us: shards(): lax.psum_scatter(out_full.astype(jnp.bfloat16), 'dp', scatter_dimension=1...]
    ppermute x0 -> x72, waiting for transfers between devices: none -> 515 us  [the longest x24 293 us: swap(): return lax.ppermute(array, axis, [(k, k ^ mask) for k in range(size)])]
    all_gather x4 -> x0, waiting for transfers between devices: 322 us -> none  [the longest x1 150 us: shards(): gathered_act = lax.all_gather(activated, 'row', axis=0, tiled=True)]
    ppermute x0 -> x72, starting transfers between devices: none -> 226 us  [the longest x12 90.9 us: gather_over_row(): right = lax.ppermute(right, 'row', [(k, k + 1) for k in range(t, n - 1)])]
    dot_general x4 -> x12, matrix products: 100 us -> 155 us  [contract(): lax.dot_general(left, right, (((left_dim,), (right_dim,)), ((), ())), pre...]
    dot_general x2 -> x0, matrix products: 50.6 us -> none  [the longest x1 26 us: shards(): jnp.dot(gathered_in, w_in, preferred_element_type=jnp.float32)]
    convert_element_type x3 -> x18, other arithmetic: 11.7 us -> 51.6 us  [the longest x16 48.6 us: plus(): (left.astype(jnp.float32) + right.astype(jnp.float32)).astype(jnp.bfloat16)]
    dynamic_update_slice x0 -> x16, other arithmetic: none -> 26 us  [the longest x12 18.4 us: gather_over_row(): lax.dynamic_update_slice_in_dim(whole, block, lax.rem(me + n - 1 - t, n), 0)]
  transfers between devices with their start and end apart: 10 -> 72, of which waited for: 8 -> 27; matrix products, arithmetic and copies ran while one was open for 14% -> 28% of each run, Pallas kernels for 0% -> 0%
where the time goes in v1:
time: 1080 us; the launch traced here: 1070 us
  waiting for transfers between devices  515 us (48%)
  starting transfers between devices  226 us (21%)
  matrix products  155 us (14%)
  other arithmetic  112 us (10%)
  local copies, waits for them, and re-layouts  62.2 us (6%)
    ppermute x24, waiting for transfers between devices, swap(): return lax.ppermute(array, axis, [(k, k ^ mask) for k in range(size)])  293 us
    dot_general x12, matrix products, contract(): lax.dot_general(left, right, (((left_dim,), (right_dim,)), ((), ())), pre...  155 us
    ppermute x12, waiting for transfers between devices, gather_over_row(): lax.ppermute(left, 'row', [(k, k - 1) for k in range(n - 1 - t, 0, -1)])  132 us
    ppermute x12, starting transfers between devices, gather_over_row(): right = lax.ppermute(right, 'row', [(k, k + 1) for k in range(t, n - 1)])  90.9 us
    ppermute x12, waiting for transfers between devices, sum_over_row(): right = lax.ppermute(block, 'row', [(k, k + 1) for k in range(t + 1)])  86.7 us
    ppermute x12, starting transfers between devices, sum_over_row(): right = lax.ppermute(block, 'row', [(k, k + 1) for k in range(t + 1)])  76.3 us
    convert_element_type x16, other arithmetic, plus(): (left.astype(jnp.float32) + right.astype(jnp.float32)).astype(jnp.bfloat16)  48.6 us
    ppermute x24, starting transfers between devices, swap(): return lax.ppermute(array, axis, [(k, k ^ mask) for k in range(size)])  25.3 us
  transfers between devices with their start and end apart: 72, of which 27 were waited for; matrix products, arithmetic and copies ran while one was open for 28% of the time, Pallas kernels for 0%

profile of v1, /device:TPU:0, one launch (start us, length us, event | category | flops | bytes accessed | tf_op | source)
XLA Modules:
  0.0 1072.4 jit_solution(10586166410072437502)
XLA Ops:
  3.6 23.4 %collective-permute-done.30 = bf16[1,1,1,256,2048]{4,3,2,1,0:T(8,128)(2,1)S(1)} collective-permute-done((bf16[1,1,1,256,2048]{4,3,2,1,0:T(8,128)(2,1)}, bf16[1,1,1,256,2048]{4,3,2,1,0:T(8,128)(2,1)S(1)}, u32[]{:S(2)}, u32[]{:S(2)}) %collective-permute-start.30) | collective-permute-done | bytes 1048608 | tf_op jit(solution)/shard_map/ppermute | solution.py:28
  32.9 67.5 %collective-permute-done = bf16[1,1,1,256,2048]{4,3,2,1,0:T(8,128)(2,1)S(1)} collective-permute-done((bf16[1,1,1,256,2048]{4,3,2,1,0:T(8,128)(2,1)S(1)}, bf16[1,1,1,256,2048]{4,3,2,1,0:T(8,128)(2,1)S(1)}, u32[]{:S(2)}, u32[]{:S(2)}) %collective-permute-start) | collective-permute-done | bytes 1048608 | tf_op jit(solution)/shard_map/ppermute | solution.py:28
  106.9 46.6 %collective-permute-done.1 = bf16[1,1,2,256,2048]{4,3,2,1,0:T(8,128)(2,1)S(1)} collective-permute-done((bf16[1,1,2,256,2048]{4,3,2,1,0:T(8,128)(2,1)S(1)}, bf16[1,1,2,256,2048]{4,3,2,1,0:T(8,128)(2,1)S(1)}, u32[]{:S(2)}, u32[]{:S(2)}) %collective-permute-start.1) | collective-permute-done | bytes 2097184 | tf_op jit(solution)/shard_map/ppermute | solution.py:28
  157.1 5.5 broadcast_select_fusion.1
  162.5 7.6 pad_maximum_fusion.1
  170.2 12.6 %convolution_convert_fusion.2 = bf16[2048,1024]{1,0:T(8,128)(2,1)S(1)} fusion(bf16[2048,2048]{1,0:T(8,128)(2,1)} %bitcast.70, bf16[8192,2048]{1,0:T(8,128)(2,1)} %param.6, s32[]{:T(128)S(6)} %select_n.307), kind=kOutput, calls=%fused_computation.16 | convolution fusion | flops 8592031744 | bytes 16777220 | tf_op jit(solution)/shard_map/dot_general | solution.py:14
  184.0 4.8 collective-permute-start.45
  188.8 3.9 broadcast_select_fusion.3
  192.8 6.3 pad_maximum_fusion
  199.1 12.6 %convolution_convert_fusion.4 = bf16[2048,1024]{1,0:T(8,128)(2,1)S(1)} fusion(bf16[2048,2048]{1,0:T(8,128)(2,1)} %bitcast.64, bf16[2048,8192]{1,0:T(8,128)(2,1)} %param.5, s32[]{:T(128)S(6)} %select_n.307), kind=kOutput, calls=%fused_computation.18 | convolution fusion | flops 8592031744 | bytes 16777220 | tf_op jit(solution)/shard_map/dot_general | solution.py:14
  216.4 11.1 %convolution_convert_fusion.5 = bf16[2048,1024]{1,0:T(8,128)(2,1)S(1)} fusion(bf16[2048,2048]{1,0:T(8,128)(2,1)S(1)} %bitcast.65, bf16[2048,8192]{1,0:T(8,128)(2,1)} %param.5, s32[]{:T(128)S(6)} %select_n.296), kind=kOutput, calls=%fused_computation.19 | convolution fusion | flops 8592031744 | bytes 16777220 | tf_op jit(solution)/shard_map/dot_general | solution.py:14
  233.0 4.1 collective-permute-done.15
  239.8 5.9 collective-permute-start.16
  245.7 11.2 %convolution_convert_fusion.3 = bf16[2048,1024]{1,0:T(8,128)(2,1)S(1)} fusion(bf16[2048,2048]{1,0:T(8,128)(2,1)S(1)} %bitcast.74, bf16[8192,2048]{1,0:T(8,128)(2,1)} %param.6, s32[]{:T(128)S(6)} %select_n.296), kind=kOutput, calls=%fused_computation.17 | convolution fusion | flops 8592031744 | bytes 16777220 | tf_op jit(solution)/shard_map/dot_general | solution.py:14
  271.5 10.7 %collective-permute-done.16 = bf16[1,512,1024]{2,1,0:T(8,128)(2,1)} collective-permute-done((bf16[1,512,1024]{2,1,0:T(8,128)(2,1)}, bf16[1,512,1024]{2,1,0:T(8,128)(2,1)}, u32[]{:S(2)}, u32[]{:S(2)}) %collective-permute-start.16) | collective-permute-done | bytes 1048608 | tf_op jit(solution)/shard_map/ppermute | solution.py:37
  282.2 5.4 collective-permute-start.4
  287.6 4.5 add_convert_fusion.16
  292.8 11.9 %collective-permute-done.33 = bf16[1,512,1024]{2,1,0:T(8,128)(2,1)} collective-permute-done((bf16[1,512,1024]{2,1,0:T(8,128)(2,1)}, bf16[1,512,1024]{2,1,0:T(8,128)(2,1)}, u32[]{:S(2)}, u32[]{:S(2)}) %collective-permute-start.33) | collective-permute-done | bytes 1048608 | tf_op jit(solution)/shard_map/ppermute | solution.py:37
  309.3 17.9 %collective-permute-done.46 = bf16[1,512,1024]{2,1,0:T(8,128)(2,1)} collective-permute-done((bf16[1,512,1024]{2,1,0:T(8,128)(2,1)}, bf16[1,512,1024]{2,1,0:T(8,128)(2,1)}, u32[]{:S(2)}, u32[]{:S(2)}) %collective-permute-start.46) | collective-permute-done | bytes 1048608 | tf_op jit(solution)/shard_map/ppermute | solution.py:37
  327.2 5.4 collective-permute-start.34
  332.5 3.9 add_convert_fusion.8
  339.1 10.5 collective-permute-done.4
  349.6 4.5 add_convert_fusion.20
  355.8 4.1 collective-permute-start.17
  363.8 8.3 collective-permute-done.34
  372.1 4.4 collective-permute-start.47
  376.6 3.9 add_convert_fusion.12
  387.9 6.7 collective-permute-done.17
  394.6 4.6 collective-permute-start.5
  402.1 15.0 %collective-permute-done.47 = bf16[1,512,1024]{2,1,0:T(8,128)(2,1)S(1)} collective-permute-done((bf16[1,512,1024]{2,1,0:T(8,128)(2,1)}, bf16[1,512,1024]{2,1,0:T(8,128)(2,1)S(1)}, u32[]{:S(2)}, u32[]{:S(2)}) %collective-permute-start.47) | collective-permute-done | bytes 1048608 | tf_op jit(solution)/shard_map/ppermute | solution.py:37
  417.0 4.3 collective-permute-start.21
  424.4 32.2 %collective-permute-start.35 = (bf16[1,512,1024]{2,1,0:T(8,128)(2,1)S(1)}, bf16[1,512,1024]{2,1,0:T(8,128)(2,1)S(1)}, u32[]{:S(2)}, u32[]{:S(2)}) collective-permute-start(bf16[1,512,1024]{2,1,0:T(8,128)(2,1)S(1)} %copy-done.57), channel_id=1, source_target_pairs={{0,2},{2,4},{4,6},{1,3},{3,5},{5,7},{8,10},{10,12},{12,14},{9,11},... | collective-permute-start | bytes 3145736 | tf_op jit(solution)/shard_map/ppermute | solution.py:37
  457.1 3.4 constant_dynamic-update-slice_fusion.12
  462.1 17.0 %collective-permute-start.51 = (bf16[1,512,1024]{2,1,0:T(8,128)(2,1)S(1)}, bf16[1,512,1024]{2,1,0:T(8,128)(2,1)S(1)}, u32[]{:S(2)}, u32[]{:S(2)}) collective-permute-start(bf16[1,512,1024]{2,1,0:T(8,128)(2,1)S(1)} %get-tuple-element.7), channel_id=1, source_target_pairs={{0,2},{2,4},{4,6},{1,3},{3,5},{5,7},{8,10},{10,12},{12,14},{9,11},... | collective-permute-start | bytes 3145736 | tf_op jit(solution)/shard_map/ppermute | solution.py:51
  487.6 37.3 %collective-permute-start.9 = (bf16[1,512,1024]{2,1,0:T(8,128)(2,1)S(1)}, bf16[1,512,1024]{2,1,0:T(8,128)(2,1)}, u32[]{:S(2)}, u32[]{:S(2)}) collective-permute-start(bf16[1,512,1024]{2,1,0:T(8,128)(2,1)S(1)} %get-tuple-element.9), channel_id=1, source_target_pairs={{0,2},{2,4},{4,6},{1,3},{3,5},{5,7},{8,10},{10,12},{12,14},{9,11},... | collective-permute-start | bytes 3145736 | tf_op jit(solution)/shard_map/ppermute | solution.py:51
  533.0 14.9 %collective-permute-done.52 = bf16[1,512,1024]{2,1,0:T(8,128)(2,1)S(1)} collective-permute-done((bf16[1,512,1024]{2,1,0:T(8,128)(2,1)S(1)}, bf16[1,512,1024]{2,1,0:T(8,128)(2,1)S(1)}, u32[]{:S(2)}, u32[]{:S(2)}) %collective-permute-start.52) | collective-permute-done | bytes 1048608 | tf_op jit(solution)/shard_map/ppermute | solution.py:52
  548.0 21.9 %collective-permute-start.39 = (bf16[1,512,1024]{2,1,0:T(8,128)(2,1)S(1)}, bf16[1,512,1024]{2,1,0:T(8,128)(2,1)}, u32[]{:S(2)}, u32[]{:S(2)}) collective-permute-start(bf16[1,512,1024]{2,1,0:T(8,128)(2,1)S(1)} %get-tuple-element.5), channel_id=1, source_target_pairs={{0,2},{2,4},{4,6},{1,3},{3,5},{5,7},{8,10},{10,12},{12,14},{9,11},... | collective-permute-start | bytes 3145736 | tf_op jit(solution)/shard_map/ppermute | solution.py:51
  574.7 18.2 %collective-permute-done.24 = bf16[1,512,1024]{2,1,0:T(8,128)(2,1)S(1)} collective-permute-done((bf16[1,512,1024]{2,1,0:T(8,128)(2,1)S(1)}, bf16[1,512,1024]{2,1,0:T(8,128)(2,1)S(1)}, u32[]{:S(2)}, u32[]{:S(2)}) %collective-permute-start.24) | collective-permute-done | bytes 1048608 | tf_op jit(solution)/shard_map/ppermute | solution.py:52
  603.6 12.0 %collective-permute-done.40 = bf16[1,512,1024]{2,1,0:T(8,128)(2,1)} collective-permute-done((bf16[1,512,1024]{2,1,0:T(8,128)(2,1)S(1)}, bf16[1,512,1024]{2,1,0:T(8,128)(2,1)}, u32[]{:S(2)}, u32[]{:S(2)}) %collective-permute-start.40) | collective-permute-done | bytes 1048608 | tf_op jit(solution)/shard_map/ppermute | solution.py:52
  619.2 18.8 %collective-permute-done.11 = bf16[1,512,1024]{2,1,0:T(8,128)(2,1)} collective-permute-done((bf16[1,512,1024]{2,1,0:T(8,128)(2,1)}, bf16[1,512,1024]{2,1,0:T(8,128)(2,1)}, u32[]{:S(2)}, u32[]{:S(2)}) %collective-permute-start.11) | collective-permute-done | bytes 1048608 | tf_op jit(solution)/shard_map/ppermute | solution.py:52
  639.3 14.2 %convolution_convert_fusion = bf16[1024,2048]{1,0:T(8,128)(2,1)} fusion(bf16[2048,1024]{1,0:T(8,128)(2,1)} %bitcast.92, bf16[2048,2048]{1,0:T(8,128)(2,1)} %bitcast.71), kind=kOutput, calls=%fused_computation.14 | convolution fusion | flops 8592031744 | bytes 16777216 | tf_op jit(solution)/shard_map/dot_general | solution.py:14
  653.5 6.9 collective-permute-done.53
  663.4 19.4 %collective-permute-done.41 = bf16[1,512,1024]{2,1,0:T(8,128)(2,1)S(1)} collective-permute-done((bf16[1,512,1024]{2,1,0:T(8,128)(2,1)}, bf16[1,512,1024]{2,1,0:T(8,128)(2,1)S(1)}, u32[]{:S(2)}, u32[]{:S(2)}) %collective-permute-start.41) | collective-permute-done | bytes 1048608 | tf_op jit(solution)/shard_map/ppermute | solution.py:52
  684.5 20.8 %collective-permute-done.12 = bf16[1,512,1024]{2,1,0:T(8,128)(2,1)S(1)} collective-permute-done((bf16[1,512,1024]{2,1,0:T(8,128)(2,1)}, bf16[1,512,1024]{2,1,0:T(8,128)(2,1)S(1)}, u32[]{:S(2)}, u32[]{:S(2)}) %collective-permute-start.12) | collective-permute-done | bytes 1048608 | tf_op jit(solution)/shard_map/ppermute | solution.py:52
  712.3 10.0 convolution_convert_fusion.1
  724.8 21.4 %collective-permute-done.42 = bf16[1,512,1024]{2,1,0:T(8,128)(2,1)S(1)} collective-permute-done((bf16[1,512,1024]{2,1,0:T(8,128)(2,1)S(1)}, bf16[1,512,1024]{2,1,0:T(8,128)(2,1)S(1)}, u32[]{:S(2)}, u32[]{:S(2)}) %collective-permute-start.42) | collective-permute-done | bytes 1048608 | tf_op jit(solution)/shard_map/ppermute | solution.py:52
  751.8 11.1 %convolution_convert_fusion.7 = bf16[2048,1024]{1,0:T(8,128)(2,1)} fusion(bf16[2048,2048]{1,0:T(8,128)(2,1)S(1)} %bitcast.68, bf16[2048,1024]{1,0:T(8,128)(2,1)S(1)} %bitcast.88), kind=kOutput, calls=%fused_computation.21 | convolution fusion | flops 8592031744 | bytes 16777216 | tf_op jit(solution)/shard_map/dot_general | solution.py:14
  766.5 14.2 %fusion.1 = f32[2048,2048]{1,0:T(8,128)} fusion(bf16[2048,1024]{1,0:T(8,128)(2,1)S(1)} %bitcast.93, bf16[8192,2048]{1,0:T(8,128)(2,1)} %param.6, s32[]{:T(128)S(6)} %select_n.307), kind=kOutput, calls=%fused_computation.23 | convolution fusion | flops 8589934592 | bytes 25165828 | tf_op jit(solution)/shard_map/dot_general | solution.py:14
  783.1 14.3 %fusion.3 = f32[2048,2048]{1,0:T(8,128)} fusion(bf16[2048,1024]{1,0:T(8,128)(2,1)S(1)} %bitcast.90, bf16[2048,8192]{1,0:T(8,128)(2,1)} %param.5, s32[]{:T(128)S(6)} %select_n.307), kind=kOutput, calls=%fused_computation.25 | convolution fusion | flops 8589934592 | bytes 25165828 | tf_op jit(solution)/shard_map/dot_general | solution.py:14
  797.4 16.6 %add_convert_fusion = bf16[2048,2048]{1,0:T(8,128)(2,1)} fusion(f32[2048,2048]{1,0:T(8,128)} %fusion.3, bf16[2048,1024]{1,0:T(8,128)(2,1)} %bitcast.89, bf16[2048,8192]{1,0:T(8,128)(2,1)} %param.5, s32[]{:T(128)S(6)} %select_n.296), kind=kOutput, calls=%fused_computation | convolution fusion | flops 8598323200 | bytes 33554436 | tf_op jit(solution)/shard_map/dot_general | solution.py:14
  814.0 4.8 constant_dynamic-slice_fusion.14
  819.3 16.3 %add_convert_fusion.1 = bf16[2048,2048]{1,0:T(8,128)(2,1)} fusion(f32[2048,2048]{1,0:T(8,128)} %fusion.1, bf16[2048,1024]{1,0:T(8,128)(2,1)} %bitcast.95, bf16[8192,2048]{1,0:T(8,128)(2,1)} %param.6, s32[]{:T(128)S(6)} %select_n.296), kind=kOutput, calls=%fused_computation.1 | convolution fusion | flops 8598323200 | bytes 33554436 | tf_op jit(solution)/shard_map/dot_general | solution.py:14
  835.6 4.8 constant_dynamic-slice_fusion.21
  845.0 11.2 %convolution_convert_fusion.6 = bf16[2048,1024]{1,0:T(8,128)(2,1)} fusion(bf16[2048,2048]{1,0:T(8,128)(2,1)S(1)} %bitcast.69, bf16[2048,1024]{1,0:T(8,128)(2,1)S(1)} %bitcast.91), kind=kOutput, calls=%fused_computation.20 | convolution fusion | flops 8592031744 | bytes 16777216 | tf_op jit(solution)/shard_map/dot_general | solution.py:14
  865.5 25.5 %collective-permute-done.61 = bf16[512,1024]{1,0:T(8,128)(2,1)S(1)} collective-permute-done((bf16[512,1024]{1,0:T(8,128)(2,1)S(1)}, bf16[512,1024]{1,0:T(8,128)(2,1)S(1)}, u32[]{:S(2)}, u32[]{:S(2)}) %collective-permute-start.61) | collective-permute-done | bytes 1048608 | tf_op jit(solution)/shard_map/ppermute | solution.py:28
  891.2 3.4 copy-done.21
  895.6 4.7 add_convert_fusion.2
  903.5 4.1 add_convert_fusion.3
  915.7 6.0 collective-permute-start.70
  927.9 21.7 %collective-permute-done.58 = bf16[2,1,1,256,2048]{4,3,2,1,0:T(8,128)(2,1)S(1)} collective-permute-done((bf16[2,1,1,256,2048]{4,3,2,1,0:T(8,128)(2,1)}, bf16[2,1,1,256,2048]{4,3,2,1,0:T(8,128)(2,1)S(1)}, u32[]{:S(2)}, u32[]{:S(2)}) %collective-permute-start.58) | collective-permute-done | bytes 2097184 | tf_op jit(solution)/shard_map/ppermute | solution.py:28
  951.7 6.4 collective-permute-done.28
  961.5 41.4 %collective-permute-done.70 = bf16[1024,512]{1,0:T(8,128)(2,1)S(1)} collective-permute-done((bf16[1024,512]{1,0:T(8,128)(2,1)}, bf16[1024,512]{1,0:T(8,128)(2,1)S(1)}, u32[]{:S(2)}, u32[]{:S(2)}) %collective-permute-start.70) | collective-permute-done | bytes 1048608 | tf_op jit(solution)/shard_map/ppermute | solution.py:28
  1004.8 43.0 %collective-permute-done.64 = bf16[512,1024]{1,0:T(8,128)(2,1)S(1)} collective-permute-done((bf16[512,1024]{1,0:T(8,128)(2,1)}, bf16[512,1024]{1,0:T(8,128)(2,1)S(1)}, u32[]{:S(2)}, u32[]{:S(2)}) %collective-permute-start.64) | collective-permute-done | bytes 1048608 | tf_op jit(solution)/shard_map/ppermute | solution.py:28
  1050.9 18.0 %collective-permute-done.59 = bf16[1,1,1,256,2048]{4,3,2,1,0:T(8,128)(2,1)S(1)} collective-permute-done((bf16[1,1,1,256,2048]{4,3,2,1,0:T(8,128)(2,1)S(1)}, bf16[1,1,1,256,2048]{4,3,2,1,0:T(8,128)(2,1)S(1)}, u32[]{:S(2)}, u32[]{:S(2)}) %collective-permute-start.59) | collective-permute-done | bytes 1048608 | tf_op jit(solution)/shard_map/ppermute | solution.py:28
  (313 shorter events, 184.8 us)
Async XLA Ops:
  30.8 69.6 %collective-permute-start.31 = (bf16[2,1,1,256,2048]{4,3,2,1,0:T(8,128)(2,1)}, bf16[2,1,1,256,2048]{4,3,2,1,0:T(8,128)(2,1)}, u32[]{:S(2)}, u32[]{:S(2)}) collective-permute-start(bf16[2,1,1,256,2048]{4,3,2,1,0:T(8,128)(2,1)} %pad_maximum_fusion.5), channel_id=1, source_target_pairs={{0,1},{1,0},{2,3},{3,2},{4,5},{5,4},{6,7},{7,6},{8,9},{9,8},{10,11... | collective-permute-start | bytes 6291464 | tf_op jit(solution)/shard_map/ppermute | solution.py:28
  32.6 67.7 %collective-permute-start = (bf16[1,1,1,256,2048]{4,3,2,1,0:T(8,128)(2,1)S(1)}, bf16[1,1,1,256,2048]{4,3,2,1,0:T(8,128)(2,1)S(1)}, u32[]{:S(2)}, u32[]{:S(2)}) collective-permute-start(bf16[1,1,1,256,2048]{4,3,2,1,0:T(8,128)(2,1)S(1)} %bitcast.87), channel_id=1, source_target_pairs={{0,1},{1,0},{2,3},{3,2},{4,5},{5,4},{6,7},{7,6},{8,9},{9,8},{10,11... | collective-permute-start | bytes 3145736 | tf_op jit(solution)/shard_map/ppermute | solution.py:28
  105.2 51.8 %collective-permute-start.32 = (bf16[2,1,2,256,2048]{4,3,2,1,0:T(8,128)(2,1)}, bf16[2,1,2,256,2048]{4,3,2,1,0:T(8,128)(2,1)}, u32[]{:S(2)}, u32[]{:S(2)}) collective-permute-start(bf16[2,1,2,256,2048]{4,3,2,1,0:T(8,128)(2,1)} %pad_maximum_fusion.3), channel_id=1, source_target_pairs={{0,8},{8,0},{16,24},{24,16},{1,9},{9,1},{17,25},{25,17},{2,10},{10... | collective-permute-start | bytes 12582920 | tf_op jit(solution)/shard_map/ppermute | solution.py:28
  105.4 48.1 %collective-permute-start.1 = (bf16[1,1,2,256,2048]{4,3,2,1,0:T(8,128)(2,1)S(1)}, bf16[1,1,2,256,2048]{4,3,2,1,0:T(8,128)(2,1)S(1)}, u32[]{:S(2)}, u32[]{:S(2)}) collective-permute-start(bf16[1,1,2,256,2048]{4,3,2,1,0:T(8,128)(2,1)S(1)} %pad_maximum_fusion.4), channel_id=1, source_target_pairs={{0,16},{8,24},{16,0},{24,8},{1,17},{9,25},{17,1},{25,9},{2,18},{10... | collective-permute-start | bytes 6291464 | tf_op jit(solution)/shard_map/ppermute | solution.py:28
  184.0 76.2 %collective-permute-start.45 = (bf16[1,512,1024]{2,1,0:T(8,128)(2,1)}, bf16[1,512,1024]{2,1,0:T(8,128)(2,1)}, u32[]{:S(2)}, u32[]{:S(2)}) collective-permute-start(bf16[1,512,1024]{2,1,0:T(8,128)(2,1)} %get-tuple-element.38), channel_id=1, source_target_pairs={{0,2},{1,3},{8,10},{9,11},{16,18},{17,19},{24,26},{25,27}} | collective-permute-start | bytes 3145736 | tf_op jit(solution)/shard_map/ppermute | solution.py:37
  214.6 50.9 %collective-permute-start.18 = (bf16[1,512,1024]{2,1,0:T(8,128)(2,1)S(1)}, bf16[1,512,1024]{2,1,0:T(8,128)(2,1)}, u32[]{:S(2)}, u32[]{:S(2)}) collective-permute-start(bf16[1,512,1024]{2,1,0:T(8,128)(2,1)S(1)} %get-tuple-element.49), channel_id=1, source_target_pairs={{6,4},{7,5},{14,12},{15,13},{22,20},{23,21},{30,28},{31,29}} | collective-permute-start | bytes 3145736 | tf_op jit(solution)/shard_map/ppermute | solution.py:40
  230.7 37.1 %collective-permute-start.3 = (bf16[1,512,1024]{2,1,0:T(8,128)(2,1)}, bf16[1,512,1024]{2,1,0:T(8,128)(2,1)}, u32[]{:S(2)}, u32[]{:S(2)}) collective-permute-start(bf16[1,512,1024]{2,1,0:T(8,128)(2,1)} %get-tuple-element.44), channel_id=1, source_target_pairs={{0,2},{1,3},{8,10},{9,11},{16,18},{17,19},{24,26},{25,27}} | collective-permute-start | bytes 3145736 | tf_op jit(solution)/shard_map/ppermute | solution.py:37
  239.8 42.4 %collective-permute-start.16 = (bf16[1,512,1024]{2,1,0:T(8,128)(2,1)}, bf16[1,512,1024]{2,1,0:T(8,128)(2,1)}, u32[]{:S(2)}, u32[]{:S(2)}) collective-permute-start(bf16[1,512,1024]{2,1,0:T(8,128)(2,1)} %add_convert_fusion.17), channel_id=1, source_target_pairs={{0,2},{2,4},{1,3},{3,5},{8,10},{10,12},{9,11},{11,13},{16,18},{18,... | collective-permute-start | bytes 3145736 | tf_op jit(solution)/shard_map/ppermute | solution.py:37
  260.2 44.5 %collective-permute-start.33 = (bf16[1,512,1024]{2,1,0:T(8,128)(2,1)}, bf16[1,512,1024]{2,1,0:T(8,128)(2,1)}, u32[]{:S(2)}, u32[]{:S(2)}) collective-permute-start(bf16[1,512,1024]{2,1,0:T(8,128)(2,1)} %get-tuple-element.34), channel_id=1, source_target_pairs={{0,2},{1,3},{8,10},{9,11},{16,18},{17,19},{24,26},{25,27}} | collective-permute-start | bytes 3145736 | tf_op jit(solution)/shard_map/ppermute | solution.py:37
  265.5 61.6 %collective-permute-start.46 = (bf16[1,512,1024]{2,1,0:T(8,128)(2,1)}, bf16[1,512,1024]{2,1,0:T(8,128)(2,1)}, u32[]{:S(2)}, u32[]{:S(2)}) collective-permute-start(bf16[1,512,1024]{2,1,0:T(8,128)(2,1)} %add_convert_fusion.9), channel_id=1, source_target_pairs={{0,2},{2,4},{1,3},{3,5},{8,10},{10,12},{9,11},{11,13},{16,18},{18,... | collective-permute-start | bytes 3145736 | tf_op jit(solution)/shard_map/ppermute | solution.py:37
  267.8 68.7 %collective-permute-start.6 = (bf16[1,512,1024]{2,1,0:T(8,128)(2,1)S(1)}, bf16[1,512,1024]{2,1,0:T(8,128)(2,1)S(1)}, u32[]{:S(2)}, u32[]{:S(2)}) collective-permute-start(bf16[1,512,1024]{2,1,0:T(8,128)(2,1)S(1)} %get-tuple-element.45), channel_id=1, source_target_pairs={{6,4},{7,5},{14,12},{15,13},{22,20},{23,21},{30,28},{31,29}} | collective-permute-start | bytes 3145736 | tf_op jit(solution)/shard_map/ppermute | solution.py:40
  282.2 67.4 %collective-permute-start.4 = (bf16[1,512,1024]{2,1,0:T(8,128)(2,1)}, bf16[1,512,1024]{2,1,0:T(8,128)(2,1)}, u32[]{:S(2)}, u32[]{:S(2)}) collective-permute-start(bf16[1,512,1024]{2,1,0:T(8,128)(2,1)} %add_convert_fusion.21), channel_id=1, source_target_pairs={{0,2},{2,4},{1,3},{3,5},{8,10},{10,12},{9,11},{11,13},{16,18},{18,... | collective-permute-start | bytes 3145736 | tf_op jit(solution)/shard_map/ppermute | solution.py:37
  292.1 63.7 %collective-permute-start.19 = (bf16[1,512,1024]{2,1,0:T(8,128)(2,1)}, bf16[1,512,1024]{2,1,0:T(8,128)(2,1)S(1)}, u32[]{:S(2)}, u32[]{:S(2)}) collective-permute-start(bf16[1,512,1024]{2,1,0:T(8,128)(2,1)} %get-tuple-element.47), channel_id=1, source_target_pairs={{6,4},{4,2},{7,5},{5,3},{14,12},{12,10},{15,13},{13,11},{22,20},{2... | collective-permute-start | bytes 3145736 | tf_op jit(solution)/shard_map/ppermute | solution.py:40
  304.7 57.8 %collective-permute-start.36 = (bf16[1,512,1024]{2,1,0:T(8,128)(2,1)S(1)}, bf16[1,512,1024]{2,1,0:T(8,128)(2,1)}, u32[]{:S(2)}, u32[]{:S(2)}) collective-permute-start(bf16[1,512,1024]{2,1,0:T(8,128)(2,1)S(1)} %get-tuple-element.35), channel_id=1, source_target_pairs={{6,4},{7,5},{14,12},{15,13},{22,20},{23,21},{30,28},{31,29}} | collective-permute-start | bytes 3145736 | tf_op jit(solution)/shard_map/ppermute | solution.py:40
  327.2 44.9 %collective-permute-start.34 = (bf16[1,512,1024]{2,1,0:T(8,128)(2,1)}, bf16[1,512,1024]{2,1,0:T(8,128)(2,1)}, u32[]{:S(2)}, u32[]{:S(2)}) collective-permute-start(bf16[1,512,1024]{2,1,0:T(8,128)(2,1)} %add_convert_fusion.13), channel_id=1, source_target_pairs={{0,2},{2,4},{1,3},{3,5},{8,10},{10,12},{9,11},{11,13},{16,18},{18,... | collective-permute-start | bytes 3145736 | tf_op jit(solution)/shard_map/ppermute | solution.py:37
  337.5 43.0 %collective-permute-start.49 = (bf16[1,512,1024]{2,1,0:T(8,128)(2,1)}, bf16[1,512,1024]{2,1,0:T(8,128)(2,1)}, u32[]{:S(2)}, u32[]{:S(2)}) collective-permute-start(bf16[1,512,1024]{2,1,0:T(8,128)(2,1)} %get-tuple-element.37), channel_id=1, source_target_pairs={{6,4},{4,2},{7,5},{5,3},{14,12},{12,10},{15,13},{13,11},{22,20},{2... | collective-permute-start | bytes 3145736 | tf_op jit(solution)/shard_map/ppermute | solution.py:40
  355.8 38.7 %collective-permute-start.17 = (bf16[1,512,1024]{2,1,0:T(8,128)(2,1)}, bf16[1,512,1024]{2,1,0:T(8,128)(2,1)S(1)}, u32[]{:S(2)}, u32[]{:S(2)}) collective-permute-start(bf16[1,512,1024]{2,1,0:T(8,128)(2,1)} %get-tuple-element.46), channel_id=1, source_target_pairs={{0,2},{2,4},{4,6},{1,3},{3,5},{5,7},{8,10},{10,12},{12,14},{9,11},... | collective-permute-start | bytes 3145736 | tf_op jit(solution)/shard_map/ppermute | solution.py:37
  362.5 36.7 %collective-permute-start.20 = (bf16[1,512,1024]{2,1,0:T(8,128)(2,1)}, bf16[1,512,1024]{2,1,0:T(8,128)(2,1)S(1)}, u32[]{:S(2)}, u32[]{:S(2)}) collective-permute-start(bf16[1,512,1024]{2,1,0:T(8,128)(2,1)} %add_convert_fusion.14), channel_id=1, source_target_pairs={{6,4},{4,2},{2,0},{7,5},{5,3},{3,1},{14,12},{12,10},{10,8},{15,13}... | collective-permute-start | bytes 3145736 | tf_op jit(solution)/shard_map/ppermute | solution.py:40
  372.1 44.9 %collective-permute-start.47 = (bf16[1,512,1024]{2,1,0:T(8,128)(2,1)}, bf16[1,512,1024]{2,1,0:T(8,128)(2,1)S(1)}, u32[]{:S(2)}, u32[]{:S(2)}) collective-permute-start(bf16[1,512,1024]{2,1,0:T(8,128)(2,1)} %get-tuple-element.36), channel_id=1, source_target_pairs={{0,2},{2,4},{4,6},{1,3},{3,5},{5,7},{8,10},{10,12},{12,14},{9,11},... | collective-permute-start | bytes 3145736 | tf_op jit(solution)/shard_map/ppermute | solution.py:37
  380.4 40.9 %collective-permute-start.37 = (bf16[1,512,1024]{2,1,0:T(8,128)(2,1)}, bf16[1,512,1024]{2,1,0:T(8,128)(2,1)}, u32[]{:S(2)}, u32[]{:S(2)}) collective-permute-start(bf16[1,512,1024]{2,1,0:T(8,128)(2,1)} %get-tuple-element.33), channel_id=1, source_target_pairs={{6,4},{4,2},{7,5},{5,3},{14,12},{12,10},{15,13},{13,11},{22,20},{2... | collective-permute-start | bytes 3145736 | tf_op jit(solution)/shard_map/ppermute | solution.py:40
  384.4 40.0 %collective-permute-start.50 = (bf16[1,512,1024]{2,1,0:T(8,128)(2,1)S(1)}, bf16[1,512,1024]{2,1,0:T(8,128)(2,1)S(1)}, u32[]{:S(2)}, u32[]{:S(2)}) collective-permute-start(bf16[1,512,1024]{2,1,0:T(8,128)(2,1)S(1)} %add_convert_fusion.6), channel_id=1, source_target_pairs={{6,4},{4,2},{2,0},{7,5},{5,3},{3,1},{14,12},{12,10},{10,8},{15,13}... | collective-permute-start | bytes 3145736 | tf_op jit(solution)/shard_map/ppermute | solution.py:40
  394.6 65.9 %collective-permute-start.5 = (bf16[1,512,1024]{2,1,0:T(8,128)(2,1)S(1)}, bf16[1,512,1024]{2,1,0:T(8,128)(2,1)S(1)}, u32[]{:S(2)}, u32[]{:S(2)}) collective-permute-start(bf16[1,512,1024]{2,1,0:T(8,128)(2,1)S(1)} %copy-done.56), channel_id=1, source_target_pairs={{0,2},{2,4},{4,6},{1,3},{3,5},{5,7},{8,10},{10,12},{12,14},{9,11},... | collective-permute-start | bytes 3145736 | tf_op jit(solution)/shard_map/ppermute | solution.py:37
  399.2 62.9 %collective-permute-start.8 = (bf16[1,512,1024]{2,1,0:T(8,128)(2,1)S(1)}, bf16[1,512,1024]{2,1,0:T(8,128)(2,1)S(1)}, u32[]{:S(2)}, u32[]{:S(2)}) collective-permute-start(bf16[1,512,1024]{2,1,0:T(8,128)(2,1)S(1)} %add_convert_fusion.18), channel_id=1, source_target_pairs={{6,4},{4,2},{2,0},{7,5},{5,3},{3,1},{14,12},{12,10},{10,8},{15,13}... | collective-permute-start | bytes 3145736 | tf_op jit(solution)/shard_map/ppermute | solution.py:40
  417.0 62.0 %collective-permute-start.21 = (bf16[1,512,1024]{2,1,0:T(8,128)(2,1)S(1)}, bf16[1,512,1024]{2,1,0:T(8,128)(2,1)S(1)}, u32[]{:S(2)}, u32[]{:S(2)}) collective-permute-start(bf16[1,512,1024]{2,1,0:T(8,128)(2,1)S(1)} %get-tuple-element.11), channel_id=1, source_target_pairs={{0,2},{2,4},{4,6},{1,3},{3,5},{5,7},{8,10},{10,12},{12,14},{9,11},... | collective-permute-start | bytes 3145736 | tf_op jit(solution)/shard_map/ppermute | solution.py:51
  421.4 58.4 %collective-permute-start.22 = (bf16[1,512,1024]{2,1,0:T(8,128)(2,1)S(1)}, bf16[1,512,1024]{2,1,0:T(8,128)(2,1)S(1)}, u32[]{:S(2)}, u32[]{:S(2)}) collective-permute-start(bf16[1,512,1024]{2,1,0:T(8,128)(2,1)S(1)} %get-tuple-element.11), channel_id=1, source_target_pairs={{6,4},{4,2},{2,0},{7,5},{5,3},{3,1},{14,12},{12,10},{10,8},{15,13}... | collective-permute-start | bytes 3145736 | tf_op jit(solution)/shard_map/ppermute | solution.py:52
  424.4 60.0 %collective-permute-start.35 = (bf16[1,512,1024]{2,1,0:T(8,128)(2,1)S(1)}, bf16[1,512,1024]{2,1,0:T(8,128)(2,1)S(1)}, u32[]{:S(2)}, u32[]{:S(2)}) collective-permute-start(bf16[1,512,1024]{2,1,0:T(8,128)(2,1)S(1)} %copy-done.57), channel_id=1, source_target_pairs={{0,2},{2,4},{4,6},{1,3},{3,5},{5,7},{8,10},{10,12},{12,14},{9,11},... | collective-permute-start | bytes 3145736 | tf_op jit(solution)/shard_map/ppermute | solution.py:37
  462.1 62.8 %collective-permute-start.51 = (bf16[1,512,1024]{2,1,0:T(8,128)(2,1)S(1)}, bf16[1,512,1024]{2,1,0:T(8,128)(2,1)S(1)}, u32[]{:S(2)}, u32[]{:S(2)}) collective-permute-start(bf16[1,512,1024]{2,1,0:T(8,128)(2,1)S(1)} %get-tuple-element.7), channel_id=1, source_target_pairs={{0,2},{2,4},{4,6},{1,3},{3,5},{5,7},{8,10},{10,12},{12,14},{9,11},... | collective-permute-start | bytes 3145736 | tf_op jit(solution)/shard_map/ppermute | solution.py:51
  479.1 47.1 %collective-permute-start.25 = (bf16[1,512,1024]{2,1,0:T(8,128)(2,1)S(1)}, bf16[1,512,1024]{2,1,0:T(8,128)(2,1)S(1)}, u32[]{:S(2)}, u32[]{:S(2)}) collective-permute-start(bf16[1,512,1024]{2,1,0:T(8,128)(2,1)S(1)} %collective-permute-done.21), channel_id=1, source_target_pairs={{2,4},{4,6},{3,5},{5,7},{10,12},{12,14},{11,13},{13,15},{18,20},{2... | collective-permute-start | bytes 3145736 | tf_op jit(solution)/shard_map/ppermute | solution.py:51
  479.8 47.1 %collective-permute-start.23 = (bf16[1,512,1024]{2,1,0:T(8,128)(2,1)S(1)}, bf16[1,512,1024]{2,1,0:T(8,128)(2,1)S(1)}, u32[]{:S(2)}, u32[]{:S(2)}) collective-permute-start(bf16[1,512,1024]{2,1,0:T(8,128)(2,1)S(1)} %collective-permute-done.22), channel_id=1, source_target_pairs={{4,2},{2,0},{5,3},{3,1},{12,10},{10,8},{13,11},{11,9},{20,18},{18,... | collective-permute-start | bytes 3145736 | tf_op jit(solution)/shard_map/ppermute | solution.py:52
  484.3 63.6 %collective-permute-start.52 = (bf16[1,512,1024]{2,1,0:T(8,128)(2,1)S(1)}, bf16[1,512,1024]{2,1,0:T(8,128)(2,1)S(1)}, u32[]{:S(2)}, u32[]{:S(2)}) collective-permute-start(bf16[1,512,1024]{2,1,0:T(8,128)(2,1)S(1)} %get-tuple-element.7), channel_id=1, source_target_pairs={{6,4},{4,2},{2,0},{7,5},{5,3},{3,1},{14,12},{12,10},{10,8},{15,13}... | collective-permute-start | bytes 3145736 | tf_op jit(solution)/shard_map/ppermute | solution.py:52
  487.6 82.2 %collective-permute-start.9 = (bf16[1,512,1024]{2,1,0:T(8,128)(2,1)S(1)}, bf16[1,512,1024]{2,1,0:T(8,128)(2,1)}, u32[]{:S(2)}, u32[]{:S(2)}) collective-permute-start(bf16[1,512,1024]{2,1,0:T(8,128)(2,1)S(1)} %get-tuple-element.9), channel_id=1, source_target_pairs={{0,2},{2,4},{4,6},{1,3},{3,5},{5,7},{8,10},{10,12},{12,14},{9,11},... | collective-permute-start | bytes 3145736 | tf_op jit(solution)/shard_map/ppermute | solution.py:51
  524.9 46.4 %collective-permute-start.10 = (bf16[1,512,1024]{2,1,0:T(8,128)(2,1)S(1)}, bf16[1,512,1024]{2,1,0:T(8,128)(2,1)}, u32[]{:S(2)}, u32[]{:S(2)}) collective-permute-start(bf16[1,512,1024]{2,1,0:T(8,128)(2,1)S(1)} %get-tuple-element.9), channel_id=1, source_target_pairs={{6,4},{4,2},{2,0},{7,5},{5,3},{3,1},{14,12},{12,10},{10,8},{15,13}... | collective-permute-start | bytes 3145736 | tf_op jit(solution)/shard_map/ppermute | solution.py:52
  526.2 46.9 %collective-permute-start.26 = (bf16[1,512,1024]{2,1,0:T(8,128)(2,1)S(1)}, bf16[1,512,1024]{2,1,0:T(8,128)(2,1)S(1)}, u32[]{:S(2)}, u32[]{:S(2)}) collective-permute-start(bf16[1,512,1024]{2,1,0:T(8,128)(2,1)S(1)} %collective-permute-done.25), channel_id=1, source_target_pairs={{4,6},{5,7},{12,14},{13,15},{20,22},{21,23},{28,30},{29,31}} | collective-permute-start | bytes 3145736 | tf_op jit(solution)/shard_map/ppermute | solution.py:51
  527.0 65.9 %collective-permute-start.24 = (bf16[1,512,1024]{2,1,0:T(8,128)(2,1)S(1)}, bf16[1,512,1024]{2,1,0:T(8,128)(2,1)S(1)}, u32[]{:S(2)}, u32[]{:S(2)}) collective-permute-start(bf16[1,512,1024]{2,1,0:T(8,128)(2,1)S(1)} %collective-permute-done.23), channel_id=1, source_target_pairs={{2,0},{3,1},{10,8},{11,9},{18,16},{19,17},{26,24},{27,25}} | collective-permute-start | bytes 3145736 | tf_op jit(solution)/shard_map/ppermute | solution.py:52
  548.0 54.3 %collective-permute-start.39 = (bf16[1,512,1024]{2,1,0:T(8,128)(2,1)S(1)}, bf16[1,512,1024]{2,1,0:T(8,128)(2,1)}, u32[]{:S(2)}, u32[]{:S(2)}) collective-permute-start(bf16[1,512,1024]{2,1,0:T(8,128)(2,1)S(1)} %get-tuple-element.5), channel_id=1, source_target_pairs={{0,2},{2,4},{4,6},{1,3},{3,5},{5,7},{8,10},{10,12},{12,14},{9,11},... | collective-permute-start | bytes 3145736 | tf_op jit(solution)/shard_map/ppermute | solution.py:51
  569.9 45.6 %collective-permute-start.40 = (bf16[1,512,1024]{2,1,0:T(8,128)(2,1)S(1)}, bf16[1,512,1024]{2,1,0:T(8,128)(2,1)}, u32[]{:S(2)}, u32[]{:S(2)}) collective-permute-start(bf16[1,512,1024]{2,1,0:T(8,128)(2,1)S(1)} %get-tuple-element.5), channel_id=1, source_target_pairs={{6,4},{4,2},{2,0},{7,5},{5,3},{3,1},{14,12},{12,10},{10,8},{15,13}... | collective-permute-start | bytes 3145736 | tf_op jit(solution)/shard_map/ppermute | solution.py:52
  571.4 45.8 %collective-permute-start.55 = (bf16[1,512,1024]{2,1,0:T(8,128)(2,1)S(1)}, bf16[1,512,1024]{2,1,0:T(8,128)(2,1)}, u32[]{:S(2)}, u32[]{:S(2)}) collective-permute-start(bf16[1,512,1024]{2,1,0:T(8,128)(2,1)S(1)} %collective-permute-done.51), channel_id=1, source_target_pairs={{2,4},{4,6},{3,5},{5,7},{10,12},{12,14},{11,13},{13,15},{18,20},{2... | collective-permute-start | bytes 3145736 | tf_op jit(solution)/shard_map/ppermute | solution.py:51
  573.1 45.4 %collective-permute-start.13 = (bf16[1,512,1024]{2,1,0:T(8,128)(2,1)}, bf16[1,512,1024]{2,1,0:T(8,128)(2,1)}, u32[]{:S(2)}, u32[]{:S(2)}) collective-permute-start(bf16[1,512,1024]{2,1,0:T(8,128)(2,1)} %collective-permute-done.9), channel_id=1, source_target_pairs={{2,4},{4,6},{3,5},{5,7},{10,12},{12,14},{11,13},{13,15},{18,20},{2... | collective-permute-start | bytes 3145736 | tf_op jit(solution)/shard_map/ppermute | solution.py:51
  593.9 44.1 %collective-permute-start.11 = (bf16[1,512,1024]{2,1,0:T(8,128)(2,1)}, bf16[1,512,1024]{2,1,0:T(8,128)(2,1)}, u32[]{:S(2)}, u32[]{:S(2)}) collective-permute-start(bf16[1,512,1024]{2,1,0:T(8,128)(2,1)} %collective-permute-done.10), channel_id=1, source_target_pairs={{4,2},{2,0},{5,3},{3,1},{12,10},{10,8},{13,11},{11,9},{20,18},{18,... | collective-permute-start | bytes 3145736 | tf_op jit(solution)/shard_map/ppermute | solution.py:52
  602.3 58.2 %collective-permute-start.53 = (bf16[1,512,1024]{2,1,0:T(8,128)(2,1)S(1)}, bf16[1,512,1024]{2,1,0:T(8,128)(2,1)}, u32[]{:S(2)}, u32[]{:S(2)}) collective-permute-start(bf16[1,512,1024]{2,1,0:T(8,128)(2,1)S(1)} %collective-permute-done.52), channel_id=1, source_target_pairs={{4,2},{2,0},{5,3},{3,1},{12,10},{10,8},{13,11},{11,9},{20,18},{18,... | collective-permute-start | bytes 3145736 | tf_op jit(solution)/shard_map/ppermute | solution.py:52
  615.5 46.6 %collective-permute-start.43 = (bf16[1,512,1024]{2,1,0:T(8,128)(2,1)}, bf16[1,512,1024]{2,1,0:T(8,128)(2,1)}, u32[]{:S(2)}, u32[]{:S(2)}) collective-permute-start(bf16[1,512,1024]{2,1,0:T(8,128)(2,1)} %collective-permute-done.39), channel_id=1, source_target_pairs={{2,4},{4,6},{3,5},{5,7},{10,12},{12,14},{11,13},{13,15},{18,20},{2... | collective-permute-start | bytes 3145736 | tf_op jit(solution)/shard_map/ppermute | solution.py:51
  617.2 65.6 %collective-permute-start.41 = (bf16[1,512,1024]{2,1,0:T(8,128)(2,1)}, bf16[1,512,1024]{2,1,0:T(8,128)(2,1)S(1)}, u32[]{:S(2)}, u32[]{:S(2)}) collective-permute-start(bf16[1,512,1024]{2,1,0:T(8,128)(2,1)} %collective-permute-done.40), channel_id=1, source_target_pairs={{4,2},{2,0},{5,3},{3,1},{12,10},{10,8},{13,11},{11,9},{20,18},{18,... | collective-permute-start | bytes 3145736 | tf_op jit(solution)/shard_map/ppermute | solution.py:52
  618.5 90.2 %collective-permute-start.14 = (bf16[1,512,1024]{2,1,0:T(8,128)(2,1)}, bf16[1,512,1024]{2,1,0:T(8,128)(2,1)S(1)}, u32[]{:S(2)}, u32[]{:S(2)}) collective-permute-start(bf16[1,512,1024]{2,1,0:T(8,128)(2,1)} %collective-permute-done.13), channel_id=1, source_target_pairs={{4,6},{5,7},{12,14},{13,15},{20,22},{21,23},{28,30},{29,31}} | collective-permute-start | bytes 3145736 | tf_op jit(solution)/shard_map/ppermute | solution.py:51
  638.0 67.3 %collective-permute-start.12 = (bf16[1,512,1024]{2,1,0:T(8,128)(2,1)}, bf16[1,512,1024]{2,1,0:T(8,128)(2,1)S(1)}, u32[]{:S(2)}, u32[]{:S(2)}) collective-permute-start(bf16[1,512,1024]{2,1,0:T(8,128)(2,1)} %collective-permute-done.11), channel_id=1, source_target_pairs={{2,0},{3,1},{10,8},{11,9},{18,16},{19,17},{26,24},{27,25}} | collective-permute-start | bytes 3145736 | tf_op jit(solution)/shard_map/ppermute | solution.py:52
  660.4 120.2 %collective-permute-start.56 = (bf16[1,512,1024]{2,1,0:T(8,128)(2,1)}, bf16[1,512,1024]{2,1,0:T(8,128)(2,1)}, u32[]{:S(2)}, u32[]{:S(2)}) collective-permute-start(bf16[1,512,1024]{2,1,0:T(8,128)(2,1)} %collective-permute-done.55), channel_id=1, source_target_pairs={{4,6},{5,7},{12,14},{13,15},{20,22},{21,23},{28,30},{29,31}} | collective-permute-start | bytes 3145736 | tf_op jit(solution)/shard_map/ppermute | solution.py:51
  662.1 100.9 %collective-permute-start.54 = (bf16[1,512,1024]{2,1,0:T(8,128)(2,1)}, bf16[1,512,1024]{2,1,0:T(8,128)(2,1)}, u32[]{:S(2)}, u32[]{:S(2)}) collective-permute-start(bf16[1,512,1024]{2,1,0:T(8,128)(2,1)} %collective-permute-done.53), channel_id=1, source_target_pairs={{2,0},{3,1},{10,8},{11,9},{18,16},{19,17},{26,24},{27,25}} | collective-permute-start | bytes 3145736 | tf_op jit(solution)/shard_map/ppermute | solution.py:52
  682.8 67.2 %collective-permute-start.44 = (bf16[1,512,1024]{2,1,0:T(8,128)(2,1)}, bf16[1,512,1024]{2,1,0:T(8,128)(2,1)}, u32[]{:S(2)}, u32[]{:S(2)}) collective-permute-start(bf16[1,512,1024]{2,1,0:T(8,128)(2,1)} %collective-permute-done.43), channel_id=1, source_target_pairs={{4,6},{5,7},{12,14},{13,15},{20,22},{21,23},{28,30},{29,31}} | collective-permute-start | bytes 3145736 | tf_op jit(solution)/shard_map/ppermute | solution.py:51
  705.3 40.9 %collective-permute-start.42 = (bf16[1,512,1024]{2,1,0:T(8,128)(2,1)S(1)}, bf16[1,512,1024]{2,1,0:T(8,128)(2,1)S(1)}, u32[]{:S(2)}, u32[]{:S(2)}) collective-permute-start(bf16[1,512,1024]{2,1,0:T(8,128)(2,1)S(1)} %collective-permute-done.41), channel_id=1, source_target_pairs={{2,0},{3,1},{10,8},{11,9},{18,16},{19,17},{26,24},{27,25}} | collective-permute-start | bytes 3145736 | tf_op jit(solution)/shard_map/ppermute | solution.py:52
  724.8 118.2 %collective-permute-start.68 = (bf16[1024,512]{1,0:T(8,128)(2,1)}, bf16[1024,512]{1,0:T(8,128)(2,1)}, u32[]{:S(2)}, u32[]{:S(2)}) collective-permute-start(bf16[1024,512]{1,0:T(8,128)(2,1)} %get-tuple-element.20), channel_id=1, source_target_pairs={{0,24},{8,16},{16,8},{24,0},{1,25},{9,17},{17,9},{25,1},{2,26},{10... | collective-permute-start | bytes 3145736 | tf_op jit(solution)/shard_map/ppermute | solution.py:28
  746.2 97.5 %collective-permute-start.67 = (bf16[1024,512]{1,0:T(8,128)(2,1)}, bf16[1024,512]{1,0:T(8,128)(2,1)}, u32[]{:S(2)}, u32[]{:S(2)}) collective-permute-start(bf16[1024,512]{1,0:T(8,128)(2,1)} %get-tuple-element.21), channel_id=1, source_target_pairs={{0,16},{8,24},{16,0},{24,8},{1,17},{9,25},{17,1},{25,9},{2,18},{10... | collective-permute-start | bytes 3145736 | tf_op jit(solution)/shard_map/ppermute | solution.py:28
  750.0 94.8 %collective-permute-start.66 = (bf16[1024,512]{1,0:T(8,128)(2,1)S(1)}, bf16[1024,512]{1,0:T(8,128)(2,1)}, u32[]{:S(2)}, u32[]{:S(2)}) collective-permute-start(bf16[1024,512]{1,0:T(8,128)(2,1)S(1)} %get-tuple-element.22), channel_id=1, source_target_pairs={{0,8},{8,0},{16,24},{24,16},{1,9},{9,1},{17,25},{25,17},{2,10},{10... | collective-permute-start | bytes 3145736 | tf_op jit(solution)/shard_map/ppermute | solution.py:28
  818.8 76.8 %collective-permute-start.57 = (bf16[2,1,2,256,2048]{4,3,2,1,0:T(8,128)(2,1)}, bf16[2,1,2,256,2048]{4,3,2,1,0:T(8,128)(2,1)}, u32[]{:S(2)}, u32[]{:S(2)}) collective-permute-start(bf16[2,1,2,256,2048]{4,3,2,1,0:T(8,128)(2,1)} %constant_dynamic-slice_fusion.14), channel_id=1, source_target_pairs={{0,8},{8,0},{16,24},{24,16},{1,9},{9,1},{17,25},{25,17},{2,10},{10... | collective-permute-start | bytes 12582920 | tf_op jit(solution)/shard_map/ppermute | solution.py:28
  840.4 63.1 %collective-permute-start.27 = (bf16[2,1,2,256,2048]{4,3,2,1,0:T(8,128)(2,1)}, bf16[2,1,2,256,2048]{4,3,2,1,0:T(8,128)(2,1)}, u32[]{:S(2)}, u32[]{:S(2)}) collective-permute-start(bf16[2,1,2,256,2048]{4,3,2,1,0:T(8,128)(2,1)} %constant_dynamic-slice_fusion.21), channel_id=1, source_target_pairs={{0,8},{8,0},{16,24},{24,16},{1,9},{9,1},{17,25},{25,17},{2,10},{10... | collective-permute-start | bytes 12582920 | tf_op jit(solution)/shard_map/ppermute | solution.py:28
  843.0 51.5 %collective-permute-start.62 = (bf16[512,1024]{1,0:T(8,128)(2,1)S(1)}, bf16[512,1024]{1,0:T(8,128)(2,1)S(1)}, u32[]{:S(2)}, u32[]{:S(2)}) collective-permute-start(bf16[512,1024]{1,0:T(8,128)(2,1)S(1)} %get-tuple-element.28), channel_id=1, source_target_pairs={{0,24},{8,16},{16,8},{24,0},{1,25},{9,17},{17,9},{25,1},{2,26},{10... | collective-permute-start | bytes 3145736 | tf_op jit(solution)/shard_map/ppermute | solution.py:28
  843.7 47.3 %collective-permute-start.61 = (bf16[512,1024]{1,0:T(8,128)(2,1)S(1)}, bf16[512,1024]{1,0:T(8,128)(2,1)S(1)}, u32[]{:S(2)}, u32[]{:S(2)}) collective-permute-start(bf16[512,1024]{1,0:T(8,128)(2,1)S(1)} %get-tuple-element.29), channel_id=1, source_target_pairs={{0,16},{8,24},{16,0},{24,8},{1,17},{9,25},{17,1},{25,9},{2,18},{10... | collective-permute-start | bytes 3145736 | tf_op jit(solution)/shard_map/ppermute | solution.py:28
  865.1 50.6 %collective-permute-start.69 = (bf16[1024,512]{1,0:T(8,128)(2,1)}, bf16[1024,512]{1,0:T(8,128)(2,1)}, u32[]{:S(2)}, u32[]{:S(2)}) collective-permute-start(bf16[1024,512]{1,0:T(8,128)(2,1)} %get-tuple-element.18), channel_id=1, source_target_pairs={{0,8},{8,0},{16,24},{24,16},{1,9},{9,1},{17,25},{25,17},{2,10},{10... | collective-permute-start | bytes 3145736 | tf_op jit(solution)/shard_map/ppermute | solution.py:28
  902.0 47.7 %collective-permute-start.58 = (bf16[2,1,1,256,2048]{4,3,2,1,0:T(8,128)(2,1)}, bf16[2,1,1,256,2048]{4,3,2,1,0:T(8,128)(2,1)S(1)}, u32[]{:S(2)}, u32[]{:S(2)}) collective-permute-start(bf16[2,1,1,256,2048]{4,3,2,1,0:T(8,128)(2,1)} %constant_dynamic-slice_fusion.13), channel_id=1, source_target_pairs={{0,1},{1,0},{2,3},{3,2},{4,5},{5,4},{6,7},{7,6},{8,9},{9,8},{10,11... | collective-permute-start | bytes 6291464 | tf_op jit(solution)/shard_map/ppermute | solution.py:28
  909.2 48.9 %collective-permute-start.28 = (bf16[1,1,2,256,2048]{4,3,2,1,0:T(8,128)(2,1)}, bf16[1,1,2,256,2048]{4,3,2,1,0:T(8,128)(2,1)}, u32[]{:S(2)}, u32[]{:S(2)}) collective-permute-start(bf16[1,1,2,256,2048]{4,3,2,1,0:T(8,128)(2,1)} %constant_dynamic-slice_fusion.20), channel_id=1, source_target_pairs={{0,16},{8,24},{16,0},{24,8},{1,17},{9,25},{17,1},{25,9},{2,18},{10... | collective-permute-start | bytes 6291464 | tf_op jit(solution)/shard_map/ppermute | solution.py:28
  914.1 134.7 %collective-permute-start.71 = (bf16[1024,512]{1,0:T(8,128)(2,1)S(1)}, bf16[1024,512]{1,0:T(8,128)(2,1)S(1)}, u32[]{:S(2)}, u32[]{:S(2)}) collective-permute-start(bf16[1024,512]{1,0:T(8,128)(2,1)S(1)} %get-tuple-element.16), channel_id=1, source_target_pairs={{0,24},{8,16},{16,8},{24,0},{1,25},{9,17},{17,9},{25,1},{2,26},{10... | collective-permute-start | bytes 3145736 | tf_op jit(solution)/shard_map/ppermute | solution.py:28
  915.7 87.1 %collective-permute-start.70 = (bf16[1024,512]{1,0:T(8,128)(2,1)}, bf16[1024,512]{1,0:T(8,128)(2,1)S(1)}, u32[]{:S(2)}, u32[]{:S(2)}) collective-permute-start(bf16[1024,512]{1,0:T(8,128)(2,1)} %get-tuple-element.17), channel_id=1, source_target_pairs={{0,16},{8,24},{16,0},{24,8},{1,17},{9,25},{17,1},{25,9},{2,18},{10... | collective-permute-start | bytes 3145736 | tf_op jit(solution)/shard_map/ppermute | solution.py:28
  924.0 125.9 %collective-permute-start.65 = (bf16[512,1024]{1,0:T(8,128)(2,1)}, bf16[512,1024]{1,0:T(8,128)(2,1)S(1)}, u32[]{:S(2)}, u32[]{:S(2)}) collective-permute-start(bf16[512,1024]{1,0:T(8,128)(2,1)} %get-tuple-element.24), channel_id=1, source_target_pairs={{0,24},{8,16},{16,8},{24,0},{1,25},{9,17},{17,9},{25,1},{2,26},{10... | collective-permute-start | bytes 3145736 | tf_op jit(solution)/shard_map/ppermute | solution.py:28
  949.7 98.2 %collective-permute-start.64 = (bf16[512,1024]{1,0:T(8,128)(2,1)}, bf16[512,1024]{1,0:T(8,128)(2,1)S(1)}, u32[]{:S(2)}, u32[]{:S(2)}) collective-permute-start(bf16[512,1024]{1,0:T(8,128)(2,1)} %get-tuple-element.25), channel_id=1, source_target_pairs={{0,16},{8,24},{16,0},{24,8},{1,17},{9,25},{17,1},{25,9},{2,18},{10... | collective-permute-start | bytes 3145736 | tf_op jit(solution)/shard_map/ppermute | solution.py:28
  958.0 110.9 %collective-permute-start.59 = (bf16[1,1,1,256,2048]{4,3,2,1,0:T(8,128)(2,1)S(1)}, bf16[1,1,1,256,2048]{4,3,2,1,0:T(8,128)(2,1)S(1)}, u32[]{:S(2)}, u32[]{:S(2)}) collective-permute-start(bf16[1,1,1,256,2048]{4,3,2,1,0:T(8,128)(2,1)S(1)} %constant_dynamic-slice_fusion.12), channel_id=1, source_target_pairs={{0,16},{8,24},{16,0},{24,8},{1,17},{9,25},{17,1},{25,9},{2,18},{10... | collective-permute-start | bytes 3145736 | tf_op jit(solution)/shard_map/ppermute | solution.py:28
  1002.9 67.5 %collective-permute-start.29 = (bf16[1,1,1,256,2048]{4,3,2,1,0:T(8,128)(2,1)S(1)}, bf16[1,1,1,256,2048]{4,3,2,1,0:T(8,128)(2,1)S(1)}, u32[]{:S(2)}, u32[]{:S(2)}) collective-permute-start(bf16[1,1,1,256,2048]{4,3,2,1,0:T(8,128)(2,1)S(1)} %constant_dynamic-slice_fusion.19), channel_id=1, source_target_pairs={{0,1},{1,0},{2,3},{3,2},{4,5},{5,4},{6,7},{7,6},{8,9},{9,8},{10,11... | collective-permute-start | bytes 3145736 | tf_op jit(solution)/shard_map/ppermute | solution.py:28
  (77 other events, 1700.8 us)

commit v2 on v1

v2 whole, which is shorter than its diff:
```python
import jax
import jax.numpy as jnp
from jax import lax
from jax.sharding import PartitionSpec as P

PARTS = 2


def gelu_fn(values):
    return jax.nn.gelu(values, approximate=True)


def contract(left, right, left_dim, right_dim):
    return lax.dot_general(
        left, right, (((left_dim,), (right_dim,)), ((), ())), preferred_element_type=jnp.float32
    )


def swap(array, axis, size, mask):
    return lax.ppermute(array, axis, [(k, k ^ mask) for k in range(size)])


def sum_over_row(part):
    return lax.psum_scatter(part, "row", scatter_dimension=0, tiled=True)


def gather_over_row(own, n):
    me = lax.axis_index("row")
    right = left = own
    rights, lefts = [], []
    for t in range(n - 1):
        right = lax.ppermute(right, "row", [(k, k + 1) for k in range(t, n - 1)])
        left = lax.ppermute(left, "row", [(k, k - 1) for k in range(n - 1 - t, 0, -1)])
        rights.append(right)
        lefts.append(left)
    whole = jnp.zeros((n,) + own.shape[1:], own.dtype)
    whole = lax.dynamic_update_slice_in_dim(whole, own, me, 0)
    for t in range(n - 1):
        block = jnp.where(me >= t + 1, rights[t], lefts[n - 2 - t])
        whole = lax.dynamic_update_slice_in_dim(whole, block, lax.rem(me + n - 1 - t, n), 0)
    return whole


def solution(mesh):
    n_dp, n_row, n_col = mesh.shape["dp"], mesh.shape["row"], mesh.shape["col"]
    dp_bits, col_bits = n_dp.bit_length() - 1, n_col.bit_length() - 1
    digits = [("dp", n_dp, 1 << b) for b in reversed(range(dp_bits))]
    digits += [("col", n_col, 1 << b) for b in reversed(range(col_bits))]
    core = [dp_bits - 1]
    far = list(range(dp_bits - 1))
    cols = list(range(dp_bits, dp_bits + col_bits))

    def digit(d):
        axis, _, weight = digits[d]
        return lax.rem(lax.axis_index(axis) // weight, 2)

    def gather_tokens(block, order):
        array = block.reshape((1,) * len(digits) + block.shape)
        for d in order:
            axis, size, weight = digits[d]
            other = swap(array, axis, size, weight)
            low = digit(d) == 0
            array = jnp.concatenate(
                [jnp.where(low, array, other), jnp.where(low, other, array)], axis=d
            )
        return array.reshape(-1, block.shape[-1])

    def scatter_tokens(part):
        return lax.psum_scatter(
            part.astype(jnp.bfloat16), ("dp", "col"), scatter_dimension=0, tiled=True
        ).astype(jnp.float32)

    def shards(inputs, w_in, w_out, grad_outputs):
        dp = lax.axis_index("dp")
        model, hidden = w_in.shape
        share = hidden // n_dp
        width = share // PARTS
        piece = model // n_dp

        all_in = lax.all_gather(inputs, ("dp", "col"), axis=0, tiled=True)
        all_cot = gather_tokens(grad_outputs, far + cols + core)
        tokens = all_in.shape[0]

        def blocks_of_peers(whole, dim):
            return [
                lax.dynamic_slice_in_dim(whole, (dp ^ mask) * piece, piece, dim)
                for mask in range(n_dp)
            ]

        def exchange(blocks):
            return [
                swap(block, "dp", n_dp, mask) if mask else block
                for mask, block in enumerate(blocks)
            ]

        firsts = [dp * share + h * width for h in range(PARTS)]
        w_ins = [lax.dynamic_slice_in_dim(w_in, first, width, 1) for first in firsts]
        w_outs = [lax.dynamic_slice_in_dim(w_out, first, width, 0) for first in firsts]

        units = [(back, h) for h in range(PARTS) for back in range(2)]
        parts = [
            contract(all_cot, w_outs[h], 1, 1) if back else contract(all_in, w_ins[h], 1, 0)
            for back, h in units
        ]
        parts = [part.astype(jnp.bfloat16) for part in parts]
        early = [sum_over_row(part) for part in parts[:2]]
        held = lax.optimization_barrier((early[0], *parts[2:]))
        sums = [held[0], early[1]] + [sum_over_row(part) for part in held[1:]]

        totals = [None, None]
        received = {}

        def products(u, every):
            back, h = units[u]
            if back:
                blocks = blocks_of_peers(contract(all_in, every, 0, 0).astype(jnp.bfloat16), 0)
                term = contract(every, w_ins[h], 1, 1)
            else:
                blocks = blocks_of_peers(contract(every, all_cot, 0, 0).astype(jnp.bfloat16), 1)
                term = contract(every, w_outs[h], 1, 0)
            received[units[u]] = exchange(blocks)
            totals[back] = term if totals[back] is None else totals[back] + term

        preact = every = None
        for u, (back, h) in enumerate(units):
            total = sums[u]
            if u >= 1:
                total, every = lax.optimization_barrier((total, every))
            if u >= 2:
                held = (total, every, received[units[u - 2]], totals[units[u - 2][0]])
                total, every, received[units[u - 2]], totals[units[u - 2][0]] = (
                    lax.optimization_barrier(held)
                )
            if u >= 1:
                products(u - 1, every)
            total = total.astype(jnp.float32)
            if back:
                own = jax.vjp(gelu_fn, preact)[1](total)[0].astype(jnp.bfloat16)
            else:
                preact = total
                own = gelu_fn(preact).astype(jnp.bfloat16)
            every = gather_over_row(own[None], n_row).reshape(tokens, width)
        last = len(units) - 1
        out_sum = scatter_tokens(totals[0])
        every, received[units[last - 1]] = lax.optimization_barrier(
            (every, received[units[last - 1]])
        )
        products(last, every)
        out_sum, input_total = lax.optimization_barrier((out_sum, totals[1].astype(jnp.bfloat16)))
        input_sum = scatter_tokens(input_total)

        grad_w_in = jnp.zeros((piece, hidden), jnp.bfloat16)
        grad_w_out = jnp.zeros((hidden, piece), jnp.bfloat16)
        for h in range(PARTS):
            for mask in range(n_dp):
                place = (dp ^ mask) * share + h * width
                grad_w_out = lax.dynamic_update_slice_in_dim(
                    grad_w_out, received[0, h][mask], place, 0
                )
                grad_w_in = lax.dynamic_update_slice_in_dim(grad_w_in, received[1, h][mask], place, 1)
        outputs = inputs.astype(jnp.float32) + out_sum
        grad_inputs = grad_outputs.astype(jnp.float32) + input_sum
        return (
            outputs.astype(jnp.bfloat16),
            grad_inputs.astype(jnp.bfloat16),
            grad_w_in,
            grad_w_out,
        )

    return jax.shard_map(
        shards,
        mesh=mesh,
        in_specs=(
            P(("dp", "col"), "row"),
            P("row", "col"),
            P("col", "row"),
            P(("dp", "col"), "row"),
        ),
        out_specs=(
            P(("dp", "col"), "row"),
            P(("dp", "col"), "row"),
            P(("row", "dp"), "col"),
            P("col", ("row", "dp")),
        ),
        check_vma=False,
    )
```

time: 1080 us -> 1040 us (0.963)
  starting transfers between devices: 226 us -> 59.1 us
  waiting for transfers between devices: 515 us -> 593 us
  local copies, waits for them, and re-layouts: 62.2 us -> 117 us
  other arithmetic: 112 us -> 76.5 us
  between operations: 2.61 us -> 15.1 us
  matrix products: 155 us -> 166 us
    ppermute x24 -> x15, waiting for transfers between devices: 293 us -> 176 us  [swap(): return lax.ppermute(array, axis, [(k, k ^ mask) for k in range(size)])]
    ppermute x12, waiting for transfers between devices: 0.03 us -> 116 us  [gather_over_row(): right = lax.ppermute(right, 'row', [(k, k + 1) for k in range(t, n - 1)])]
    ppermute x12, waiting for transfers between devices: 132 us -> 244 us  [gather_over_row(): lax.ppermute(left, 'row', [(k, k - 1) for k in range(n - 1 - t, 0, -1)])]
    ppermute x24 -> x0, starting transfers between devices: 94.1 us -> none  [the longest x12 76.3 us: sum_over_row(): right = lax.ppermute(block, 'row', [(k, k + 1) for k in range(t + 1)])]
    ppermute x24 -> x0, waiting for transfers between devices: 88.7 us -> none  [the longest x12 86.7 us: sum_over_row(): right = lax.ppermute(block, 'row', [(k, k + 1) for k in range(t + 1)])]
    ppermute x12, starting transfers between devices: 90.9 us -> 29.6 us  [gather_over_row(): right = lax.ppermute(right, 'row', [(k, k + 1) for k in range(t, n - 1)])]
    all_gather x0 -> x1, waiting for transfers between devices: none -> 50.5 us  [shards(): all_in = lax.all_gather(inputs, ('dp', 'col'), axis=0, tiled=True)]
    dynamic_update_slice x12 -> x32, local copies, waits for them, and re-layouts: 17 us -> 44.7 us  [the longest x12 17.4 us: gather_over_row(): lax.dynamic_update_slice_in_dim(whole, block, lax.rem(me + n - 1 - t, n), 0)]
  transfers between devices with their start and end apart: 72 -> 46, of which waited for: 27 -> 26; matrix products, arithmetic and copies ran while one was open for 28% -> 31% of each run, Pallas kernels for 0% -> 0%
where the time goes in v2:
time: 1040 us; the launch traced here: 1030 us
  waiting for transfers between devices  593 us (57%)
  matrix products  166 us (16%)
  local copies, waits for them, and re-layouts  117 us (11%)
  other arithmetic  76.5 us (7%)
  starting transfers between devices  59.1 us (6%)
  between operations  15.1 us (1%)
    ppermute x12, waiting for transfers between devices, gather_over_row(): lax.ppermute(left, 'row', [(k, k - 1) for k in range(n - 1 - t, 0, -1)])  244 us
    ppermute x15, waiting for transfers between devices, swap(): return lax.ppermute(array, axis, [(k, k ^ mask) for k in range(size)])  176 us
    dot_general x12, matrix products, contract(): lax.dot_general(left, right, (((left_dim,), (right_dim,)), ((), ())), pre...  166 us
    ppermute x12, waiting for transfers between devices, gather_over_row(): right = lax.ppermute(right, 'row', [(k, k + 1) for k in range(t, n - 1)])  116 us
    all_gather x1, waiting for transfers between devices, shards(): all_in = lax.all_gather(inputs, ('dp', 'col'), axis=0, tiled=True)  50.5 us
    ppermute x12, starting transfers between devices, gather_over_row(): right = lax.ppermute(right, 'row', [(k, k + 1) for k in range(t, n - 1)])  29.6 us
    select_n x12, other arithmetic, gather_over_row(): block = jnp.where(me >= t + 1, rights[t], lefts[n - 2 - t])  23.9 us
  transfers between devices with their start and end apart: 46, of which 26 were waited for; matrix products, arithmetic and copies ran while one was open for 31% of the time, Pallas kernels for 0%

profile of v2, /device:TPU:0, one launch (start us, length us, event | category | flops | bytes accessed | tf_op | source)
XLA Modules:
  0.0 1027.0 jit_solution(17119324432958518871)
XLA Ops:
  7.9 3.0 collective-permute-start
  10.9 34.6 %collective-permute-done = bf16[1,1,1,256,2048]{4,3,2,1,0:T(8,128)(2,1)S(1)} collective-permute-done((bf16[1,1,1,256,2048]{4,3,2,1,0:T(8,128)(2,1)}, bf16[1,1,1,256,2048]{4,3,2,1,0:T(8,128)(2,1)S(1)}, u32[]{:S(2)}, u32[]{:S(2)}) %collective-permute-start) | collective-permute-done | bytes 1048608 | tf_op jit(solution)/shard_map/ppermute | solution.py:20
  49.9 50.5 %all-gather.2.cloned.1.call-done = bf16[2048,2048]{1,0:T(8,128)(2,1)} async-done(((bf16[256,2048]{1,0:T(8,128)(2,1)}), bf16[2048,2048]{1,0:T(8,128)(2,1)}) %all-gather.2.cloned.1.call-update) | async-done | bytes 8388624 | tf_op jit(solution)/shard_map/all_gather | solution.py:80
  100.4 13.9 %convert_bitcast_fusion.1 = bf16[2048,1024]{0,1:T(8,128)(2,1)} fusion(bf16[2048,2048]{1,0:T(8,128)(2,1)} %all-gather.2.cloned.1.call-done, bf16[2048,8192]{1,0:T(8,128)(2,1)} %param.5, s32[]{:T(128)S(6)} %select_n.183), kind=kOutput, calls=%fused_computation.15 | convolution fusion | flops 8592031744 | bytes 16777220 | tf_op jit(solution)/shard_map/dot_general | solution.py:14
  118.8 2.6 pad_maximum_fusion.1
  121.7 7.5 collective-permute-done.2
  129.2 5.5 broadcast_select_fusion.1
  134.7 7.7 pad_maximum_fusion
  142.4 13.9 %convolution_convert_fusion.4 = bf16[2048,1024]{0,1:T(8,128)(2,1)} fusion(bf16[2048,2048]{1,0:T(8,128)(2,1)} %bitcast.54, bf16[8192,2048]{1,0:T(8,128)(2,1)} %param.6, s32[]{:T(128)S(6)} %select_n.183), kind=kOutput, calls=%fused_computation.22 | convolution fusion | flops 8592031744 | bytes 16777220 | tf_op jit(solution)/shard_map/dot_general | solution.py:14
  156.8 13.9 %convolution_convert_fusion.5 = bf16[2048,1024]{0,1:T(8,128)(2,1)} fusion(bf16[2048,2048]{1,0:T(8,128)(2,1)} %bitcast.55, bf16[8192,2048]{1,0:T(8,128)(2,1)} %param.6, s32[]{:T(128)S(6)} %select_n.184), kind=kOutput, calls=%fused_computation.23 | convolution fusion | flops 8592031744 | bytes 16777220 | tf_op jit(solution)/shard_map/dot_general | solution.py:14
  170.8 14.0 %convert_bitcast_fusion = bf16[2048,1024]{0,1:T(8,128)(2,1)} fusion(bf16[2048,2048]{1,0:T(8,128)(2,1)} %all-gather.2.cloned.1.call-done, bf16[2048,8192]{1,0:T(8,128)(2,1)} %param.5, s32[]{:T(128)S(6)} %select_n.184), kind=kOutput, calls=%fused_computation.14 | convolution fusion | flops 8592031744 | bytes 16777220 | tf_op jit(solution)/shard_map/dot_general | solution.py:14
  184.8 6.4 reduce-scatter.7.cloned.1.call-done
  193.1 3.5 collective-permute-start.3
  197.9 41.1 %collective-permute-done.3 = bf16[1,512,1024]{1,2,0:T(8,128)(2,1)S(1)} collective-permute-done((bf16[1,512,1024]{1,2,0:T(8,128)(2,1)S(1)}, bf16[1,512,1024]{1,2,0:T(8,128)(2,1)S(1)}, u32[]{:S(2)}, u32[]{:S(2)}) %collective-permute-start.3) | collective-permute-done | bytes 1048608 | tf_op jit(solution)/shard_map/ppermute | solution.py:32
  240.6 27.9 %collective-permute-done.4 = bf16[1,512,1024]{1,2,0:T(8,128)(2,1)S(1)} collective-permute-done((bf16[1,512,1024]{1,2,0:T(8,128)(2,1)S(1)}, bf16[1,512,1024]{1,2,0:T(8,128)(2,1)S(1)}, u32[]{:S(2)}, u32[]{:S(2)}) %collective-permute-start.4) | collective-permute-done | bytes 1048608 | tf_op jit(solution)/shard_map/ppermute | solution.py:33
  271.5 47.1 %collective-permute-done.5 = bf16[1,512,1024]{1,2,0:T(8,128)(2,1)} collective-permute-done((bf16[1,512,1024]{1,2,0:T(8,128)(2,1)S(1)}, bf16[1,512,1024]{1,2,0:T(8,128)(2,1)}, u32[]{:S(2)}, u32[]{:S(2)}) %collective-permute-start.5) | collective-permute-done | bytes 1048608 | tf_op jit(solution)/shard_map/ppermute | solution.py:33
  325.1 2.3 broadcast_select_fusion.7
  328.9 67.0 %collective-permute-done.6 = bf16[1,512,1024]{1,2,0:T(8,128)(2,1)} collective-permute-done((bf16[1,512,1024]{1,2,0:T(8,128)(2,1)}, bf16[1,512,1024]{1,2,0:T(8,128)(2,1)}, u32[]{:S(2)}, u32[]{:S(2)}) %collective-permute-start.6) | collective-permute-done | bytes 1048608 | tf_op jit(solution)/shard_map/ppermute | solution.py:33
  404.9 2.8 fusion.37
  410.6 31.8 %collective-permute-done.9 = bf16[1,512,1024]{1,2,0:T(8,128)(2,1)S(1)} collective-permute-done((bf16[1,512,1024]{1,2,0:T(8,128)(2,1)S(1)}, bf16[1,512,1024]{1,2,0:T(8,128)(2,1)S(1)}, u32[]{:S(2)}, u32[]{:S(2)}) %collective-permute-start.9) | collective-permute-done | bytes 1048608 | tf_op jit(solution)/shard_map/ppermute | solution.py:32
  444.0 23.7 %collective-permute-done.10 = bf16[1,512,1024]{1,2,0:T(8,128)(2,1)S(1)} collective-permute-done((bf16[1,512,1024]{1,2,0:T(8,128)(2,1)S(1)}, bf16[1,512,1024]{1,2,0:T(8,128)(2,1)S(1)}, u32[]{:S(2)}, u32[]{:S(2)}) %collective-permute-start.10) | collective-permute-done | bytes 1048608 | tf_op jit(solution)/shard_map/ppermute | solution.py:33
  469.0 14.1 %convolution_convert_fusion.3 = bf16[1024,2048]{1,0:T(8,128)(2,1)} fusion(bf16[2048,1024]{1,0:T(8,128)(2,1)} %bitcast.61, bf16[2048,2048]{1,0:T(8,128)(2,1)} %bitcast.56), kind=kOutput, calls=%fused_computation.21 | convolution fusion | flops 8592031744 | bytes 16777216 | tf_op jit(solution)/shard_map/dot_general | solution.py:14
  484.8 38.6 %collective-permute-done.11 = bf16[1,512,1024]{1,2,0:T(8,128)(2,1)} collective-permute-done((bf16[1,512,1024]{1,2,0:T(8,128)(2,1)S(1)}, bf16[1,512,1024]{1,2,0:T(8,128)(2,1)}, u32[]{:S(2)}, u32[]{:S(2)}) %collective-permute-start.11) | collective-permute-done | bytes 1048608 | tf_op jit(solution)/shard_map/ppermute | solution.py:33
  524.9 14.0 %fusion = f32[2048,2048]{1,0:T(8,128)} fusion(bf16[2048,1024]{1,0:T(8,128)(2,1)S(1)} %bitcast.62, bf16[8192,2048]{1,0:T(8,128)(2,1)} %param.6, s32[]{:T(128)S(6)} %select_n.183), kind=kOutput, calls=%fused_computation.24 | convolution fusion | flops 8589934592 | bytes 25165828 | tf_op jit(solution)/shard_map/dot_general | solution.py:14
  539.4 4.0 constant_dynamic-slice_fusion.4
  549.8 2.3 broadcast_select_fusion.6
  553.6 2.3 broadcast_select_fusion.14
  562.5 7.1 collective-permute-done.16
  569.7 21.7 %collective-permute-done.17 = bf16[1024,512]{1,0:T(8,128)(2,1)} collective-permute-done((bf16[1024,512]{1,0:T(8,128)(2,1)}, bf16[1024,512]{1,0:T(8,128)(2,1)}, u32[]{:S(2)}, u32[]{:S(2)}) %collective-permute-start.17) | collective-permute-done | bytes 1048608 | tf_op jit(solution)/shard_map/ppermute | solution.py:20
  593.3 5.8 collective-permute-start.18
  600.5 21.4 %collective-permute-done.18 = bf16[1,512,1024]{1,2,0:T(8,128)(2,1)S(1)} collective-permute-done((bf16[1,512,1024]{1,2,0:T(8,128)(2,1)S(1)}, bf16[1,512,1024]{1,2,0:T(8,128)(2,1)S(1)}, u32[]{:S(2)}, u32[]{:S(2)}) %collective-permute-start.18) | collective-permute-done | bytes 1048608 | tf_op jit(solution)/shard_map/ppermute | solution.py:32
  623.5 3.0 collective-permute-done.19
  627.8 14.0 %convolution_convert_fusion.2 = bf16[1024,2048]{1,0:T(8,128)(2,1)} fusion(bf16[2048,1024]{1,0:T(8,128)(2,1)} %bitcast.63, bf16[2048,2048]{1,0:T(8,128)(2,1)} %all-gather.2.cloned.1.call-done), kind=kOutput, calls=%fused_computation.20 | convolution fusion | flops 8592031744 | bytes 16777216 | tf_op jit(solution)/shard_map/dot_general | solution.py:14
  643.5 10.4 %collective-permute-done.20 = bf16[1,512,1024]{1,2,0:T(8,128)(2,1)} collective-permute-done((bf16[1,512,1024]{1,2,0:T(8,128)(2,1)S(1)}, bf16[1,512,1024]{1,2,0:T(8,128)(2,1)}, u32[]{:S(2)}, u32[]{:S(2)}) %collective-permute-start.20) | collective-permute-done | bytes 1048608 | tf_op jit(solution)/shard_map/ppermute | solution.py:33
  655.7 14.0 %fusion.9 = f32[2048,2048]{1,0:T(8,128)} fusion(bf16[2048,1024]{1,0:T(8,128)(2,1)S(1)} %bitcast.64, bf16[2048,8192]{1,0:T(8,128)(2,1)} %param.5, s32[]{:T(128)S(6)} %select_n.183), kind=kOutput, calls=%fused_computation.33 | convolution fusion | flops 8589934592 | bytes 25165828 | tf_op jit(solution)/shard_map/dot_general | solution.py:14
  670.2 4.3 dynamic-slice_bitcast_fusion.4
  684.7 2.3 broadcast_select_fusion.13
  693.6 7.1 collective-permute-done.25
  700.8 21.7 %collective-permute-done.26 = bf16[512,1024]{0,1:T(8,128)(2,1)} collective-permute-done((bf16[512,1024]{0,1:T(8,128)(2,1)}, bf16[512,1024]{0,1:T(8,128)(2,1)}, u32[]{:S(2)}, u32[]{:S(2)}) %collective-permute-start.26) | collective-permute-done | bytes 1048608 | tf_op jit(solution)/shard_map/ppermute | solution.py:20
  722.5 12.3 %fusion.3 = f32[2048,2048]{1,0:T(8,128)S(1)} fusion(bf16[2048,1024]{1,0:T(8,128)(2,1)} %bitcast.65, bf16[8192,2048]{1,0:T(8,128)(2,1)} %param.6, s32[]{:T(128)S(6)} %select_n.184), kind=kOutput, calls=%fused_computation.27 | convolution fusion | flops 8589934592 | bytes 25165828 | tf_op jit(solution)/shard_map/dot_general | solution.py:14
  734.7 9.7 add_convert_fusion.1
  745.7 2.8 fusion.36
  748.5 5.6 collective-permute-start.27
  755.4 21.4 %collective-permute-done.27 = bf16[1,512,1024]{1,2,0:T(8,128)(2,1)S(1)} collective-permute-done((bf16[1,512,1024]{1,2,0:T(8,128)(2,1)S(1)}, bf16[1,512,1024]{1,2,0:T(8,128)(2,1)S(1)}, u32[]{:S(2)}, u32[]{:S(2)}) %collective-permute-start.27) | collective-permute-done | bytes 1048608 | tf_op jit(solution)/shard_map/ppermute | solution.py:32
  778.4 2.5 collective-permute-done.28
  783.9 23.4 %collective-permute-done.29 = bf16[1,512,1024]{1,2,0:T(8,128)(2,1)} collective-permute-done((bf16[1,512,1024]{1,2,0:T(8,128)(2,1)S(1)}, bf16[1,512,1024]{1,2,0:T(8,128)(2,1)}, u32[]{:S(2)}, u32[]{:S(2)}) %collective-permute-start.29) | collective-permute-done | bytes 1048608 | tf_op jit(solution)/shard_map/ppermute | solution.py:33
  808.6 14.1 %convolution_convert_fusion.1 = bf16[1024,2048]{1,0:T(8,128)(2,1)} fusion(bf16[2048,1024]{1,0:T(8,128)(2,1)} %bitcast.66, bf16[2048,2048]{1,0:T(8,128)(2,1)} %bitcast.57), kind=kOutput, calls=%fused_computation.19 | convolution fusion | flops 8592031744 | bytes 16777216 | tf_op jit(solution)/shard_map/dot_general | solution.py:14
  823.2 4.3 constant_dynamic-slice_fusion
  837.9 2.3 broadcast_select_fusion.12
  846.8 7.0 collective-permute-done.34
  853.8 21.7 %collective-permute-done.35 = bf16[1024,512]{1,0:T(8,128)(2,1)} collective-permute-done((bf16[1024,512]{1,0:T(8,128)(2,1)}, bf16[1024,512]{1,0:T(8,128)(2,1)}, u32[]{:S(2)}, u32[]{:S(2)}) %collective-permute-start.35) | collective-permute-done | bytes 1048608 | tf_op jit(solution)/shard_map/ppermute | solution.py:20
  875.5 15.3 %fusion.6 = f32[2048,2048]{1,0:T(8,128)} fusion(bf16[2048,1024]{1,0:T(8,128)(2,1)} %bitcast.59, bf16[2048,8192]{1,0:T(8,128)(2,1)} %param.5, s32[]{:T(128)S(6)} %select_n.184), kind=kOutput, calls=%fused_computation.30 | convolution fusion | flops 8589934592 | bytes 25165828 | tf_op jit(solution)/shard_map/dot_general | solution.py:14
  890.9 9.9 add_convert_fusion
  902.3 3.9 broadcast_in_dim.23
  907.3 2.4 constant_dynamic-update-slice_fusion.6
  911.9 2.5 constant_dynamic-update-slice_fusion.4
  915.7 2.4 copy.37
  918.1 2.4 copy.38
  922.8 4.4 broadcast_in_dim.22
  928.3 12.1 %convolution_convert_fusion = bf16[1024,2048]{1,0:T(8,128)(2,1)S(1)} fusion(bf16[2048,1024]{1,0:T(8,128)(2,1)S(1)} %bitcast.60, bf16[2048,2048]{1,0:T(8,128)(2,1)} %all-gather.2.cloned.1.call-done), kind=kOutput, calls=%fused_computation.18 | convolution fusion | flops 8592031744 | bytes 16777216 | tf_op jit(solution)/shard_map/dot_general | solution.py:14
  961.5 17.5 %collective-permute-done.37 = bf16[512,1024]{0,1:T(8,128)(2,1)} collective-permute-done((bf16[512,1024]{0,1:T(8,128)(2,1)}, bf16[512,1024]{0,1:T(8,128)(2,1)}, u32[]{:S(2)}, u32[]{:S(2)}) %collective-permute-start.37) | collective-permute-done | bytes 1048608 | tf_op jit(solution)/shard_map/ppermute | solution.py:20
  981.3 28.0 %collective-permute-done.38 = bf16[512,1024]{0,1:T(8,128)(2,1)} collective-permute-done((bf16[512,1024]{0,1:T(8,128)(2,1)}, bf16[512,1024]{0,1:T(8,128)(2,1)}, u32[]{:S(2)}, u32[]{:S(2)}) %collective-permute-start.38) | collective-permute-done | bytes 1048608 | tf_op jit(solution)/shard_map/ppermute | solution.py:20
  1012.6 2.4 constant_dynamic-update-slice_fusion.9
  1017.3 2.6 add_convert_fusion.2
  (205 shorter events, 150.2 us)
Async XLA Ops:
  7.2 93.3 %all-gather.2.cloned.1.call-start = ((), (), s32[]{:S(2)}) async-start(), calls=%async_computation.6 | async-start | bytes 9437184 | tf_op jit(solution)/shard_map/all_gather | solution.py:80
  7.9 183.3 %reduce-scatter.7.cloned.1.call-start = ((), (), s32[]{:S(2)}) async-start(), calls=%async_computation.7 | async-start | bytes 5242880 | tf_op jit(solution)/shard_map/reduce_scatter | solution.py:24
  7.9 37.6 %collective-permute-start = (bf16[1,1,1,256,2048]{4,3,2,1,0:T(8,128)(2,1)}, bf16[1,1,1,256,2048]{4,3,2,1,0:T(8,128)(2,1)S(1)}, u32[]{:S(2)}, u32[]{:S(2)}) collective-permute-start(bf16[1,1,1,256,2048]{4,3,2,1,0:T(8,128)(2,1)} %bitcast.58), channel_id=1, source_target_pairs={{0,16},{8,24},{16,0},{24,8},{1,17},{9,25},{17,1},{25,9},{2,18},{10... | collective-permute-start | bytes 3145736 | tf_op jit(solution)/shard_map/ppermute | solution.py:20
  48.1 68.6 %collective-permute-start.1 = (bf16[2,1,1,256,2048]{4,3,2,1,0:T(8,128)(2,1)S(1)}, bf16[2,1,1,256,2048]{4,3,2,1,0:T(8,128)(2,1)}, u32[]{:S(2)}, u32[]{:S(2)}) collective-permute-start(bf16[2,1,1,256,2048]{4,3,2,1,0:T(8,128)(2,1)S(1)} %pad_maximum_fusion.2), channel_id=1, source_target_pairs={{0,1},{1,0},{2,3},{3,2},{4,5},{5,4},{6,7},{7,6},{8,9},{9,8},{10,11... | collective-permute-start | bytes 6291464 | tf_op jit(solution)/shard_map/ppermute | solution.py:20
  114.4 290.5 %reduce-scatter.11.cloned.1.call-start = ((), (), s32[]{:S(2)}) async-start(), calls=%async_computation.9 | async-start | bytes 5242880 | tf_op jit(solution)/shard_map/reduce_scatter | solution.py:24
  121.7 7.5 collective-permute-start.2
  156.3 406.2 %reduce-scatter.9.cloned.1.call-start = ((), (), s32[]{:S(2)}) async-start(), calls=%async_computation.8 | async-start | bytes 5242880 | tf_op jit(solution)/shard_map/reduce_scatter | solution.py:24
  191.2 502.4 %reduce-scatter.13.cloned.1.call-start = ((), (), s32[]{:S(2)}) async-start(), calls=%async_computation.10 | async-start | bytes 5242880 | tf_op jit(solution)/shard_map/reduce_scatter | solution.py:24
  193.1 45.9 %collective-permute-start.3 = (bf16[1,512,1024]{1,2,0:T(8,128)(2,1)S(1)}, bf16[1,512,1024]{1,2,0:T(8,128)(2,1)S(1)}, u32[]{:S(2)}, u32[]{:S(2)}) collective-permute-start(bf16[1,512,1024]{1,2,0:T(8,128)(2,1)S(1)} %fusion.35), channel_id=1, source_target_pairs={{0,2},{2,4},{4,6},{1,3},{3,5},{5,7},{8,10},{10,12},{12,14},{9,11},... | collective-permute-start | bytes 3145736 | tf_op jit(solution)/shard_map/ppermute | solution.py:32
  196.6 71.9 %collective-permute-start.4 = (bf16[1,512,1024]{1,2,0:T(8,128)(2,1)S(1)}, bf16[1,512,1024]{1,2,0:T(8,128)(2,1)S(1)}, u32[]{:S(2)}, u32[]{:S(2)}) collective-permute-start(bf16[1,512,1024]{1,2,0:T(8,128)(2,1)S(1)} %fusion.35), channel_id=1, source_target_pairs={{6,4},{4,2},{2,0},{7,5},{5,3},{3,1},{14,12},{12,10},{10,8},{15,13}... | collective-permute-start | bytes 3145736 | tf_op jit(solution)/shard_map/ppermute | solution.py:33
  239.0 81.0 %copy-start.20 = (bf16[1,512,1024]{1,2,0:T(8,128)(2,1)}, bf16[1,512,1024]{1,2,0:T(8,128)(2,1)S(1)}, u32[]{:S(2)}) copy-start(bf16[1,512,1024]{1,2,0:T(8,128)(2,1)S(1)} %collective-permute-done.3) | copy-start | bytes 3145732
  239.0 30.8 %collective-permute-start.7 = (bf16[1,512,1024]{1,2,0:T(8,128)(2,1)S(1)}, bf16[1,512,1024]{1,2,0:T(8,128)(2,1)}, u32[]{:S(2)}, u32[]{:S(2)}) collective-permute-start(bf16[1,512,1024]{1,2,0:T(8,128)(2,1)S(1)} %collective-permute-done.3), channel_id=1, source_target_pairs={{2,4},{4,6},{3,5},{5,7},{10,12},{12,14},{11,13},{13,15},{18,20},{2... | collective-permute-start | bytes 3145736 | tf_op jit(solution)/shard_map/ppermute | solution.py:32
  268.5 50.0 %collective-permute-start.5 = (bf16[1,512,1024]{1,2,0:T(8,128)(2,1)S(1)}, bf16[1,512,1024]{1,2,0:T(8,128)(2,1)}, u32[]{:S(2)}, u32[]{:S(2)}) collective-permute-start(bf16[1,512,1024]{1,2,0:T(8,128)(2,1)S(1)} %collective-permute-done.4), channel_id=1, source_target_pairs={{4,2},{2,0},{5,3},{3,1},{12,10},{10,8},{13,11},{11,9},{20,18},{18,... | collective-permute-start | bytes 3145736 | tf_op jit(solution)/shard_map/ppermute | solution.py:33
  269.8 55.3 %collective-permute-start.8 = (bf16[1,512,1024]{1,2,0:T(8,128)(2,1)}, bf16[1,512,1024]{1,2,0:T(8,128)(2,1)}, u32[]{:S(2)}, u32[]{:S(2)}) collective-permute-start(bf16[1,512,1024]{1,2,0:T(8,128)(2,1)} %collective-permute-done.7), channel_id=1, source_target_pairs={{4,6},{5,7},{12,14},{13,15},{20,22},{21,23},{28,30},{29,31}} | collective-permute-start | bytes 3145736 | tf_op jit(solution)/shard_map/ppermute | solution.py:32
  318.5 77.4 %collective-permute-start.6 = (bf16[1,512,1024]{1,2,0:T(8,128)(2,1)}, bf16[1,512,1024]{1,2,0:T(8,128)(2,1)}, u32[]{:S(2)}, u32[]{:S(2)}) collective-permute-start(bf16[1,512,1024]{1,2,0:T(8,128)(2,1)} %collective-permute-done.5), channel_id=1, source_target_pairs={{2,0},{3,1},{10,8},{11,9},{18,16},{19,17},{26,24},{27,25}} | collective-permute-start | bytes 3145736 | tf_op jit(solution)/shard_map/ppermute | solution.py:33
  407.6 34.7 %collective-permute-start.9 = (bf16[1,512,1024]{1,2,0:T(8,128)(2,1)S(1)}, bf16[1,512,1024]{1,2,0:T(8,128)(2,1)S(1)}, u32[]{:S(2)}, u32[]{:S(2)}) collective-permute-start(bf16[1,512,1024]{1,2,0:T(8,128)(2,1)S(1)} %fusion.37), channel_id=1, source_target_pairs={{0,2},{2,4},{4,6},{1,3},{3,5},{5,7},{8,10},{10,12},{12,14},{9,11},... | collective-permute-start | bytes 3145736 | tf_op jit(solution)/shard_map/ppermute | solution.py:32
  409.2 58.5 %collective-permute-start.10 = (bf16[1,512,1024]{1,2,0:T(8,128)(2,1)S(1)}, bf16[1,512,1024]{1,2,0:T(8,128)(2,1)S(1)}, u32[]{:S(2)}, u32[]{:S(2)}) collective-permute-start(bf16[1,512,1024]{1,2,0:T(8,128)(2,1)S(1)} %fusion.37), channel_id=1, source_target_pairs={{6,4},{4,2},{2,0},{7,5},{5,3},{3,1},{14,12},{12,10},{10,8},{15,13}... | collective-permute-start | bytes 3145736 | tf_op jit(solution)/shard_map/ppermute | solution.py:33
  410.5 490.3 %reduce-scatter.15.cloned.1.call-start = ((), (), s32[]{:S(2)}) async-start(), calls=%async_computation.11 | async-start | bytes 9437184 | tf_op jit(solution)/shard_map/reduce_scatter | solution.py:69
  410.6 114.3 %copy-start.15 = (bf16[4,512,1024]{2,1,0:T(8,128)(2,1)S(1)}, bf16[4,512,1024]{2,1,0:T(8,128)(2,1)}, u32[]{:S(2)}) copy-start(bf16[4,512,1024]{2,1,0:T(8,128)(2,1)} %constant_dynamic-update-slice_fusion.28) | copy-start | bytes 12582916
  442.4 40.7 %copy-start.21 = (bf16[1,512,1024]{1,2,0:T(8,128)(2,1)}, bf16[1,512,1024]{1,2,0:T(8,128)(2,1)S(1)}, u32[]{:S(2)}) copy-start(bf16[1,512,1024]{1,2,0:T(8,128)(2,1)S(1)} %collective-permute-done.9) | copy-start | bytes 3145732
  442.4 40.7 %collective-permute-start.13 = (bf16[1,512,1024]{1,2,0:T(8,128)(2,1)S(1)}, bf16[1,512,1024]{1,2,0:T(8,128)(2,1)}, u32[]{:S(2)}, u32[]{:S(2)}) collective-permute-start(bf16[1,512,1024]{1,2,0:T(8,128)(2,1)S(1)} %collective-permute-done.9), channel_id=1, source_target_pairs={{2,4},{4,6},{3,5},{5,7},{10,12},{12,14},{11,13},{13,15},{18,20},{2... | collective-permute-start | bytes 3145736 | tf_op jit(solution)/shard_map/ppermute | solution.py:32
  467.7 15.4 %copy-start.23 = (bf16[1,512,1024]{1,2,0:T(8,128)(2,1)}, bf16[1,512,1024]{1,2,0:T(8,128)(2,1)S(1)}, u32[]{:S(2)}) copy-start(bf16[1,512,1024]{1,2,0:T(8,128)(2,1)S(1)} %collective-permute-done.10) | copy-start | bytes 3145732
  467.7 55.7 %collective-permute-start.11 = (bf16[1,512,1024]{1,2,0:T(8,128)(2,1)S(1)}, bf16[1,512,1024]{1,2,0:T(8,128)(2,1)}, u32[]{:S(2)}, u32[]{:S(2)}) collective-permute-start(bf16[1,512,1024]{1,2,0:T(8,128)(2,1)S(1)} %collective-permute-done.10), channel_id=1, source_target_pairs={{4,2},{2,0},{5,3},{3,1},{12,10},{10,8},{13,11},{11,9},{20,18},{18,... | collective-permute-start | bytes 3145736 | tf_op jit(solution)/shard_map/ppermute | solution.py:33
  483.0 66.7 %collective-permute-start.14 = (bf16[1,512,1024]{1,2,0:T(8,128)(2,1)}, bf16[1,512,1024]{1,2,0:T(8,128)(2,1)}, u32[]{:S(2)}, u32[]{:S(2)}) collective-permute-start(bf16[1,512,1024]{1,2,0:T(8,128)(2,1)} %collective-permute-done.13), channel_id=1, source_target_pairs={{4,6},{5,7},{12,14},{13,15},{20,22},{21,23},{28,30},{29,31}} | collective-permute-start | bytes 3145736 | tf_op jit(solution)/shard_map/ppermute | solution.py:32
  523.4 30.2 %collective-permute-start.12 = (bf16[1,512,1024]{1,2,0:T(8,128)(2,1)}, bf16[1,512,1024]{1,2,0:T(8,128)(2,1)}, u32[]{:S(2)}, u32[]{:S(2)}) collective-permute-start(bf16[1,512,1024]{1,2,0:T(8,128)(2,1)} %collective-permute-done.11), channel_id=1, source_target_pairs={{2,0},{3,1},{10,8},{11,9},{18,16},{19,17},{26,24},{27,25}} | collective-permute-start | bytes 3145736 | tf_op jit(solution)/shard_map/ppermute | solution.py:33
  543.4 19.2 %collective-permute-start.15 = (bf16[1024,512]{1,0:T(8,128)(2,1)}, bf16[1024,512]{1,0:T(8,128)(2,1)}, u32[]{:S(2)}, u32[]{:S(2)}) collective-permute-start(bf16[1024,512]{1,0:T(8,128)(2,1)} %get-tuple-element.80), channel_id=1, source_target_pairs={{0,8},{8,0},{16,24},{24,16},{1,9},{9,1},{17,25},{25,17},{2,10},{10... | collective-permute-start | bytes 3145736 | tf_op jit(solution)/shard_map/ppermute | solution.py:20
  543.4 26.3 %collective-permute-start.16 = (bf16[1024,512]{1,0:T(8,128)(2,1)}, bf16[1024,512]{1,0:T(8,128)(2,1)}, u32[]{:S(2)}, u32[]{:S(2)}) collective-permute-start(bf16[1024,512]{1,0:T(8,128)(2,1)} %get-tuple-element.79), channel_id=1, source_target_pairs={{0,16},{8,24},{16,0},{24,8},{1,17},{9,25},{17,1},{25,9},{2,18},{10... | collective-permute-start | bytes 3145736 | tf_op jit(solution)/shard_map/ppermute | solution.py:20
  544.9 46.5 %collective-permute-start.17 = (bf16[1024,512]{1,0:T(8,128)(2,1)}, bf16[1024,512]{1,0:T(8,128)(2,1)}, u32[]{:S(2)}, u32[]{:S(2)}) collective-permute-start(bf16[1024,512]{1,0:T(8,128)(2,1)} %get-tuple-element.78), channel_id=1, source_target_pairs={{0,24},{8,16},{16,8},{24,0},{1,25},{9,17},{17,9},{25,1},{2,26},{10... | collective-permute-start | bytes 3145736 | tf_op jit(solution)/shard_map/ppermute | solution.py:20
  593.3 62.4 %copy-start.17 = (bf16[4,512,1024]{2,1,0:T(8,128)(2,1)S(1)}, bf16[4,512,1024]{2,1,0:T(8,128)(2,1)}, u32[]{:S(2)}) copy-start(bf16[4,512,1024]{2,1,0:T(8,128)(2,1)} %constant_dynamic-update-slice_fusion.24) | copy-start | bytes 12582916
  593.3 28.6 %collective-permute-start.18 = (bf16[1,512,1024]{1,2,0:T(8,128)(2,1)S(1)}, bf16[1,512,1024]{1,2,0:T(8,128)(2,1)S(1)}, u32[]{:S(2)}, u32[]{:S(2)}) collective-permute-start(bf16[1,512,1024]{1,2,0:T(8,128)(2,1)S(1)} %fusion.34), channel_id=1, source_target_pairs={{0,2},{2,4},{4,6},{1,3},{3,5},{5,7},{8,10},{10,12},{12,14},{9,11},... | collective-permute-start | bytes 3145736 | tf_op jit(solution)/shard_map/ppermute | solution.py:32
  599.2 27.3 %collective-permute-start.19 = (bf16[1,512,1024]{1,2,0:T(8,128)(2,1)S(1)}, bf16[1,512,1024]{1,2,0:T(8,128)(2,1)S(1)}, u32[]{:S(2)}, u32[]{:S(2)}) collective-permute-start(bf16[1,512,1024]{1,2,0:T(8,128)(2,1)S(1)} %fusion.34), channel_id=1, source_target_pairs={{6,4},{4,2},{2,0},{7,5},{5,3},{3,1},{14,12},{12,10},{10,8},{15,13}... | collective-permute-start | bytes 3145736 | tf_op jit(solution)/shard_map/ppermute | solution.py:33
  621.9 20.0 %copy-start.25 = (bf16[1,512,1024]{1,2,0:T(8,128)(2,1)}, bf16[1,512,1024]{1,2,0:T(8,128)(2,1)S(1)}, u32[]{:S(2)}) copy-start(bf16[1,512,1024]{1,2,0:T(8,128)(2,1)S(1)} %collective-permute-done.18) | copy-start | bytes 3145732
  621.9 20.0 %collective-permute-start.22 = (bf16[1,512,1024]{1,2,0:T(8,128)(2,1)S(1)}, bf16[1,512,1024]{1,2,0:T(8,128)(2,1)}, u32[]{:S(2)}, u32[]{:S(2)}) collective-permute-start(bf16[1,512,1024]{1,2,0:T(8,128)(2,1)S(1)} %collective-permute-done.18), channel_id=1, source_target_pairs={{2,4},{4,6},{3,5},{5,7},{10,12},{12,14},{11,13},{13,15},{18,20},{2... | collective-permute-start | bytes 3145736 | tf_op jit(solution)/shard_map/ppermute | solution.py:32
  626.5 15.3 %copy-start.27 = (bf16[1,512,1024]{1,2,0:T(8,128)(2,1)}, bf16[1,512,1024]{1,2,0:T(8,128)(2,1)S(1)}, u32[]{:S(2)}) copy-start(bf16[1,512,1024]{1,2,0:T(8,128)(2,1)S(1)} %collective-permute-done.19) | copy-start | bytes 3145732
  626.5 27.4 %collective-permute-start.20 = (bf16[1,512,1024]{1,2,0:T(8,128)(2,1)S(1)}, bf16[1,512,1024]{1,2,0:T(8,128)(2,1)}, u32[]{:S(2)}, u32[]{:S(2)}) collective-permute-start(bf16[1,512,1024]{1,2,0:T(8,128)(2,1)S(1)} %collective-permute-done.19), channel_id=1, source_target_pairs={{4,2},{2,0},{5,3},{3,1},{12,10},{10,8},{13,11},{11,9},{20,18},{18,... | collective-permute-start | bytes 3145736 | tf_op jit(solution)/shard_map/ppermute | solution.py:33
  641.8 39.0 %collective-permute-start.23 = (bf16[1,512,1024]{1,2,0:T(8,128)(2,1)}, bf16[1,512,1024]{1,2,0:T(8,128)(2,1)}, u32[]{:S(2)}, u32[]{:S(2)}) collective-permute-start(bf16[1,512,1024]{1,2,0:T(8,128)(2,1)} %collective-permute-done.22), channel_id=1, source_target_pairs={{4,6},{5,7},{12,14},{13,15},{20,22},{21,23},{28,30},{29,31}} | collective-permute-start | bytes 3145736 | tf_op jit(solution)/shard_map/ppermute | solution.py:32
  653.9 30.8 %collective-permute-start.21 = (bf16[1,512,1024]{1,2,0:T(8,128)(2,1)}, bf16[1,512,1024]{1,2,0:T(8,128)(2,1)}, u32[]{:S(2)}, u32[]{:S(2)}) collective-permute-start(bf16[1,512,1024]{1,2,0:T(8,128)(2,1)} %collective-permute-done.20), channel_id=1, source_target_pairs={{2,0},{3,1},{10,8},{11,9},{18,16},{19,17},{26,24},{27,25}} | collective-permute-start | bytes 3145736 | tf_op jit(solution)/shard_map/ppermute | solution.py:33
  674.5 19.1 %collective-permute-start.24 = (bf16[512,1024]{0,1:T(8,128)(2,1)}, bf16[512,1024]{0,1:T(8,128)(2,1)}, u32[]{:S(2)}, u32[]{:S(2)}) collective-permute-start(bf16[512,1024]{0,1:T(8,128)(2,1)} %get-tuple-element.76), channel_id=1, source_target_pairs={{0,8},{8,0},{16,24},{24,16},{1,9},{9,1},{17,25},{25,17},{2,10},{10... | collective-permute-start | bytes 3145736 | tf_op jit(solution)/shard_map/ppermute | solution.py:20
  674.5 26.3 %collective-permute-start.25 = (bf16[512,1024]{0,1:T(8,128)(2,1)}, bf16[512,1024]{0,1:T(8,128)(2,1)}, u32[]{:S(2)}, u32[]{:S(2)}) collective-permute-start(bf16[512,1024]{0,1:T(8,128)(2,1)} %get-tuple-element.75), channel_id=1, source_target_pairs={{0,16},{8,24},{16,0},{24,8},{1,17},{9,25},{17,1},{25,9},{2,18},{10... | collective-permute-start | bytes 3145736 | tf_op jit(solution)/shard_map/ppermute | solution.py:20
  676.0 46.5 %collective-permute-start.26 = (bf16[512,1024]{0,1:T(8,128)(2,1)}, bf16[512,1024]{0,1:T(8,128)(2,1)}, u32[]{:S(2)}, u32[]{:S(2)}) collective-permute-start(bf16[512,1024]{0,1:T(8,128)(2,1)} %get-tuple-element.74), channel_id=1, source_target_pairs={{0,24},{8,16},{16,8},{24,0},{1,25},{9,17},{17,9},{25,1},{2,26},{10... | collective-permute-start | bytes 3145736 | tf_op jit(solution)/shard_map/ppermute | solution.py:20
  744.5 272.8 %reduce-scatter.17.cloned.1.call-start = ((), (), s32[]{:S(2)}) async-start(), calls=%async_computation.12 | async-start | bytes 9437184 | tf_op jit(solution)/shard_map/reduce_scatter | solution.py:69
  748.5 28.3 %collective-permute-start.27 = (bf16[1,512,1024]{1,2,0:T(8,128)(2,1)S(1)}, bf16[1,512,1024]{1,2,0:T(8,128)(2,1)S(1)}, u32[]{:S(2)}, u32[]{:S(2)}) collective-permute-start(bf16[1,512,1024]{1,2,0:T(8,128)(2,1)S(1)} %fusion.36), channel_id=1, source_target_pairs={{0,2},{2,4},{4,6},{1,3},{3,5},{5,7},{8,10},{10,12},{12,14},{9,11},... | collective-permute-start | bytes 3145736 | tf_op jit(solution)/shard_map/ppermute | solution.py:32
  754.1 26.9 %collective-permute-start.28 = (bf16[1,512,1024]{1,2,0:T(8,128)(2,1)S(1)}, bf16[1,512,1024]{1,2,0:T(8,128)(2,1)S(1)}, u32[]{:S(2)}, u32[]{:S(2)}) collective-permute-start(bf16[1,512,1024]{1,2,0:T(8,128)(2,1)S(1)} %fusion.36), channel_id=1, source_target_pairs={{6,4},{4,2},{2,0},{7,5},{5,3},{3,1},{14,12},{12,10},{10,8},{15,13}... | collective-permute-start | bytes 3145736 | tf_op jit(solution)/shard_map/ppermute | solution.py:33
  776.8 5.5 collective-permute-start.31
  781.0 26.3 %collective-permute-start.29 = (bf16[1,512,1024]{1,2,0:T(8,128)(2,1)S(1)}, bf16[1,512,1024]{1,2,0:T(8,128)(2,1)}, u32[]{:S(2)}, u32[]{:S(2)}) collective-permute-start(bf16[1,512,1024]{1,2,0:T(8,128)(2,1)S(1)} %collective-permute-done.28), channel_id=1, source_target_pairs={{4,2},{2,0},{5,3},{3,1},{12,10},{10,8},{13,11},{11,9},{20,18},{18,... | collective-permute-start | bytes 3145736 | tf_op jit(solution)/shard_map/ppermute | solution.py:33
  782.3 51.8 %collective-permute-start.32 = (bf16[1,512,1024]{1,2,0:T(8,128)(2,1)}, bf16[1,512,1024]{1,2,0:T(8,128)(2,1)}, u32[]{:S(2)}, u32[]{:S(2)}) collective-permute-start(bf16[1,512,1024]{1,2,0:T(8,128)(2,1)} %collective-permute-done.31), channel_id=1, source_target_pairs={{4,6},{5,7},{12,14},{13,15},{20,22},{21,23},{28,30},{29,31}} | collective-permute-start | bytes 3145736 | tf_op jit(solution)/shard_map/ppermute | solution.py:32
  807.3 30.6 %collective-permute-start.30 = (bf16[1,512,1024]{1,2,0:T(8,128)(2,1)}, bf16[1,512,1024]{1,2,0:T(8,128)(2,1)}, u32[]{:S(2)}, u32[]{:S(2)}) collective-permute-start(bf16[1,512,1024]{1,2,0:T(8,128)(2,1)} %collective-permute-done.29), channel_id=1, source_target_pairs={{2,0},{3,1},{10,8},{11,9},{18,16},{19,17},{26,24},{27,25}} | collective-permute-start | bytes 3145736 | tf_op jit(solution)/shard_map/ppermute | solution.py:33
  827.6 19.2 %collective-permute-start.33 = (bf16[1024,512]{1,0:T(8,128)(2,1)}, bf16[1024,512]{1,0:T(8,128)(2,1)}, u32[]{:S(2)}, u32[]{:S(2)}) collective-permute-start(bf16[1024,512]{1,0:T(8,128)(2,1)} %get-tuple-element.72), channel_id=1, source_target_pairs={{0,8},{8,0},{16,24},{24,16},{1,9},{9,1},{17,25},{25,17},{2,10},{10... | collective-permute-start | bytes 3145736 | tf_op jit(solution)/shard_map/ppermute | solution.py:20
  827.6 26.3 %collective-permute-start.34 = (bf16[1024,512]{1,0:T(8,128)(2,1)}, bf16[1024,512]{1,0:T(8,128)(2,1)}, u32[]{:S(2)}, u32[]{:S(2)}) collective-permute-start(bf16[1024,512]{1,0:T(8,128)(2,1)} %get-tuple-element.71), channel_id=1, source_target_pairs={{0,16},{8,24},{16,0},{24,8},{1,17},{9,25},{17,1},{25,9},{2,18},{10... | collective-permute-start | bytes 3145736 | tf_op jit(solution)/shard_map/ppermute | solution.py:20
  829.1 46.5 %collective-permute-start.35 = (bf16[1024,512]{1,0:T(8,128)(2,1)}, bf16[1024,512]{1,0:T(8,128)(2,1)}, u32[]{:S(2)}, u32[]{:S(2)}) collective-permute-start(bf16[1024,512]{1,0:T(8,128)(2,1)} %get-tuple-element.70), channel_id=1, source_target_pairs={{0,24},{8,16},{16,8},{24,0},{1,25},{9,17},{17,9},{25,1},{2,26},{10... | collective-permute-start | bytes 3145736 | tf_op jit(solution)/shard_map/ppermute | solution.py:20
  844.7 46.1 %slice-start = ((s8[16777216]{0:T(1024)(128)(4,1)}), s8[4194304]{0:T(1024)(128)(4,1)S(1)}, s32[]{:S(2)}) async-start(s8[16777216]{0:T(1024)(128)(4,1)} %bitcast.52), calls=%async_computation.13 | async-start | bytes 8388608
  875.5 15.3 %slice-start.1 = ((s8[16777216]{0:T(1024)(128)(4,1)}), s8[4194304]{0:T(1024)(128)(4,1)S(1)}, s32[]{:S(2)}) async-start(s8[16777216]{0:T(1024)(128)(4,1)} %bitcast.52), calls=%async_computation.14 | async-start | bytes 8388608
  875.5 15.3 %slice-start.2 = ((s8[16777216]{0:T(1024)(128)(4,1)}), s8[4194304]{0:T(1024)(128)(4,1)S(1)}, s32[]{:S(2)}) async-start(s8[16777216]{0:T(1024)(128)(4,1)} %bitcast.52), calls=%async_computation.15 | async-start | bytes 8388608
  875.5 15.3 %slice-start.3 = ((s8[16777216]{0:T(1024)(128)(4,1)}), s8[4194304]{0:T(1024)(128)(4,1)S(1)}, s32[]{:S(2)}) async-start(s8[16777216]{0:T(1024)(128)(4,1)} %bitcast.52), calls=%async_computation.16 | async-start | bytes 8388608
  907.3 7.1 copy-start.5
  922.8 4.4 copy-start.10
  922.8 5.5 copy-start.13
  940.4 5.2 copy-start.8
  942.6 17.4 %collective-permute-start.36 = (bf16[512,1024]{0,1:T(8,128)(2,1)}, bf16[512,1024]{0,1:T(8,128)(2,1)}, u32[]{:S(2)}, u32[]{:S(2)}) collective-permute-start(bf16[512,1024]{0,1:T(8,128)(2,1)} %get-tuple-element.68), channel_id=1, source_target_pairs={{0,8},{8,0},{16,24},{24,16},{1,9},{9,1},{17,25},{25,17},{2,10},{10... | collective-permute-start | bytes 3145736 | tf_op jit(solution)/shard_map/ppermute | solution.py:20
  942.9 36.1 %collective-permute-start.37 = (bf16[512,1024]{0,1:T(8,128)(2,1)}, bf16[512,1024]{0,1:T(8,128)(2,1)}, u32[]{:S(2)}, u32[]{:S(2)}) collective-permute-start(bf16[512,1024]{0,1:T(8,128)(2,1)} %get-tuple-element.67), channel_id=1, source_target_pairs={{0,16},{8,24},{16,0},{24,8},{1,17},{9,25},{17,1},{25,9},{2,18},{10... | collective-permute-start | bytes 3145736 | tf_op jit(solution)/shard_map/ppermute | solution.py:20
  944.6 5.4 copy-start.3
  944.6 64.8 %collective-permute-start.38 = (bf16[512,1024]{0,1:T(8,128)(2,1)}, bf16[512,1024]{0,1:T(8,128)(2,1)}, u32[]{:S(2)}, u32[]{:S(2)}) collective-permute-start(bf16[512,1024]{0,1:T(8,128)(2,1)} %get-tuple-element.66), channel_id=1, source_target_pairs={{0,24},{8,16},{16,8},{24,0},{1,25},{9,17},{17,9},{25,1},{2,26},{10... | collective-permute-start | bytes 3145736 | tf_op jit(solution)/shard_map/ppermute | solution.py:20
  1011.6 4.4 copy-start.19
  1012.6 4.7 copy-start.2
  (14 other events, 32.7 us)
Sparse Core Ops, SparseCore 0:
  9.9 90.5 all-gather.1
  114.5 76.6 reduce-scatter.6
  193.6 108.6 reduce-scatter.10
  304.4 100.0 reduce-scatter.8
  410.6 108.1 reduce-scatter.12
  744.6 72.5 reduce-scatter.14
  902.4 94.5 reduce-scatter.16

commit v3 on v1

--- a/solution.py
+++ b/solution.py
@@ -43,7 +43,7 @@
     )
 
 
-def gather_over_row(own, n):
+def gather_over_row(own, n, whole, column):
     me = lax.axis_index("row")
     right = left = own
     rights, lefts = [], []
@@ -52,11 +52,10 @@
         left = lax.ppermute(left, "row", [(k, k - 1) for k in range(n - 1 - t, 0, -1)])
         rights.append(right)
         lefts.append(left)
-    whole = jnp.zeros((n,) + own.shape[1:], own.dtype)
-    whole = lax.dynamic_update_slice_in_dim(whole, own, me, 0)
+    whole = lax.dynamic_update_slice(whole, own, (me, 0, column))
     for t in range(n - 1):
         block = jnp.where(me >= t + 1, rights[t], lefts[n - 2 - t])
-        whole = lax.dynamic_update_slice_in_dim(whole, block, lax.rem(me + n - 1 - t, n), 0)
+        whole = lax.dynamic_update_slice(whole, block, (lax.rem(me + n - 1 - t, n), 0, column))
     return whole
 
 
@@ -103,47 +102,79 @@
         width = share // PARTS
         piece = model // n_dp
 
-        all_in = gather_tokens(inputs, cols + far + core)
+        all_in = lax.all_gather(inputs, ("dp", "col"), axis=0, tiled=True)
         all_cot = gather_tokens(grad_outputs, far + cols + core)
         tokens = all_in.shape[0]
-        blocks = (n_row, tokens // n_row, width)
+
+        def blocks_of_peers(whole, dim):
+            return [
+                lax.dynamic_slice_in_dim(whole, (dp ^ mask) * piece, piece, dim)
+                for mask in range(n_dp)
+            ]
+
+        def exchange(blocks):
+            return [
+                swap(block, "dp", n_dp, mask) if mask else block
+                for mask, block in enumerate(blocks)
+            ]
+
+        firsts = [dp * share + h * width for h in range(PARTS)]
+        w_ins = [lax.dynamic_slice_in_dim(w_in, first, width, 1) for first in firsts]
+        w_outs = [lax.dynamic_slice_in_dim(w_out, first, width, 0) for first in firsts]
+
+        lines = (n_row, tokens // n_row)
+
+        def part_of(left, weights, dim):
+            part = contract(left, weights, 1, dim).astype(jnp.bfloat16)
+            return part.reshape(lines + (width,))
+
+        def gather(owns):
+            whole = jnp.zeros(lines + (share,), jnp.bfloat16)
+            for h, own in enumerate(owns):
+                whole = gather_over_row(own, n_row, whole, h * width)
+            return whole.reshape(tokens, share)
+
+        preacts = [sum_over_row(part_of(all_in, w_h, 0), n_row) for w_h in w_ins]
+        parts = [part_of(all_cot, w_h, 1) for w_h in w_outs]
+        for h in range(PARTS):
+            preacts[h], parts[h] = lax.optimization_barrier((preacts[h], parts[h]))
+        all_act = gather([gelu_fn(preact).astype(jnp.bfloat16) for preact in preacts])
+        grads = [sum_over_row(part, n_row) for part in parts]
+        grads, all_act = lax.optimization_barrier((grads, all_act))
+        owns = [
+            jax.vjp(gelu_fn, preact)[1](grad)[0].astype(jnp.bfloat16)
+            for preact, grad in zip(preacts, grads)
+        ]
+        whole_out = contract(all_act, all_cot, 0, 0).astype(jnp.bfloat16)
+        owns[-1], whole_out = lax.optimization_barrier((owns[-1], whole_out))
+        all_grad = gather(owns)
+        w_in_own = lax.dynamic_slice_in_dim(w_in, dp * share, share, 1)
+        w_out_own = lax.dynamic_slice_in_dim(w_out, dp * share, share, 0)
+        from_peers_out = exchange(blocks_of_peers(whole_out, 1))
+        out_part = contract(all_act, w_out_own, 1, 0).astype(jnp.bfloat16)
+        out_sum = scatter_tokens(out_part, core + far + cols)
+        all_grad, from_peers_out, out_sum = lax.optimization_barrier(
+            (all_grad, from_peers_out, out_sum)
+        )
+        whole_in = contract(all_in, all_grad, 0, 0).astype(jnp.bfloat16)
+        from_peers_in = exchange(blocks_of_peers(whole_in, 0))
+        input_part = contract(all_grad, w_in_own, 1, 1).astype(jnp.bfloat16)
+        input_sum = scatter_tokens(input_part, core + cols + far)
+
         grad_w_in = jnp.zeros((piece, hidden), jnp.bfloat16)
         grad_w_out = jnp.zeros((hidden, piece), jnp.bfloat16)
-        out_part = input_part = None
-        for h in range(PARTS):
-            first = dp * share + h * width
-            w_in_h = lax.dynamic_slice_in_dim(w_in, first, width, 1)
-            w_out_h = lax.dynamic_slice_in_dim(w_out, first, width, 0)
-            part = contract(all_in, w_in_h, 1, 0).astype(jnp.bfloat16)
-            preact = sum_over_row(part.reshape(blocks), n_row)
-            activated = gelu_fn(preact).astype(jnp.bfloat16)
-            part = contract(all_cot, w_out_h, 1, 1).astype(jnp.bfloat16)
-            grad_activated = sum_over_row(part.reshape(blocks), n_row)
-            grad_preact = jax.vjp(gelu_fn, preact)[1](grad_activated)[0].astype(jnp.bfloat16)
-            all_act = gather_over_row(activated, n_row).reshape(tokens, width)
-            all_grad = gather_over_row(grad_preact, n_row).reshape(tokens, width)
-
-            term = contract(all_act, w_out_h, 1, 0)
-            out_part = term if out_part is None else out_part + term
-            term = contract(all_grad, w_in_h, 1, 1)
-            input_part = term if input_part is None else input_part + term
-
-            whole_out = contract(all_act, all_cot, 0, 0).astype(jnp.bfloat16)
-            whole_in = contract(all_in, all_grad, 0, 0).astype(jnp.bfloat16)
-            for mask in range(n_dp):
-                peer = dp ^ mask
-                place = peer * share + h * width
-                block = lax.dynamic_slice_in_dim(whole_out, peer * piece, piece, 1)
-                block = swap(block, "dp", n_dp, mask) if mask else block
-                grad_w_out = lax.dynamic_update_slice_in_dim(grad_w_out, block, place, 0)
-                block = lax.dynamic_slice_in_dim(whole_in, peer * piece, piece, 0)
-                block = swap(block, "dp", n_dp, mask) if mask else block
-                grad_w_in = lax.dynamic_update_slice_in_dim(grad_w_in, block, place, 1)
-        out_sum = scatter_tokens(out_part.astype(jnp.bfloat16), core + far + cols)
-        outputs = (inputs.astype(jnp.float32) + out_sum).astype(jnp.bfloat16)
-        input_sum = scatter_tokens(input_part.astype(jnp.bfloat16), core + cols + far)
-        grad_inputs = (grad_outputs.astype(jnp.float32) + input_sum).astype(jnp.bfloat16)
-        return (outputs, grad_inputs, grad_w_in, grad_w_out)
+        for mask in range(n_dp):
+            place = (dp ^ mask) * share
+            grad_w_out = lax.dynamic_update_slice_in_dim(grad_w_out, from_peers_out[mask], place, 0)
+            grad_w_in = lax.dynamic_update_slice_in_dim(grad_w_in, from_peers_in[mask], place, 1)
+        outputs = inputs.astype(jnp.float32) + out_sum
+        grad_inputs = grad_outputs.astype(jnp.float32) + input_sum
+        return (
+            outputs.astype(jnp.bfloat16),
+            grad_inputs.astype(jnp.bfloat16),
+            grad_w_in,
+            grad_w_out,
+        )
 
     return jax.shard_map(
         shards,

time: 1080 us -> 1010 us (0.935)
  waiting for transfers between devices: 515 us -> 457 us
  starting transfers between devices: 226 us -> 188 us
  local copies, waits for them, and re-layouts: 62.2 us -> 97.2 us
  matrix products: 155 us -> 139 us
  between operations: 2.61 us -> 15.2 us
    ppermute x24 -> x15, waiting for transfers between devices: 293 us -> 229 us  [swap(): return lax.ppermute(array, axis, [(k, k ^ mask) for k in range(size)])]
    ppermute x12, starting transfers between devices: 90.9 us -> 61.4 us  [gather_over_row(): right = lax.ppermute(right, 'row', [(k, k + 1) for k in range(t, n - 1)])]
    ppermute x12, waiting for transfers between devices: 132 us -> 109 us  [gather_over_row(): lax.ppermute(left, 'row', [(k, k - 1) for k in range(n - 1 - t, 0, -1)])]
    ppermute x12, waiting for transfers between devices: 2.03 us -> 24.7 us  [sum_over_row(): lax.ppermute(block, 'row', [(k, k - 1) for k in range(n - 1, n - 2 - t, -...]
    dot_general x12 -> x8, matrix products: 155 us -> 139 us  [contract(): lax.dot_general(left, right, (((left_dim,), (right_dim,)), ((), ())), pre...]
    ppermute x12, waiting for transfers between devices: 0.03 us -> 13.3 us  [gather_over_row(): right = lax.ppermute(right, 'row', [(k, k + 1) for k in range(t, n - 1)])]
    reshape x0 -> x2, local copies, waits for them, and re-layouts: none -> 12.8 us  [part_of(): return part.reshape(lines + (width,))]
    ppermute x0 -> x3, local copies, waits for them, and re-layouts: none -> 11.9 us  [swap(): return lax.ppermute(array, axis, [(k, k ^ mask) for k in range(size)])]
  transfers between devices with their start and end apart: 72 -> 64, of which waited for: 27 -> 27; matrix products, arithmetic and copies ran while one was open for 28% -> 29% of each run, Pallas kernels for 0% -> 0%
where the time goes in v3:
time: 1010 us; the launch traced here: 1000 us
  waiting for transfers between devices  457 us (45%)
  starting transfers between devices  188 us (19%)
  matrix products  139 us (14%)
  other arithmetic  106 us (10%)
  local copies, waits for them, and re-layouts  97.2 us (10%)
  between operations  15.2 us (2%)
    ppermute x15, waiting for transfers between devices, swap(): return lax.ppermute(array, axis, [(k, k ^ mask) for k in range(size)])  229 us
    dot_general x8, matrix products, contract(): lax.dot_general(left, right, (((left_dim,), (right_dim,)), ((), ())), pre...  139 us
    ppermute x12, waiting for transfers between devices, gather_over_row(): lax.ppermute(left, 'row', [(k, k - 1) for k in range(n - 1 - t, 0, -1)])  109 us
    ppermute x12, waiting for transfers between devices, sum_over_row(): right = lax.ppermute(block, 'row', [(k, k + 1) for k in range(t + 1)])  80.6 us
    ppermute x12, starting transfers between devices, sum_over_row(): right = lax.ppermute(block, 'row', [(k, k + 1) for k in range(t + 1)])  79.7 us
    ppermute x12, starting transfers between devices, gather_over_row(): right = lax.ppermute(right, 'row', [(k, k + 1) for k in range(t, n - 1)])  61.4 us
    convert_element_type x16, other arithmetic, plus(): (left.astype(jnp.float32) + right.astype(jnp.float32)).astype(jnp.bfloat16)  39.6 us
    dynamic_update_slice x12, other arithmetic, gather_over_row(): lax.dynamic_update_slice(whole, block, (lax.rem(me + n - 1 - t, n), 0, co...  25.2 us
  transfers between devices with their start and end apart: 64, of which 27 were waited for; matrix products, arithmetic and copies ran while one was open for 29% of the time, Pallas kernels for 0%

profile of v3, /device:TPU:0, one launch (start us, length us, event | category | flops | bytes accessed | tf_op | source)
XLA Modules:
  0.0 1002.0 jit_solution(17745631601991309786)
XLA Ops:
  10.9 34.6 %collective-permute-done.6 = bf16[1,1,1,256,2048]{4,3,2,1,0:T(8,128)(2,1)S(1)} collective-permute-done((bf16[1,1,1,256,2048]{4,3,2,1,0:T(8,128)(2,1)}, bf16[1,1,1,256,2048]{4,3,2,1,0:T(8,128)(2,1)S(1)}, u32[]{:S(2)}, u32[]{:S(2)}) %collective-permute-start.6) | collective-permute-done | bytes 1048608 | tf_op jit(solution)/shard_map/ppermute | solution.py:28
  49.6 66.7 %collective-permute-done.7 = bf16[2,1,1,256,2048]{4,3,2,1,0:T(8,128)(2,1)} collective-permute-done((bf16[2,1,1,256,2048]{4,3,2,1,0:T(8,128)(2,1)S(1)}, bf16[2,1,1,256,2048]{4,3,2,1,0:T(8,128)(2,1)}, u32[]{:S(2)}, u32[]{:S(2)}) %collective-permute-start.7) | collective-permute-done | bytes 2097184 | tf_op jit(solution)/shard_map/ppermute | solution.py:28
  121.1 13.9 %convert_bitcast_fusion.1 = bf16[2048,1024]{0,1:T(8,128)(2,1)} fusion(bf16[2048,2048]{1,0:T(8,128)(2,1)} %all-gather.2.cloned.1.call-done, bf16[2048,8192]{1,0:T(8,128)(2,1)} %param.5, s32[]{:T(128)S(6)} %select_n.233), kind=kOutput, calls=%fused_computation.21 | convolution fusion | flops 8592031744 | bytes 16777220 | tf_op jit(solution)/shard_map/dot_general | solution.py:14
  135.0 6.4 copy.44
  144.4 4.5 collective-permute-start
  148.9 13.9 %convert_bitcast_fusion = bf16[2048,1024]{0,1:T(8,128)(2,1)} fusion(bf16[2048,2048]{1,0:T(8,128)(2,1)} %all-gather.2.cloned.1.call-done, bf16[2048,8192]{1,0:T(8,128)(2,1)} %param.5, s32[]{:T(128)S(6)} %select_n.245), kind=kOutput, calls=%fused_computation.16 | convolution fusion | flops 8592031744 | bytes 16777220 | tf_op jit(solution)/shard_map/dot_general | solution.py:14
  162.8 6.4 copy.45
  182.9 14.0 %collective-permute-done.15 = bf16[1,512,1024]{2,1,0:T(8,128)(2,1)} collective-permute-done((bf16[1,512,1024]{2,1,0:T(8,128)(2,1)}, bf16[1,512,1024]{2,1,0:T(8,128)(2,1)}, u32[]{:S(2)}, u32[]{:S(2)}) %collective-permute-start.15) | collective-permute-done | bytes 1048608 | tf_op jit(solution)/shard_map/ppermute | solution.py:37
  199.8 5.5 collective-permute-start.16
  205.4 14.0 %collective-permute-done.1 = bf16[1,512,1024]{2,1,0:T(8,128)(2,1)} collective-permute-done((bf16[1,512,1024]{2,1,0:T(8,128)(2,1)}, bf16[1,512,1024]{2,1,0:T(8,128)(2,1)}, u32[]{:S(2)}, u32[]{:S(2)}) %collective-permute-start.1) | collective-permute-done | bytes 1048608 | tf_op jit(solution)/shard_map/ppermute | solution.py:37
  219.4 4.5 add_convert_fusion.19
  225.6 5.2 broadcast_select_fusion.1
  230.8 7.8 pad_maximum_fusion
  238.6 4.3 collective-permute-start.2
  242.9 3.5 add_convert_fusion.11
  250.2 12.6 %fusion.18 = bf16[2048,1024]{1,0:T(8,128)(2,1)S(1)} fusion(bf16[2048,2048]{1,0:T(8,128)(2,1)} %bitcast.60, bf16[8192,2048]{1,0:T(8,128)(2,1)} %param.6, s32[]{:T(128)S(6)} %select_n.233), kind=kOutput, calls=%fused_computation.26 | convolution fusion | flops 8592031744 | bytes 16777220 | tf_op jit(solution)/shard_map/dot_general | solution.py:14
  262.7 9.7 collective-permute-start.17
  278.9 4.8 broadcast.29.clone
  286.6 25.1 %collective-permute-start.27 = (bf16[1,512,1024]{2,1,0:T(8,128)(2,1)S(1)}, bf16[1,512,1024]{2,1,0:T(8,128)(2,1)}, u32[]{:S(2)}, u32[]{:S(2)}) collective-permute-start(bf16[1,512,1024]{2,1,0:T(8,128)(2,1)S(1)} %get-tuple-element.39), channel_id=1, source_target_pairs={{0,2},{2,4},{4,6},{1,3},{3,5},{5,7},{8,10},{10,12},{12,14},{9,11},... | collective-permute-start | bytes 3145736 | tf_op jit(solution)/shard_map/ppermute | solution.py:51
  311.8 10.8 %fusion.21 = bf16[2048,1024]{1,0:T(8,128)(2,1)S(1)} fusion(bf16[2048,2048]{1,0:T(8,128)(2,1)S(1)} %bitcast.63, bf16[8192,2048]{1,0:T(8,128)(2,1)} %param.6, s32[]{:T(128)S(6)} %select_n.245), kind=kOutput, calls=%fused_computation.27 | convolution fusion | flops 8592031744 | bytes 16777220 | tf_op jit(solution)/shard_map/dot_general | solution.py:14
  322.6 5.9 collective-permute-done.28
  329.7 3.5 convert_add_fusion.1
  334.7 17.9 %collective-permute-start.21 = (bf16[1,512,1024]{2,1,0:T(8,128)(2,1)}, bf16[1,512,1024]{2,1,0:T(8,128)(2,1)}, u32[]{:S(2)}, u32[]{:S(2)}) collective-permute-start(bf16[1,512,1024]{2,1,0:T(8,128)(2,1)} %get-tuple-element.52), channel_id=1, source_target_pairs={{0,2},{1,3},{8,10},{9,11},{16,18},{17,19},{24,26},{25,27}} | collective-permute-start | bytes 3145736 | tf_op jit(solution)/shard_map/ppermute | solution.py:37
  355.8 5.9 collective-permute-start.9
  361.7 4.8 collective-permute-done.29
  368.5 7.0 collective-permute-done.21
  378.9 16.4 %collective-permute-done.9 = bf16[1,512,1024]{2,1,0:T(8,128)(2,1)} collective-permute-done((bf16[1,512,1024]{2,1,0:T(8,128)(2,1)}, bf16[1,512,1024]{2,1,0:T(8,128)(2,1)}, u32[]{:S(2)}, u32[]{:S(2)}) %collective-permute-start.9) | collective-permute-done | bytes 1048608 | tf_op jit(solution)/shard_map/ppermute | solution.py:37
  395.3 4.4 collective-permute-start.22
  414.1 9.2 collective-permute-done.22
  425.0 6.0 collective-permute-start.33
  431.0 14.8 %collective-permute-done.10 = bf16[1,512,1024]{2,1,0:T(8,128)(2,1)S(1)} collective-permute-done((bf16[1,512,1024]{2,1,0:T(8,128)(2,1)S(1)}, bf16[1,512,1024]{2,1,0:T(8,128)(2,1)S(1)}, u32[]{:S(2)}, u32[]{:S(2)}) %collective-permute-start.10) | collective-permute-done | bytes 1048608 | tf_op jit(solution)/shard_map/ppermute | solution.py:37
  448.6 5.0 collective-permute-start.23
  454.9 13.3 %collective-permute-done.33 = bf16[1,512,1024]{2,1,0:T(8,128)(2,1)} collective-permute-done((bf16[1,512,1024]{2,1,0:T(8,128)(2,1)S(1)}, bf16[1,512,1024]{2,1,0:T(8,128)(2,1)}, u32[]{:S(2)}, u32[]{:S(2)}) %collective-permute-start.33) | collective-permute-done | bytes 1048608 | tf_op jit(solution)/shard_map/ppermute | solution.py:51
  472.6 16.0 %collective-permute-start.11 = (bf16[1,512,1024]{2,1,0:T(8,128)(2,1)}, bf16[1,512,1024]{2,1,0:T(8,128)(2,1)}, u32[]{:S(2)}, u32[]{:S(2)}) collective-permute-start(bf16[1,512,1024]{2,1,0:T(8,128)(2,1)} %get-tuple-element.58), channel_id=1, source_target_pairs={{0,2},{2,4},{4,6},{1,3},{3,5},{5,7},{8,10},{10,12},{12,14},{9,11},... | collective-permute-start | bytes 3145736 | tf_op jit(solution)/shard_map/ppermute | solution.py:37
  494.1 7.4 collective-permute-done.26
  501.4 3.8 convert_add_fusion
  505.2 4.5 collective-permute-done.11
  509.7 14.2 %collective-permute-done.14 = bf16[1,512,1024]{2,1,0:T(8,128)(2,1)} collective-permute-done((bf16[1,512,1024]{2,1,0:T(8,128)(2,1)}, bf16[1,512,1024]{2,1,0:T(8,128)(2,1)}, u32[]{:S(2)}, u32[]{:S(2)}) %collective-permute-start.14) | collective-permute-done | bytes 1048608 | tf_op jit(solution)/shard_map/ppermute | solution.py:40
  526.3 15.0 %collective-permute-done.36 = bf16[1,512,1024]{2,1,0:T(8,128)(2,1)} collective-permute-done((bf16[1,512,1024]{2,1,0:T(8,128)(2,1)}, bf16[1,512,1024]{2,1,0:T(8,128)(2,1)}, u32[]{:S(2)}, u32[]{:S(2)}) %collective-permute-start.36) | collective-permute-done | bytes 1048608 | tf_op jit(solution)/shard_map/ppermute | solution.py:52
  555.8 14.1 %collective-permute-start.39 = (bf16[1,512,1024]{2,1,0:T(8,128)(2,1)}, bf16[1,512,1024]{2,1,0:T(8,128)(2,1)}, u32[]{:S(2)}, u32[]{:S(2)}) collective-permute-start(bf16[1,512,1024]{2,1,0:T(8,128)(2,1)} %get-tuple-element.35), channel_id=1, source_target_pairs={{0,2},{2,4},{4,6},{1,3},{3,5},{5,7},{8,10},{10,12},{12,14},{9,11},... | collective-permute-start | bytes 3145736 | tf_op jit(solution)/shard_map/ppermute | solution.py:51
  569.9 22.2 %fusion.4 = bf16[2048,2048]{1,0:T(8,128)(2,1)S(1)} fusion(bf16[2048,2048]{1,0:T(8,128)(2,1)} %bitcast.73, bf16[8192,2048]{1,0:T(8,128)(2,1)} %param.6, s32[]{:T(128)S(6)} %select_n.233), kind=kOutput, calls=%fused_computation.7 | convolution fusion | flops 17184063488 | bytes 25165828 | tf_op jit(solution)/shard_map/dot_general | solution.py:14
  594.5 20.7 %convolution_convert_fusion.1 = bf16[2048,2048]{1,0:T(8,128)(2,1)} fusion(bf16[2048,2048]{1,0:T(8,128)(2,1)S(1)} %bitcast.76, bf16[2048,2048]{1,0:T(8,128)(2,1)S(1)} %bitcast.66), kind=kOutput, calls=%fused_computation.10 | convolution fusion | flops 17184063488 | bytes 25165824 | tf_op jit(solution)/shard_map/dot_general | solution.py:14
  617.9 5.5 collective-permute-start.45
  626.8 4.1 add_convert_fusion.1
  636.0 30.7 %collective-permute-done.41 = bf16[1,512,1024]{2,1,0:T(8,128)(2,1)} collective-permute-done((bf16[1,512,1024]{2,1,0:T(8,128)(2,1)}, bf16[1,512,1024]{2,1,0:T(8,128)(2,1)}, u32[]{:S(2)}, u32[]{:S(2)}) %collective-permute-start.41) | collective-permute-done | bytes 1048608 | tf_op jit(solution)/shard_map/ppermute | solution.py:52
  672.6 4.1 constant_dynamic-slice_fusion.6
  676.6 18.3 %collective-permute-done.42 = bf16[1,512,1024]{2,1,0:T(8,128)(2,1)} collective-permute-done((bf16[1,512,1024]{2,1,0:T(8,128)(2,1)}, bf16[1,512,1024]{2,1,0:T(8,128)(2,1)}, u32[]{:S(2)}, u32[]{:S(2)}) %collective-permute-start.42) | collective-permute-done | bytes 1048608 | tf_op jit(solution)/shard_map/ppermute | solution.py:52
  700.4 15.7 %collective-permute-done.47 = bf16[1,512,1024]{2,1,0:T(8,128)(2,1)} collective-permute-done((bf16[1,512,1024]{2,1,0:T(8,128)(2,1)}, bf16[1,512,1024]{2,1,0:T(8,128)(2,1)}, u32[]{:S(2)}, u32[]{:S(2)}) %collective-permute-start.47) | collective-permute-done | bytes 1048608 | tf_op jit(solution)/shard_map/ppermute | solution.py:52
  726.0 18.3 %collective-permute-done.48 = bf16[1,512,1024]{2,1,0:T(8,128)(2,1)S(1)} collective-permute-done((bf16[1,512,1024]{2,1,0:T(8,128)(2,1)}, bf16[1,512,1024]{2,1,0:T(8,128)(2,1)S(1)}, u32[]{:S(2)}, u32[]{:S(2)}) %collective-permute-start.48) | collective-permute-done | bytes 1048608 | tf_op jit(solution)/shard_map/ppermute | solution.py:52
  749.5 17.4 %collective-permute-done.56 = bf16[1,1,1,256,2048]{4,3,2,1,0:T(8,128)(2,1)S(1)} collective-permute-done((bf16[1,1,1,256,2048]{4,3,2,1,0:T(8,128)(2,1)S(1)}, bf16[1,1,1,256,2048]{4,3,2,1,0:T(8,128)(2,1)S(1)}, u32[]{:S(2)}, u32[]{:S(2)}) %collective-permute-start.56) | collective-permute-done | bytes 1048608 | tf_op jit(solution)/shard_map/ppermute | solution.py:28
  768.6 38.7 %collective-permute-done.53 = bf16[2048,512]{1,0:T(8,128)(2,1)S(1)} collective-permute-done((bf16[2048,512]{1,0:T(8,128)(2,1)S(1)}, bf16[2048,512]{1,0:T(8,128)(2,1)S(1)}, u32[]{:S(2)}, u32[]{:S(2)}) %collective-permute-start.53) | collective-permute-done | bytes 2097184 | tf_op jit(solution)/shard_map/ppermute | solution.py:28
  808.7 20.8 %fusion.7 = bf16[2048,2048]{1,0:T(8,128)(2,1)S(1)} fusion(bf16[2048,2048]{1,0:T(8,128)(2,1)S(1)} %bitcast.71, bf16[2048,8192]{1,0:T(8,128)(2,1)} %param.5, s32[]{:T(128)S(6)} %select_n.233), kind=kOutput, calls=%fused_computation.8 | convolution fusion | flops 17184063488 | bytes 25165828 | tf_op jit(solution)/shard_map/dot_general | solution.py:14
  834.7 24.0 %convolution_convert_fusion = bf16[2048,2048]{1,0:T(8,128)(2,1)} fusion(bf16[2048,2048]{1,0:T(8,128)(2,1)} %bitcast.72, bf16[2048,2048]{1,0:T(8,128)(2,1)} %all-gather.2.cloned.1.call-done), kind=kOutput, calls=%fused_computation.9 | convolution fusion | flops 17184063488 | bytes 25165824 | tf_op jit(solution)/shard_map/dot_general | solution.py:14
  858.7 4.1 add_convert_fusion
  867.0 7.0 dynamic-slice_bitcast_fusion
  873.9 3.9 copy.40
  879.7 3.9 broadcast_in_dim.7
  896.4 17.0 %collective-permute-done.58 = bf16[2,1,1,256,2048]{4,3,2,1,0:T(8,128)(2,1)} collective-permute-done((bf16[2,1,1,256,2048]{4,3,2,1,0:T(8,128)(2,1)}, bf16[2,1,1,256,2048]{4,3,2,1,0:T(8,128)(2,1)}, u32[]{:S(2)}, u32[]{:S(2)}) %collective-permute-start.58) | collective-permute-done | bytes 2097184 | tf_op jit(solution)/shard_map/ppermute | solution.py:28
  920.0 4.0 copy.41
  926.6 3.9 copy.42
  930.5 40.3 %collective-permute-done.62 = bf16[512,2048]{0,1:T(8,128)(2,1)} collective-permute-done((bf16[512,2048]{0,1:T(8,128)(2,1)}, bf16[512,2048]{0,1:T(8,128)(2,1)}, u32[]{:S(2)}, u32[]{:S(2)}) %collective-permute-start.62) | collective-permute-done | bytes 2097184 | tf_op jit(solution)/shard_map/ppermute | solution.py:28
  970.8 4.0 copy.43
  974.8 3.3 constant_dynamic-update-slice_fusion.6
  981.9 11.6 %collective-permute-done.59 = bf16[1,1,1,256,2048]{4,3,2,1,0:T(8,128)(2,1)S(1)} collective-permute-done((bf16[1,1,1,256,2048]{4,3,2,1,0:T(8,128)(2,1)}, bf16[1,1,1,256,2048]{4,3,2,1,0:T(8,128)(2,1)S(1)}, u32[]{:S(2)}, u32[]{:S(2)}) %collective-permute-start.59) | collective-permute-done | bytes 1048608 | tf_op jit(solution)/shard_map/ppermute | solution.py:28
  (244 shorter events, 186.3 us)
Async XLA Ops:
  7.2 113.9 %all-gather.2.cloned.1.call-start = ((), (), s32[]{:S(2)}) async-start(), calls=%async_computation | async-start | bytes 9437184 | tf_op jit(solution)/shard_map/all_gather | solution.py:105
  7.9 37.6 %collective-permute-start.6 = (bf16[1,1,1,256,2048]{4,3,2,1,0:T(8,128)(2,1)}, bf16[1,1,1,256,2048]{4,3,2,1,0:T(8,128)(2,1)S(1)}, u32[]{:S(2)}, u32[]{:S(2)}) collective-permute-start(bf16[1,1,1,256,2048]{4,3,2,1,0:T(8,128)(2,1)} %bitcast.77), channel_id=1, source_target_pairs={{0,16},{8,24},{16,0},{24,8},{1,17},{9,25},{17,1},{25,9},{2,18},{10... | collective-permute-start | bytes 3145736 | tf_op jit(solution)/shard_map/ppermute | solution.py:28
  47.9 68.5 %collective-permute-start.7 = (bf16[2,1,1,256,2048]{4,3,2,1,0:T(8,128)(2,1)S(1)}, bf16[2,1,1,256,2048]{4,3,2,1,0:T(8,128)(2,1)}, u32[]{:S(2)}, u32[]{:S(2)}) collective-permute-start(bf16[2,1,1,256,2048]{4,3,2,1,0:T(8,128)(2,1)S(1)} %pad_maximum_fusion.2), channel_id=1, source_target_pairs={{0,1},{1,0},{2,3},{3,2},{4,5},{5,4},{6,7},{7,6},{8,9},{9,8},{10,11... | collective-permute-start | bytes 6291464 | tf_op jit(solution)/shard_map/ppermute | solution.py:28
  121.1 104.5 %collective-permute-start.8 = (bf16[2,1,2,256,2048]{4,3,2,1,0:T(8,128)(2,1)}, bf16[2,1,2,256,2048]{4,3,2,1,0:T(8,128)(2,1)}, u32[]{:S(2)}, u32[]{:S(2)}) collective-permute-start(bf16[2,1,2,256,2048]{4,3,2,1,0:T(8,128)(2,1)} %pad_maximum_fusion.1), channel_id=1, source_target_pairs={{0,8},{8,0},{16,24},{24,16},{1,9},{9,1},{17,25},{25,17},{2,10},{10... | collective-permute-start | bytes 12582920 | tf_op jit(solution)/shard_map/ppermute | solution.py:28
  144.4 31.6 %collective-permute-start = (bf16[1,512,1024]{2,1,0:T(8,128)(2,1)}, bf16[1,512,1024]{2,1,0:T(8,128)(2,1)}, u32[]{:S(2)}, u32[]{:S(2)}) collective-permute-start(bf16[1,512,1024]{2,1,0:T(8,128)(2,1)} %get-tuple-element.66), channel_id=1, source_target_pairs={{0,2},{1,3},{8,10},{9,11},{16,18},{17,19},{24,26},{25,27}} | collective-permute-start | bytes 3145736 | tf_op jit(solution)/shard_map/ppermute | solution.py:37
  171.9 25.1 %collective-permute-start.15 = (bf16[1,512,1024]{2,1,0:T(8,128)(2,1)}, bf16[1,512,1024]{2,1,0:T(8,128)(2,1)}, u32[]{:S(2)}, u32[]{:S(2)}) collective-permute-start(bf16[1,512,1024]{2,1,0:T(8,128)(2,1)} %get-tuple-element.56), channel_id=1, source_target_pairs={{0,2},{1,3},{8,10},{9,11},{16,18},{17,19},{24,26},{25,27}} | collective-permute-start | bytes 3145736 | tf_op jit(solution)/shard_map/ppermute | solution.py:37
  174.1 31.2 %collective-permute-start.3 = (bf16[1,512,1024]{2,1,0:T(8,128)(2,1)}, bf16[1,512,1024]{2,1,0:T(8,128)(2,1)}, u32[]{:S(2)}, u32[]{:S(2)}) collective-permute-start(bf16[1,512,1024]{2,1,0:T(8,128)(2,1)} %get-tuple-element.67), channel_id=1, source_target_pairs={{6,4},{7,5},{14,12},{15,13},{22,20},{23,21},{30,28},{31,29}} | collective-permute-start | bytes 3145736 | tf_op jit(solution)/shard_map/ppermute | solution.py:40
  178.9 40.5 %collective-permute-start.1 = (bf16[1,512,1024]{2,1,0:T(8,128)(2,1)}, bf16[1,512,1024]{2,1,0:T(8,128)(2,1)}, u32[]{:S(2)}, u32[]{:S(2)}) collective-permute-start(bf16[1,512,1024]{2,1,0:T(8,128)(2,1)} %add_convert_fusion.20), channel_id=1, source_target_pairs={{0,2},{2,4},{1,3},{3,5},{8,10},{10,12},{9,11},{11,13},{16,18},{18,... | collective-permute-start | bytes 3145736 | tf_op jit(solution)/shard_map/ppermute | solution.py:37
  181.2 61.7 %collective-permute-start.18 = (bf16[1,512,1024]{2,1,0:T(8,128)(2,1)S(1)}, bf16[1,512,1024]{2,1,0:T(8,128)(2,1)}, u32[]{:S(2)}, u32[]{:S(2)}) collective-permute-start(bf16[1,512,1024]{2,1,0:T(8,128)(2,1)S(1)} %get-tuple-element.57), channel_id=1, source_target_pairs={{6,4},{7,5},{14,12},{15,13},{22,20},{23,21},{30,28},{31,29}} | collective-permute-start | bytes 3145736 | tf_op jit(solution)/shard_map/ppermute | solution.py:40
  199.8 43.1 %collective-permute-start.16 = (bf16[1,512,1024]{2,1,0:T(8,128)(2,1)}, bf16[1,512,1024]{2,1,0:T(8,128)(2,1)}, u32[]{:S(2)}, u32[]{:S(2)}) collective-permute-start(bf16[1,512,1024]{2,1,0:T(8,128)(2,1)} %add_convert_fusion.12), channel_id=1, source_target_pairs={{0,2},{2,4},{1,3},{3,5},{8,10},{10,12},{9,11},{11,13},{16,18},{18,... | collective-permute-start | bytes 3145736 | tf_op jit(solution)/shard_map/ppermute | solution.py:37
  223.9 23.3 %collective-permute-start.4 = (bf16[1,512,1024]{2,1,0:T(8,128)(2,1)}, bf16[1,512,1024]{2,1,0:T(8,128)(2,1)}, u32[]{:S(2)}, u32[]{:S(2)}) collective-permute-start(bf16[1,512,1024]{2,1,0:T(8,128)(2,1)} %get-tuple-element.65), channel_id=1, source_target_pairs={{6,4},{4,2},{7,5},{5,3},{14,12},{12,10},{15,13},{13,11},{22,20},{2... | collective-permute-start | bytes 3145736 | tf_op jit(solution)/shard_map/ppermute | solution.py:40
  238.6 36.6 %collective-permute-start.2 = (bf16[1,512,1024]{2,1,0:T(8,128)(2,1)S(1)}, bf16[1,512,1024]{2,1,0:T(8,128)(2,1)S(1)}, u32[]{:S(2)}, u32[]{:S(2)}) collective-permute-start(bf16[1,512,1024]{2,1,0:T(8,128)(2,1)S(1)} %copy-done.39), channel_id=1, source_target_pairs={{0,2},{2,4},{4,6},{1,3},{3,5},{5,7},{8,10},{10,12},{12,14},{9,11},... | collective-permute-start | bytes 3145736 | tf_op jit(solution)/shard_map/ppermute | solution.py:37
  246.5 26.0 %collective-permute-start.19 = (bf16[1,512,1024]{2,1,0:T(8,128)(2,1)S(1)}, bf16[1,512,1024]{2,1,0:T(8,128)(2,1)S(1)}, u32[]{:S(2)}, u32[]{:S(2)}) collective-permute-start(bf16[1,512,1024]{2,1,0:T(8,128)(2,1)S(1)} %get-tuple-element.55), channel_id=1, source_target_pairs={{6,4},{4,2},{7,5},{5,3},{14,12},{12,10},{15,13},{13,11},{22,20},{2... | collective-permute-start | bytes 3145736 | tf_op jit(solution)/shard_map/ppermute | solution.py:40
  248.9 29.5 %collective-permute-start.5 = (bf16[1,512,1024]{2,1,0:T(8,128)(2,1)S(1)}, bf16[1,512,1024]{2,1,0:T(8,128)(2,1)S(1)}, u32[]{:S(2)}, u32[]{:S(2)}) collective-permute-start(bf16[1,512,1024]{2,1,0:T(8,128)(2,1)S(1)} %add_convert_fusion.17), channel_id=1, source_target_pairs={{6,4},{4,2},{2,0},{7,5},{5,3},{3,1},{14,12},{12,10},{10,8},{15,13}... | collective-permute-start | bytes 3145736 | tf_op jit(solution)/shard_map/ppermute | solution.py:40
  262.7 67.0 %collective-permute-start.17 = (bf16[1,512,1024]{2,1,0:T(8,128)(2,1)}, bf16[1,512,1024]{2,1,0:T(8,128)(2,1)}, u32[]{:S(2)}, u32[]{:S(2)}) collective-permute-start(bf16[1,512,1024]{2,1,0:T(8,128)(2,1)} %get-tuple-element.54), channel_id=1, source_target_pairs={{0,2},{2,4},{4,6},{1,3},{3,5},{5,7},{8,10},{10,12},{12,14},{9,11},... | collective-permute-start | bytes 3145736 | tf_op jit(solution)/shard_map/ppermute | solution.py:37
  273.9 55.9 %collective-permute-start.20 = (bf16[1,512,1024]{2,1,0:T(8,128)(2,1)}, bf16[1,512,1024]{2,1,0:T(8,128)(2,1)}, u32[]{:S(2)}, u32[]{:S(2)}) collective-permute-start(bf16[1,512,1024]{2,1,0:T(8,128)(2,1)} %add_convert_fusion.9), channel_id=1, source_target_pairs={{6,4},{4,2},{2,0},{7,5},{5,3},{3,1},{14,12},{12,10},{10,8},{15,13}... | collective-permute-start | bytes 3145736 | tf_op jit(solution)/shard_map/ppermute | solution.py:40
  285.4 43.1 %collective-permute-start.28 = (bf16[1,512,1024]{2,1,0:T(8,128)(2,1)S(1)}, bf16[1,512,1024]{2,1,0:T(8,128)(2,1)S(1)}, u32[]{:S(2)}, u32[]{:S(2)}) collective-permute-start(bf16[1,512,1024]{2,1,0:T(8,128)(2,1)S(1)} %get-tuple-element.39), channel_id=1, source_target_pairs={{6,4},{4,2},{2,0},{7,5},{5,3},{3,1},{14,12},{12,10},{10,8},{15,13}... | collective-permute-start | bytes 3145736 | tf_op jit(solution)/shard_map/ppermute | solution.py:52
  286.6 66.0 %collective-permute-start.27 = (bf16[1,512,1024]{2,1,0:T(8,128)(2,1)S(1)}, bf16[1,512,1024]{2,1,0:T(8,128)(2,1)}, u32[]{:S(2)}, u32[]{:S(2)}) collective-permute-start(bf16[1,512,1024]{2,1,0:T(8,128)(2,1)S(1)} %get-tuple-element.39), channel_id=1, source_target_pairs={{0,2},{2,4},{4,6},{1,3},{3,5},{5,7},{8,10},{10,12},{12,14},{9,11},... | collective-permute-start | bytes 3145736 | tf_op jit(solution)/shard_map/ppermute | solution.py:51
  328.4 38.0 %collective-permute-start.29 = (bf16[1,512,1024]{2,1,0:T(8,128)(2,1)S(1)}, bf16[1,512,1024]{2,1,0:T(8,128)(2,1)}, u32[]{:S(2)}, u32[]{:S(2)}) collective-permute-start(bf16[1,512,1024]{2,1,0:T(8,128)(2,1)S(1)} %collective-permute-done.28), channel_id=1, source_target_pairs={{4,2},{2,0},{5,3},{3,1},{12,10},{10,8},{13,11},{11,9},{20,18},{18,... | collective-permute-start | bytes 3145736 | tf_op jit(solution)/shard_map/ppermute | solution.py:52
  334.7 40.7 %collective-permute-start.21 = (bf16[1,512,1024]{2,1,0:T(8,128)(2,1)}, bf16[1,512,1024]{2,1,0:T(8,128)(2,1)}, u32[]{:S(2)}, u32[]{:S(2)}) collective-permute-start(bf16[1,512,1024]{2,1,0:T(8,128)(2,1)} %get-tuple-element.52), channel_id=1, source_target_pairs={{0,2},{1,3},{8,10},{9,11},{16,18},{17,19},{24,26},{25,27}} | collective-permute-start | bytes 3145736 | tf_op jit(solution)/shard_map/ppermute | solution.py:37
  352.6 23.6 %collective-permute-start.31 = (bf16[1,512,1024]{2,1,0:T(8,128)(2,1)}, bf16[1,512,1024]{2,1,0:T(8,128)(2,1)}, u32[]{:S(2)}, u32[]{:S(2)}) collective-permute-start(bf16[1,512,1024]{2,1,0:T(8,128)(2,1)} %collective-permute-done.27), channel_id=1, source_target_pairs={{2,4},{4,6},{3,5},{5,7},{10,12},{12,14},{11,13},{13,15},{18,20},{2... | collective-permute-start | bytes 3145736 | tf_op jit(solution)/shard_map/ppermute | solution.py:51
  355.8 39.5 %collective-permute-start.9 = (bf16[1,512,1024]{2,1,0:T(8,128)(2,1)}, bf16[1,512,1024]{2,1,0:T(8,128)(2,1)}, u32[]{:S(2)}, u32[]{:S(2)}) collective-permute-start(bf16[1,512,1024]{2,1,0:T(8,128)(2,1)} %get-tuple-element.60), channel_id=1, source_target_pairs={{0,2},{1,3},{8,10},{9,11},{16,18},{17,19},{24,26},{25,27}} | collective-permute-start | bytes 3145736 | tf_op jit(solution)/shard_map/ppermute | solution.py:37
  366.4 35.3 %collective-permute-start.30 = (bf16[1,512,1024]{2,1,0:T(8,128)(2,1)}, bf16[1,512,1024]{2,1,0:T(8,128)(2,1)}, u32[]{:S(2)}, u32[]{:S(2)}) collective-permute-start(bf16[1,512,1024]{2,1,0:T(8,128)(2,1)} %collective-permute-done.29), channel_id=1, source_target_pairs={{2,0},{3,1},{10,8},{11,9},{18,16},{19,17},{26,24},{27,25}} | collective-permute-start | bytes 3145736 | tf_op jit(solution)/shard_map/ppermute | solution.py:52
  367.8 46.3 %collective-permute-start.24 = (bf16[1,512,1024]{2,1,0:T(8,128)(2,1)}, bf16[1,512,1024]{2,1,0:T(8,128)(2,1)S(1)}, u32[]{:S(2)}, u32[]{:S(2)}) collective-permute-start(bf16[1,512,1024]{2,1,0:T(8,128)(2,1)} %get-tuple-element.53), channel_id=1, source_target_pairs={{6,4},{7,5},{14,12},{15,13},{22,20},{23,21},{30,28},{31,29}} | collective-permute-start | bytes 3145736 | tf_op jit(solution)/shard_map/ppermute | solution.py:40
  375.5 55.5 %collective-permute-start.12 = (bf16[1,512,1024]{2,1,0:T(8,128)(2,1)}, bf16[1,512,1024]{2,1,0:T(8,128)(2,1)S(1)}, u32[]{:S(2)}, u32[]{:S(2)}) collective-permute-start(bf16[1,512,1024]{2,1,0:T(8,128)(2,1)} %get-tuple-element.61), channel_id=1, source_target_pairs={{6,4},{7,5},{14,12},{15,13},{22,20},{23,21},{30,28},{31,29}} | collective-permute-start | bytes 3145736 | tf_op jit(solution)/shard_map/ppermute | solution.py:40
  376.2 32.7 %collective-permute-start.32 = (bf16[1,512,1024]{2,1,0:T(8,128)(2,1)}, bf16[1,512,1024]{2,1,0:T(8,128)(2,1)S(1)}, u32[]{:S(2)}, u32[]{:S(2)}) collective-permute-start(bf16[1,512,1024]{2,1,0:T(8,128)(2,1)} %collective-permute-done.31), channel_id=1, source_target_pairs={{4,6},{5,7},{12,14},{13,15},{20,22},{21,23},{28,30},{29,31}} | collective-permute-start | bytes 3145736 | tf_op jit(solution)/shard_map/ppermute | solution.py:51
  395.3 28.0 %collective-permute-start.22 = (bf16[1,512,1024]{2,1,0:T(8,128)(2,1)S(1)}, bf16[1,512,1024]{2,1,0:T(8,128)(2,1)S(1)}, u32[]{:S(2)}, u32[]{:S(2)}) collective-permute-start(bf16[1,512,1024]{2,1,0:T(8,128)(2,1)S(1)} %add_convert_fusion.8), channel_id=1, source_target_pairs={{0,2},{2,4},{1,3},{3,5},{8,10},{10,12},{9,11},{11,13},{16,18},{18,... | collective-permute-start | bytes 3145736 | tf_op jit(solution)/shard_map/ppermute | solution.py:37
  401.7 44.0 %collective-permute-start.10 = (bf16[1,512,1024]{2,1,0:T(8,128)(2,1)S(1)}, bf16[1,512,1024]{2,1,0:T(8,128)(2,1)S(1)}, u32[]{:S(2)}, u32[]{:S(2)}) collective-permute-start(bf16[1,512,1024]{2,1,0:T(8,128)(2,1)S(1)} %add_convert_fusion.16), channel_id=1, source_target_pairs={{0,2},{2,4},{1,3},{3,5},{8,10},{10,12},{9,11},{11,13},{16,18},{18,... | collective-permute-start | bytes 3145736 | tf_op jit(solution)/shard_map/ppermute | solution.py:37
  412.5 41.1 %collective-permute-start.34 = (bf16[1,512,1024]{2,1,0:T(8,128)(2,1)S(1)}, bf16[1,512,1024]{2,1,0:T(8,128)(2,1)S(1)}, u32[]{:S(2)}, u32[]{:S(2)}) collective-permute-start(bf16[1,512,1024]{2,1,0:T(8,128)(2,1)S(1)} %get-tuple-element.37), channel_id=1, source_target_pairs={{6,4},{4,2},{2,0},{7,5},{5,3},{3,1},{14,12},{12,10},{10,8},{15,13}... | collective-permute-start | bytes 3145736 | tf_op jit(solution)/shard_map/ppermute | solution.py:52
  424.3 45.6 %collective-permute-start.25 = (bf16[1,512,1024]{2,1,0:T(8,128)(2,1)S(1)}, bf16[1,512,1024]{2,1,0:T(8,128)(2,1)S(1)}, u32[]{:S(2)}, u32[]{:S(2)}) collective-permute-start(bf16[1,512,1024]{2,1,0:T(8,128)(2,1)S(1)} %get-tuple-element.51), channel_id=1, source_target_pairs={{6,4},{4,2},{7,5},{5,3},{14,12},{12,10},{15,13},{13,11},{22,20},{2... | collective-permute-start | bytes 3145736 | tf_op jit(solution)/shard_map/ppermute | solution.py:40
  425.0 43.2 %collective-permute-start.33 = (bf16[1,512,1024]{2,1,0:T(8,128)(2,1)S(1)}, bf16[1,512,1024]{2,1,0:T(8,128)(2,1)}, u32[]{:S(2)}, u32[]{:S(2)}) collective-permute-start(bf16[1,512,1024]{2,1,0:T(8,128)(2,1)S(1)} %get-tuple-element.37), channel_id=1, source_target_pairs={{0,2},{2,4},{4,6},{1,3},{3,5},{5,7},{8,10},{10,12},{12,14},{9,11},... | collective-permute-start | bytes 3145736 | tf_op jit(solution)/shard_map/ppermute | solution.py:51
  447.7 24.9 %collective-permute-start.13 = (bf16[1,512,1024]{2,1,0:T(8,128)(2,1)S(1)}, bf16[1,512,1024]{2,1,0:T(8,128)(2,1)S(1)}, u32[]{:S(2)}, u32[]{:S(2)}) collective-permute-start(bf16[1,512,1024]{2,1,0:T(8,128)(2,1)S(1)} %get-tuple-element.59), channel_id=1, source_target_pairs={{6,4},{4,2},{7,5},{5,3},{14,12},{12,10},{15,13},{13,11},{22,20},{2... | collective-permute-start | bytes 3145736 | tf_op jit(solution)/shard_map/ppermute | solution.py:40
  448.6 42.1 %collective-permute-start.23 = (bf16[1,512,1024]{2,1,0:T(8,128)(2,1)S(1)}, bf16[1,512,1024]{2,1,0:T(8,128)(2,1)S(1)}, u32[]{:S(2)}, u32[]{:S(2)}) collective-permute-start(bf16[1,512,1024]{2,1,0:T(8,128)(2,1)S(1)} %get-tuple-element.50), channel_id=1, source_target_pairs={{0,2},{2,4},{4,6},{1,3},{3,5},{5,7},{8,10},{10,12},{12,14},{9,11},... | collective-permute-start | bytes 3145736 | tf_op jit(solution)/shard_map/ppermute | solution.py:37
  453.6 38.4 %collective-permute-start.35 = (bf16[1,512,1024]{2,1,0:T(8,128)(2,1)S(1)}, bf16[1,512,1024]{2,1,0:T(8,128)(2,1)}, u32[]{:S(2)}, u32[]{:S(2)}) collective-permute-start(bf16[1,512,1024]{2,1,0:T(8,128)(2,1)S(1)} %collective-permute-done.34), channel_id=1, source_target_pairs={{4,2},{2,0},{5,3},{3,1},{12,10},{10,8},{13,11},{11,9},{20,18},{18,... | collective-permute-start | bytes 3145736 | tf_op jit(solution)/shard_map/ppermute | solution.py:52
  468.2 25.1 %collective-permute-start.37 = (bf16[1,512,1024]{2,1,0:T(8,128)(2,1)}, bf16[1,512,1024]{2,1,0:T(8,128)(2,1)}, u32[]{:S(2)}, u32[]{:S(2)}) collective-permute-start(bf16[1,512,1024]{2,1,0:T(8,128)(2,1)} %collective-permute-done.33), channel_id=1, source_target_pairs={{2,4},{4,6},{3,5},{5,7},{10,12},{12,14},{11,13},{13,15},{18,20},{2... | collective-permute-start | bytes 3145736 | tf_op jit(solution)/shard_map/ppermute | solution.py:51
  471.3 30.1 %collective-permute-start.26 = (bf16[1,512,1024]{2,1,0:T(8,128)(2,1)}, bf16[1,512,1024]{2,1,0:T(8,128)(2,1)}, u32[]{:S(2)}, u32[]{:S(2)}) collective-permute-start(bf16[1,512,1024]{2,1,0:T(8,128)(2,1)} %add_convert_fusion.5), channel_id=1, source_target_pairs={{6,4},{4,2},{2,0},{7,5},{5,3},{3,1},{14,12},{12,10},{10,8},{15,13}... | collective-permute-start | bytes 3145736 | tf_op jit(solution)/shard_map/ppermute | solution.py:40
  472.6 37.1 %collective-permute-start.11 = (bf16[1,512,1024]{2,1,0:T(8,128)(2,1)}, bf16[1,512,1024]{2,1,0:T(8,128)(2,1)}, u32[]{:S(2)}, u32[]{:S(2)}) collective-permute-start(bf16[1,512,1024]{2,1,0:T(8,128)(2,1)} %get-tuple-element.58), channel_id=1, source_target_pairs={{0,2},{2,4},{4,6},{1,3},{3,5},{5,7},{8,10},{10,12},{12,14},{9,11},... | collective-permute-start | bytes 3145736 | tf_op jit(solution)/shard_map/ppermute | solution.py:37
  490.7 33.2 %collective-permute-start.14 = (bf16[1,512,1024]{2,1,0:T(8,128)(2,1)}, bf16[1,512,1024]{2,1,0:T(8,128)(2,1)}, u32[]{:S(2)}, u32[]{:S(2)}) collective-permute-start(bf16[1,512,1024]{2,1,0:T(8,128)(2,1)} %add_convert_fusion.13), channel_id=1, source_target_pairs={{6,4},{4,2},{2,0},{7,5},{5,3},{3,1},{14,12},{12,10},{10,8},{15,13}... | collective-permute-start | bytes 3145736 | tf_op jit(solution)/shard_map/ppermute | solution.py:40
  492.0 49.4 %collective-permute-start.36 = (bf16[1,512,1024]{2,1,0:T(8,128)(2,1)}, bf16[1,512,1024]{2,1,0:T(8,128)(2,1)}, u32[]{:S(2)}, u32[]{:S(2)}) collective-permute-start(bf16[1,512,1024]{2,1,0:T(8,128)(2,1)} %collective-permute-done.35), channel_id=1, source_target_pairs={{2,0},{3,1},{10,8},{11,9},{18,16},{19,17},{26,24},{27,25}} | collective-permute-start | bytes 3145736 | tf_op jit(solution)/shard_map/ppermute | solution.py:52
  493.3 53.4 %collective-permute-start.38 = (bf16[1,512,1024]{2,1,0:T(8,128)(2,1)}, bf16[1,512,1024]{2,1,0:T(8,128)(2,1)S(1)}, u32[]{:S(2)}, u32[]{:S(2)}) collective-permute-start(bf16[1,512,1024]{2,1,0:T(8,128)(2,1)} %collective-permute-done.37), channel_id=1, source_target_pairs={{4,6},{5,7},{12,14},{13,15},{20,22},{21,23},{28,30},{29,31}} | collective-permute-start | bytes 3145736 | tf_op jit(solution)/shard_map/ppermute | solution.py:51
  551.6 71.9 %collective-permute-start.40 = (bf16[1,512,1024]{2,1,0:T(8,128)(2,1)}, bf16[1,512,1024]{2,1,0:T(8,128)(2,1)}, u32[]{:S(2)}, u32[]{:S(2)}) collective-permute-start(bf16[1,512,1024]{2,1,0:T(8,128)(2,1)} %get-tuple-element.35), channel_id=1, source_target_pairs={{6,4},{4,2},{2,0},{7,5},{5,3},{3,1},{14,12},{12,10},{10,8},{15,13}... | collective-permute-start | bytes 3145736 | tf_op jit(solution)/shard_map/ppermute | solution.py:52
  555.8 69.0 %collective-permute-start.39 = (bf16[1,512,1024]{2,1,0:T(8,128)(2,1)}, bf16[1,512,1024]{2,1,0:T(8,128)(2,1)}, u32[]{:S(2)}, u32[]{:S(2)}) collective-permute-start(bf16[1,512,1024]{2,1,0:T(8,128)(2,1)} %get-tuple-element.35), channel_id=1, source_target_pairs={{0,2},{2,4},{4,6},{1,3},{3,5},{5,7},{8,10},{10,12},{12,14},{9,11},... | collective-permute-start | bytes 3145736 | tf_op jit(solution)/shard_map/ppermute | solution.py:51
  594.4 32.4 %collective-permute-start.54 = (bf16[2,1,2,256,2048]{4,3,2,1,0:T(8,128)(2,1)}, bf16[2,1,2,256,2048]{4,3,2,1,0:T(8,128)(2,1)}, u32[]{:S(2)}, u32[]{:S(2)}) collective-permute-start(bf16[2,1,2,256,2048]{4,3,2,1,0:T(8,128)(2,1)} %constant_dynamic-slice_fusion.5), channel_id=1, source_target_pairs={{0,8},{8,0},{16,24},{24,16},{1,9},{9,1},{17,25},{25,17},{2,10},{10... | collective-permute-start | bytes 12582920 | tf_op jit(solution)/shard_map/ppermute | solution.py:28
  616.6 51.3 %collective-permute-start.46 = (bf16[1,512,1024]{2,1,0:T(8,128)(2,1)S(1)}, bf16[1,512,1024]{2,1,0:T(8,128)(2,1)}, u32[]{:S(2)}, u32[]{:S(2)}) collective-permute-start(bf16[1,512,1024]{2,1,0:T(8,128)(2,1)S(1)} %fusion.41), channel_id=1, source_target_pairs={{6,4},{4,2},{2,0},{7,5},{5,3},{3,1},{14,12},{12,10},{10,8},{15,13}... | collective-permute-start | bytes 3145736 | tf_op jit(solution)/shard_map/ppermute | solution.py:52
  617.9 53.0 %collective-permute-start.45 = (bf16[1,512,1024]{2,1,0:T(8,128)(2,1)S(1)}, bf16[1,512,1024]{2,1,0:T(8,128)(2,1)}, u32[]{:S(2)}, u32[]{:S(2)}) collective-permute-start(bf16[1,512,1024]{2,1,0:T(8,128)(2,1)S(1)} %fusion.41), channel_id=1, source_target_pairs={{0,2},{2,4},{4,6},{1,3},{3,5},{5,7},{8,10},{10,12},{12,14},{9,11},... | collective-permute-start | bytes 3145736 | tf_op jit(solution)/shard_map/ppermute | solution.py:51
  623.5 43.2 %collective-permute-start.41 = (bf16[1,512,1024]{2,1,0:T(8,128)(2,1)}, bf16[1,512,1024]{2,1,0:T(8,128)(2,1)}, u32[]{:S(2)}, u32[]{:S(2)}) collective-permute-start(bf16[1,512,1024]{2,1,0:T(8,128)(2,1)} %collective-permute-done.40), channel_id=1, source_target_pairs={{4,2},{2,0},{5,3},{3,1},{12,10},{10,8},{13,11},{11,9},{20,18},{18,... | collective-permute-start | bytes 3145736 | tf_op jit(solution)/shard_map/ppermute | solution.py:52
  624.8 44.5 %collective-permute-start.43 = (bf16[1,512,1024]{2,1,0:T(8,128)(2,1)}, bf16[1,512,1024]{2,1,0:T(8,128)(2,1)}, u32[]{:S(2)}, u32[]{:S(2)}) collective-permute-start(bf16[1,512,1024]{2,1,0:T(8,128)(2,1)} %collective-permute-done.39), channel_id=1, source_target_pairs={{2,4},{4,6},{3,5},{5,7},{10,12},{12,14},{11,13},{13,15},{18,20},{2... | collective-permute-start | bytes 3145736 | tf_op jit(solution)/shard_map/ppermute | solution.py:51
  633.5 89.0 %collective-permute-start.55 = (bf16[1,1,2,256,2048]{4,3,2,1,0:T(8,128)(2,1)}, bf16[1,1,2,256,2048]{4,3,2,1,0:T(8,128)(2,1)}, u32[]{:S(2)}, u32[]{:S(2)}) collective-permute-start(bf16[1,1,2,256,2048]{4,3,2,1,0:T(8,128)(2,1)} %constant_dynamic-slice_fusion.4), channel_id=1, source_target_pairs={{0,16},{8,24},{16,0},{24,8},{1,17},{9,25},{17,1},{25,9},{2,18},{10... | collective-permute-start | bytes 6291464 | tf_op jit(solution)/shard_map/ppermute | solution.py:28
  666.6 28.3 %collective-permute-start.42 = (bf16[1,512,1024]{2,1,0:T(8,128)(2,1)}, bf16[1,512,1024]{2,1,0:T(8,128)(2,1)}, u32[]{:S(2)}, u32[]{:S(2)}) collective-permute-start(bf16[1,512,1024]{2,1,0:T(8,128)(2,1)} %collective-permute-done.41), channel_id=1, source_target_pairs={{2,0},{3,1},{10,8},{11,9},{18,16},{19,17},{26,24},{27,25}} | collective-permute-start | bytes 3145736 | tf_op jit(solution)/shard_map/ppermute | solution.py:52
  667.9 48.1 %collective-permute-start.47 = (bf16[1,512,1024]{2,1,0:T(8,128)(2,1)}, bf16[1,512,1024]{2,1,0:T(8,128)(2,1)}, u32[]{:S(2)}, u32[]{:S(2)}) collective-permute-start(bf16[1,512,1024]{2,1,0:T(8,128)(2,1)} %collective-permute-done.46), channel_id=1, source_target_pairs={{4,2},{2,0},{5,3},{3,1},{12,10},{10,8},{13,11},{11,9},{20,18},{18,... | collective-permute-start | bytes 3145736 | tf_op jit(solution)/shard_map/ppermute | solution.py:52
  669.3 49.3 %collective-permute-start.44 = (bf16[1,512,1024]{2,1,0:T(8,128)(2,1)}, bf16[1,512,1024]{2,1,0:T(8,128)(2,1)}, u32[]{:S(2)}, u32[]{:S(2)}) collective-permute-start(bf16[1,512,1024]{2,1,0:T(8,128)(2,1)} %collective-permute-done.43), channel_id=1, source_target_pairs={{4,6},{5,7},{12,14},{13,15},{20,22},{21,23},{28,30},{29,31}} | collective-permute-start | bytes 3145736 | tf_op jit(solution)/shard_map/ppermute | solution.py:51
  670.9 51.6 %collective-permute-start.49 = (bf16[1,512,1024]{2,1,0:T(8,128)(2,1)}, bf16[1,512,1024]{2,1,0:T(8,128)(2,1)}, u32[]{:S(2)}, u32[]{:S(2)}) collective-permute-start(bf16[1,512,1024]{2,1,0:T(8,128)(2,1)} %collective-permute-done.45), channel_id=1, source_target_pairs={{2,4},{4,6},{3,5},{5,7},{10,12},{12,14},{11,13},{13,15},{18,20},{2... | collective-permute-start | bytes 3145736 | tf_op jit(solution)/shard_map/ppermute | solution.py:51
  694.9 73.7 %collective-permute-start.51 = (bf16[2048,512]{1,0:T(8,128)(2,1)S(1)}, bf16[2048,512]{1,0:T(8,128)(2,1)S(1)}, u32[]{:S(2)}, u32[]{:S(2)}) collective-permute-start(bf16[2048,512]{1,0:T(8,128)(2,1)S(1)} %get-tuple-element.46), channel_id=1, source_target_pairs={{0,8},{8,0},{16,24},{24,16},{1,9},{9,1},{17,25},{25,17},{2,10},{10... | collective-permute-start | bytes 6291464 | tf_op jit(solution)/shard_map/ppermute | solution.py:28
  716.1 52.5 %collective-permute-start.52 = (bf16[2048,512]{1,0:T(8,128)(2,1)S(1)}, bf16[2048,512]{1,0:T(8,128)(2,1)S(1)}, u32[]{:S(2)}, u32[]{:S(2)}) collective-permute-start(bf16[2048,512]{1,0:T(8,128)(2,1)S(1)} %get-tuple-element.45), channel_id=1, source_target_pairs={{0,16},{8,24},{16,0},{24,8},{1,17},{9,25},{17,1},{25,9},{2,18},{10... | collective-permute-start | bytes 6291464 | tf_op jit(solution)/shard_map/ppermute | solution.py:28
  718.5 25.7 %collective-permute-start.48 = (bf16[1,512,1024]{2,1,0:T(8,128)(2,1)}, bf16[1,512,1024]{2,1,0:T(8,128)(2,1)S(1)}, u32[]{:S(2)}, u32[]{:S(2)}) collective-permute-start(bf16[1,512,1024]{2,1,0:T(8,128)(2,1)} %collective-permute-done.47), channel_id=1, source_target_pairs={{2,0},{3,1},{10,8},{11,9},{18,16},{19,17},{26,24},{27,25}} | collective-permute-start | bytes 3145736 | tf_op jit(solution)/shard_map/ppermute | solution.py:52
  722.5 84.8 %collective-permute-start.53 = (bf16[2048,512]{1,0:T(8,128)(2,1)S(1)}, bf16[2048,512]{1,0:T(8,128)(2,1)S(1)}, u32[]{:S(2)}, u32[]{:S(2)}) collective-permute-start(bf16[2048,512]{1,0:T(8,128)(2,1)S(1)} %get-tuple-element.44), channel_id=1, source_target_pairs={{0,24},{8,16},{16,8},{24,0},{1,25},{9,17},{17,9},{25,1},{2,26},{10... | collective-permute-start | bytes 6291464 | tf_op jit(solution)/shard_map/ppermute | solution.py:28
  722.6 25.3 %collective-permute-start.50 = (bf16[1,512,1024]{2,1,0:T(8,128)(2,1)}, bf16[1,512,1024]{2,1,0:T(8,128)(2,1)S(1)}, u32[]{:S(2)}, u32[]{:S(2)}) collective-permute-start(bf16[1,512,1024]{2,1,0:T(8,128)(2,1)} %collective-permute-done.49), channel_id=1, source_target_pairs={{4,6},{5,7},{12,14},{13,15},{20,22},{21,23},{28,30},{29,31}} | collective-permute-start | bytes 3145736 | tf_op jit(solution)/shard_map/ppermute | solution.py:51
  744.2 22.7 %collective-permute-start.56 = (bf16[1,1,1,256,2048]{4,3,2,1,0:T(8,128)(2,1)S(1)}, bf16[1,1,1,256,2048]{4,3,2,1,0:T(8,128)(2,1)S(1)}, u32[]{:S(2)}, u32[]{:S(2)}) collective-permute-start(bf16[1,1,1,256,2048]{4,3,2,1,0:T(8,128)(2,1)S(1)} %constant_dynamic-slice_fusion.3), channel_id=1, source_target_pairs={{0,1},{1,0},{2,3},{3,2},{4,5},{5,4},{6,7},{7,6},{8,9},{9,8},{10,11... | collective-permute-start | bytes 3145736 | tf_op jit(solution)/shard_map/ppermute | solution.py:28
  834.1 24.6 %collective-permute-start.57 = (bf16[2,1,2,256,2048]{4,3,2,1,0:T(8,128)(2,1)}, bf16[2,1,2,256,2048]{4,3,2,1,0:T(8,128)(2,1)}, u32[]{:S(2)}, u32[]{:S(2)}) collective-permute-start(bf16[2,1,2,256,2048]{4,3,2,1,0:T(8,128)(2,1)} %constant_dynamic-slice_fusion.2), channel_id=1, source_target_pairs={{0,8},{8,0},{16,24},{24,16},{1,9},{9,1},{17,25},{25,17},{2,10},{10... | collective-permute-start | bytes 12582920 | tf_op jit(solution)/shard_map/ppermute | solution.py:28
  865.5 47.9 %collective-permute-start.58 = (bf16[2,1,1,256,2048]{4,3,2,1,0:T(8,128)(2,1)}, bf16[2,1,1,256,2048]{4,3,2,1,0:T(8,128)(2,1)}, u32[]{:S(2)}, u32[]{:S(2)}) collective-permute-start(bf16[2,1,1,256,2048]{4,3,2,1,0:T(8,128)(2,1)} %constant_dynamic-slice_fusion.1), channel_id=1, source_target_pairs={{0,1},{1,0},{2,3},{3,2},{4,5},{5,4},{6,7},{7,6},{8,9},{9,8},{10,11... | collective-permute-start | bytes 6291464 | tf_op jit(solution)/shard_map/ppermute | solution.py:28
  877.8 42.2 %collective-permute-start.60 = (bf16[512,2048]{0,1:T(8,128)(2,1)}, bf16[512,2048]{0,1:T(8,128)(2,1)}, u32[]{:S(2)}, u32[]{:S(2)}) collective-permute-start(bf16[512,2048]{0,1:T(8,128)(2,1)} %get-tuple-element.42), channel_id=1, source_target_pairs={{0,8},{8,0},{16,24},{24,16},{1,9},{9,1},{17,25},{25,17},{2,10},{10... | collective-permute-start | bytes 6291464 | tf_op jit(solution)/shard_map/ppermute | solution.py:28
  877.8 48.7 %collective-permute-start.61 = (bf16[512,2048]{0,1:T(8,128)(2,1)}, bf16[512,2048]{0,1:T(8,128)(2,1)}, u32[]{:S(2)}, u32[]{:S(2)}) collective-permute-start(bf16[512,2048]{0,1:T(8,128)(2,1)} %get-tuple-element.41), channel_id=1, source_target_pairs={{0,16},{8,24},{16,0},{24,8},{1,17},{9,25},{17,1},{25,9},{2,18},{10... | collective-permute-start | bytes 6291464 | tf_op jit(solution)/shard_map/ppermute | solution.py:28
  879.6 91.2 %collective-permute-start.62 = (bf16[512,2048]{0,1:T(8,128)(2,1)}, bf16[512,2048]{0,1:T(8,128)(2,1)}, u32[]{:S(2)}, u32[]{:S(2)}) collective-permute-start(bf16[512,2048]{0,1:T(8,128)(2,1)} %get-tuple-element.40), channel_id=1, source_target_pairs={{0,24},{8,16},{16,8},{24,0},{1,25},{9,17},{17,9},{25,1},{2,26},{10... | collective-permute-start | bytes 6291464 | tf_op jit(solution)/shard_map/ppermute | solution.py:28
  916.8 76.7 %collective-permute-start.59 = (bf16[1,1,1,256,2048]{4,3,2,1,0:T(8,128)(2,1)}, bf16[1,1,1,256,2048]{4,3,2,1,0:T(8,128)(2,1)S(1)}, u32[]{:S(2)}, u32[]{:S(2)}) collective-permute-start(bf16[1,1,1,256,2048]{4,3,2,1,0:T(8,128)(2,1)} %constant_dynamic-slice_fusion), channel_id=1, source_target_pairs={{0,16},{8,24},{16,0},{24,8},{1,17},{9,25},{17,1},{25,9},{2,18},{10... | collective-permute-start | bytes 3145736 | tf_op jit(solution)/shard_map/ppermute | solution.py:28
  (46 other events, 867.9 us)
Sparse Core Ops, SparseCore 0:
  9.9 90.5 all-gather.1
